TPU v7x, 512 devices: a whole 4x8x8 slice. The times are simulated.
512 devices in a mesh: seq: 128 (over y_hi, z, x), head: 4 (over y_lo, core).
Axes of the slice: x: 4, y: 8 (y_hi: 4, y_lo: 2; y = y_hi * 2 + y_lo), z: 8, core: 2. Of those that a mesh axis runs over, the one named last changes fastest.
Arguments:
- inputs: bfloat16 [65536, 1024], P('seq', 'head'), may hold values from -6 to 6
- row_gain: float32 [1024], replicated, may hold values from 0.1 to 1.9
- row_qkv: bfloat16 [1024, 3, 1024], P(None, None, 'head'), may hold values from -4 to 4, as said below
- row_out: bfloat16 [1024, 1024], P('head'), may hold values from -0.75 to 0.75
- col_gain: float32 [1024], replicated, may hold values from 0.1 to 1.9
- col_qkv: bfloat16 [1024, 3, 1024], P(None, None, 'head'), may hold values from -4 to 4, as said below
- col_out: bfloat16 [1024, 1024], P('head'), may hold values from -0.75 to 0.75
Outputs:
- mixed: bfloat16 [65536, 1024], P('seq', 'head')
Inputs may be any that keep to these rules, and one draw needn't show every extreme that they name: `row_qkv`: Query, key and value projections of each head, stacked along the middle dimension; columns are grouped by head. `col_qkv`: laid out as row_qkv.
All inputs are finite; a program needn't handle non-finite values.
Results may differ from a plain program's by a relative error of at most 0.034.
Values may be sent and summed in bfloat16 or wider, within the bound.
No kernel may reach another device: no remote copies, remote signals or barrier semaphores. Data moves between devices by JAX's collectives and lax.ppermute only.
A program may use at most 64 MiB of HBM per device.

v0:
```python
import jax
import jax.numpy as jnp
from jax import lax
from jax.sharding import PartitionSpec as P

COLS = 512
HEAD_DIM = 64


def from_behind(block, axis, distance):
    devices = range(lax.axis_size(axis))
    route = [(i - distance, i) for i in devices if i - distance in devices]
    return lax.ppermute(block, axis, route)


def norm_rows(values, gain):
    flat = values.astype(jnp.float32)
    mean = jnp.mean(flat, axis=-1, keepdims=True)
    centered = flat - mean
    var = jnp.mean(centered * centered, axis=-1, keepdims=True)
    return (centered * lax.rsqrt(var + 1e-05) * gain).astype(jnp.bfloat16)


def project(normed, weight):
    width = weight.shape[2]
    combined = jnp.dot(
        normed, weight.reshape(weight.shape[0], 3 * width), preferred_element_type=jnp.float32
    ).astype(jnp.bfloat16)
    return (combined[:, :width], combined[:, width : 2 * width], combined[:, 2 * width :])


def softmax_bf16(scores, allowed):
    scores = jnp.where(allowed, scores, -1e30)
    peak = jnp.max(scores, axis=-1, keepdims=True)
    expo = jnp.exp(scores - peak)
    return (expo / jnp.sum(expo, axis=-1, keepdims=True)).astype(jnp.bfloat16)


def col_attend(query, keys, values):
    rows, items, width = query.shape
    heads = width // HEAD_DIM
    query = query.reshape(rows, items, heads, HEAD_DIM)
    keys = keys.reshape(rows, items, heads, HEAD_DIM)
    values = values.reshape(rows, items, heads, HEAD_DIM)
    scores = jnp.einsum(
        "rche,sche->chrs", query, keys, preferred_element_type=jnp.float32
    ) * HEAD_DIM ** (-0.5)
    allowed = (
        jnp.arange(rows, dtype=jnp.int32)[:, None] >= jnp.arange(rows, dtype=jnp.int32)[None, :]
    )
    weights = softmax_bf16(scores, allowed)
    result = jnp.einsum("chrs,sche->rche", weights, values, preferred_element_type=jnp.float32)
    return result.astype(jnp.bfloat16).reshape(rows, items, width)


def row_layer(source, gain, weight, out_weight):
    full = lax.all_gather(source, "head", axis=1, tiled=True)
    query, keys, values = project(norm_rows(full, gain), weight)
    width = query.shape[1]
    heads = width // HEAD_DIM
    rows_here = query.shape[0] // COLS
    prev_keys, prev_vals = from_behind((keys, values), "seq", 1)
    key_pad = jnp.concatenate([prev_keys, keys], axis=0)
    val_pad = jnp.concatenate([prev_vals, values], axis=0)
    first = lax.axis_index("seq") * rows_here
    column = jnp.arange(COLS, dtype=jnp.int32)[:, None]
    slot = jnp.arange(2 * COLS, dtype=jnp.int32)[None, :]

    def one_row(row):
        keys_row = key_pad.reshape(2 * COLS, heads, HEAD_DIM)
        vals_row = val_pad.reshape(2 * COLS, heads, HEAD_DIM)
        query_row = query.reshape(COLS, heads, HEAD_DIM)
        scores = jnp.einsum(
            "qhe,khe->hqk", query_row, keys_row, preferred_element_type=jnp.float32
        ) * HEAD_DIM ** (-0.5)
        allowed = (
            (slot >= column + 1) & (slot <= column + COLS) & ((first + row > 0) | (slot >= COLS))
        )
        weights = softmax_bf16(scores, allowed)
        result = jnp.einsum("hqk,khe->qhe", weights, vals_row, preferred_element_type=jnp.float32)
        return result.astype(jnp.bfloat16).reshape(COLS, width)

    att = lax.map(one_row, jnp.arange(rows_here, dtype=jnp.int32)).reshape(-1, width)
    term = jnp.dot(att, out_weight, preferred_element_type=jnp.float32)
    summed = lax.psum_scatter(
        term.astype(jnp.bfloat16), "head", scatter_dimension=1, tiled=True
    ).astype(jnp.float32)
    return (source.astype(jnp.float32) + summed).astype(jnp.bfloat16)


def col_layer(hidden, gain, weight, out_weight):
    peers = lax.axis_size("seq")
    per_dev = COLS // peers
    rows_here = hidden.shape[0] // COLS
    full = lax.all_gather(hidden, "head", axis=1, tiled=True)
    query, keys, values = project(norm_rows(full, gain), weight)
    width = query.shape[1]
    pieces = (
        lax.all_to_all(
            query.reshape(rows_here, peers, per_dev, width),
            "seq",
            split_axis=1,
            concat_axis=0,
            tiled=True,
        ),
        lax.all_to_all(
            keys.reshape(rows_here, peers, per_dev, width),
            "seq",
            split_axis=1,
            concat_axis=0,
            tiled=True,
        ),
        lax.all_to_all(
            values.reshape(rows_here, peers, per_dev, width),
            "seq",
            split_axis=1,
            concat_axis=0,
            tiled=True,
        ),
    )
    rows, _, items, _ = pieces[0].shape
    result = col_attend(
        pieces[0].reshape(rows, items, width),
        pieces[1].reshape(rows, items, width),
        pieces[2].reshape(rows, items, width),
    )
    att = lax.all_to_all(
        result.reshape(rows, 1, items, width), "seq", split_axis=0, concat_axis=1, tiled=True
    )
    att = att.reshape(-1, width)
    term = jnp.dot(att, out_weight, preferred_element_type=jnp.float32)
    summed = lax.psum_scatter(
        term.astype(jnp.bfloat16), "head", scatter_dimension=1, tiled=True
    ).astype(jnp.float32)
    result = (hidden.astype(jnp.float32) + summed).astype(jnp.bfloat16)
    return result


def on_device(inputs, row_gain, row_qkv, row_out, col_gain, col_qkv, col_out):
    hidden = row_layer(inputs, row_gain, row_qkv, row_out)
    return col_layer(hidden, col_gain, col_qkv, col_out)


def solution(mesh):
    return jax.shard_map(
        on_device,
        mesh=mesh,
        in_specs=(
            P("seq", "head"),
            P(),
            P(None, None, "head"),
            P("head", None),
            P(),
            P(None, None, "head"),
            P("head", None),
        ),
        out_specs=P("seq", "head"),
        check_vma=False,
    )
```

profile of v0, /device:TPU:1, one launch (start us, length us, event | category | flops | bytes accessed | tf_op | source)
XLA Modules:
  0.0 272.8 jit_solution(12279803644318932312)
XLA Ops:
  7.3 1.7 copy.25
  9.1 32.1 %all-gather.3.cloned.1.call-done = bf16[512,1024]{1,0:T(8,128)(2,1)} async-done(((bf16[512,256]{1,0:T(8,128)(2,1)}), bf16[512,1024]{1,0:T(8,128)(2,1)}) %all-gather.3.cloned.1.call-update) | async-done | bytes 1048592 | tf_op jit(solution)/shard_map/all_gather | solution.py:57
  41.1 1.5 convert_reduce_fusion.1
  42.7 1.6 fusion.14
  45.5 3.7 %collective-permute-start.1 = (bf16[512,256]{1,0:T(8,128)(2,1)S(1)}, bf16[512,256]{1,0:T(8,128)(2,1)S(1)}, u32[]{:S(2)}, u32[]{:S(2)}) collective-permute-start(bf16[512,256]{1,0:T(8,128)(2,1)S(1)} %get-tuple-element.22), channel_id=1, source_target_pairs={{0,4},{4,8},{8,12},{12,16},{16,20},{20,24},{24,28},{28,32},{32,36}... | collective-permute-start | bytes 786440 | tf_op jit(solution)/shard_map/ppermute | solution.py:13
  49.1 3.1 %collective-permute-start = (bf16[512,256]{1,0:T(8,128)(2,1)S(1)}, bf16[512,256]{1,0:T(8,128)(2,1)S(1)}, u32[]{:S(2)}, u32[]{:S(2)}) collective-permute-start(bf16[512,256]{1,0:T(8,128)(2,1)S(1)} %get-tuple-element.32), channel_id=1, source_target_pairs={{0,4},{4,8},{8,12},{12,16},{16,20},{20,24},{24,28},{28,32},{32,36}... | collective-permute-start | bytes 786440 | tf_op jit(solution)/shard_map/ppermute | solution.py:13
  54.9 5.4 %collective-permute-done = bf16[512,256]{1,0:T(8,128)(2,1)S(1)} collective-permute-done((bf16[512,256]{1,0:T(8,128)(2,1)S(1)}, bf16[512,256]{1,0:T(8,128)(2,1)S(1)}, u32[]{:S(2)}, u32[]{:S(2)}) %collective-permute-start) | collective-permute-done | bytes 262176 | tf_op jit(solution)/shard_map/ppermute | solution.py:13
  60.5 5.3 %fusion.41 = (f32[4,512]{1,0:T(4,128)S(1)}, f32[4,512,1024]{2,1,0:T(8,128)}) fusion(pred[512,1024]{1,0:T(8,128)(4,1)S(1)} %fusion.18, bf16[512,4,64]{0,2,1:T(8,128)(2,1)S(1)} %bitcast.43, bf16[1024,4,64]{0,2,1:T(8,128)(2,1)S(1)} %bitcast.40), kind=kOutput, calls=%fused_computation.66 | convolution fusion | flops 276825088 | bytes 9707520 | tf_op jit(solution)/shard_map/while/body/eval_jaxpr/sub | solution.py:35
  65.8 4.8 %fusion.22 = bf16[4,64,512]{2,1,0:T(8,128)(2,1)S(1)} fusion(bf16[1024,4,64]{0,2,1:T(8,128)(2,1)S(1)} %bitcast.41, f32[4,512,1024]{2,1,0:T(8,128)} %get-tuple-element.36, f32[4,512]{1,0:T(4,128)S(1)} %get-tuple-element.34), kind=kOutput, calls=%fused_computation.37 | convolution fusion | flops 272760832 | bytes 9183232 | tf_op jit(solution)/shard_map/while/body/eval_jaxpr/hqk,khe->qhe/dot_general | solution.py:80
  72.2 38.2 %reduce-scatter.3.cloned.1.call-done = bf16[512,256]{1,0:T(8,128)(2,1)} async-done(((bf16[512,1024]{1,0:T(8,128)(2,1)}), bf16[512,256]{1,0:T(8,128)(2,1)}) %reduce-scatter.3.cloned.1.call-update) | async-done | bytes 262160 | tf_op jit(solution)/shard_map/reduce_scatter | solution.py:85
  110.5 1.7 add_convert_fusion.1
  112.2 1.8 copy.29
  114.0 25.0 %all-gather.5.cloned.1.call-done = bf16[512,1024]{1,0:T(8,128)(2,1)} async-done(((bf16[512,256]{1,0:T(8,128)(2,1)}), bf16[512,1024]{1,0:T(8,128)(2,1)}) %all-gather.5.cloned.1.call-update) | async-done | bytes 1048592 | tf_op jit(solution)/shard_map/all_gather | solution.py:95
  140.6 1.6 fusion.11
  142.2 2.5 convolution_convert_fusion.2
  145.6 17.2 %all-to-all-start.1 = ((bf16[1,128,4,256]{3,2,0,1:T(4,128)(2,1)}), bf16[1,128,4,256]{3,2,0,1:T(4,128)(2,1)S(1)}, u32[]{:S(2)}, u32[]{:S(2)}) async-start(bf16[1,128,4,256]{3,2,0,1:T(4,128)(2,1)} %bitcast.9), calls=%async_computation.2 | async-start | bytes 524288 | tf_op jit(solution)/shard_map/all_to_all | solution.py:99
  163.5 14.8 %all-to-all-done.1 = bf16[1,128,4,256]{3,2,0,1:T(4,128)(2,1)S(1)} async-done(((bf16[1,128,4,256]{3,2,0,1:T(4,128)(2,1)}), bf16[1,128,4,256]{3,2,0,1:T(4,128)(2,1)S(1)}, u32[]{:S(2)}, u32[]{:S(2)}) %all-to-all-start.1) | async-done | bytes 262176 | tf_op jit(solution)/shard_map/all_to_all | solution.py:99
  178.3 6.6 %all-to-all-start.2 = ((bf16[1,128,4,256]{3,2,0,1:T(4,128)(2,1)}), bf16[1,128,4,256]{3,2,0,1:T(4,128)(2,1)S(1)}, u32[]{:S(2)}, u32[]{:S(2)}) async-start(bf16[1,128,4,256]{3,2,0,1:T(4,128)(2,1)} %bitcast.11), calls=%async_computation.3 | async-start | bytes 524288 | tf_op jit(solution)/shard_map/all_to_all | solution.py:106
  185.7 13.0 %all-to-all-done.2 = bf16[1,128,4,256]{3,2,0,1:T(4,128)(2,1)S(1)} async-done(((bf16[1,128,4,256]{3,2,0,1:T(4,128)(2,1)}), bf16[1,128,4,256]{3,2,0,1:T(4,128)(2,1)S(1)}, u32[]{:S(2)}, u32[]{:S(2)}) %all-to-all-start.2) | async-done | bytes 262176 | tf_op jit(solution)/shard_map/all_to_all | solution.py:106
  198.7 8.3 %all-to-all-start = ((bf16[1,128,4,256]{3,2,0,1:T(4,128)(2,1)}), bf16[1,128,4,256]{3,2,0,1:T(4,128)(2,1)S(1)}, u32[]{:S(2)}, u32[]{:S(2)}) async-start(bf16[1,128,4,256]{3,2,0,1:T(4,128)(2,1)} %bitcast.7), calls=%async_computation.1 | async-start | bytes 524288 | tf_op jit(solution)/shard_map/all_to_all | solution.py:113
  208.5 13.2 %all-to-all-done = bf16[1,128,4,256]{3,2,0,1:T(4,128)(2,1)S(1)} async-done(((bf16[1,128,4,256]{3,2,0,1:T(4,128)(2,1)}), bf16[1,128,4,256]{3,2,0,1:T(4,128)(2,1)S(1)}, u32[]{:S(2)}, u32[]{:S(2)}) %all-to-all-start) | async-done | bytes 262176 | tf_op jit(solution)/shard_map/all_to_all | solution.py:113
  222.5 21.3 %all_to_all.16 = bf16[128,1,4,256]{3,2,1,0:T(4,128)(2,1)S(1)} all-to-all(bf16[128,1,4,256]{3,2,1,0:T(4,128)(2,1)S(1)} %copy.37), channel_id=1, replica_groups=mesh['seq'=128,'head'=4] {'seq'}, dimensions={0} | all-to-all | bytes 524288 | tf_op jit(solution)/shard_map/all_to_all | solution.py:127
  245.4 19.1 %reduce-scatter.5.cloned.1.call-done = bf16[512,256]{1,0:T(8,128)(2,1)} async-done(((bf16[512,1024]{1,0:T(8,128)(2,1)}), bf16[512,256]{1,0:T(8,128)(2,1)}) %reduce-scatter.5.cloned.1.call-update) | async-done | bytes 262160 | tf_op jit(solution)/shard_map/reduce_scatter | solution.py:132
  264.6 1.7 add_convert_fusion
  (57 shorter events, 13.9 us)
Async XLA Ops:
  6.5 64.2 %copy-start = (bf16[256,1024]{1,0:T(8,128)(2,1)S(1)}, bf16[256,1024]{1,0:T(8,128)(2,1)}, u32[]{:S(2)}) copy-start(bf16[256,1024]{1,0:T(8,128)(2,1)} %param.10) | copy-start | bytes 1572868
  6.5 34.6 %all-gather.3.cloned.1.call-start = ((), (), s32[]{:S(2)}) async-start(), calls=%async_computation.6 | async-start | bytes 1310720 | tf_op jit(solution)/shard_map/all_gather | solution.py:57
  7.3 103.2 %reduce-scatter.3.cloned.1.call-start = ((), (), s32[]{:S(2)}) async-start(), calls=%async_computation.7 | async-start | bytes 1310720 | tf_op jit(solution)/shard_map/reduce_scatter | solution.py:85
  7.3 37.0 %copy-start.7 = (f32[1024]{0:T(1024)S(1)}, f32[1024]{0:T(1024)}, u32[]{:S(2)}) copy-start(f32[1024]{0:T(1024)} %param.8) | copy-start | bytes 12292
  41.1 3.2 %copy-start.1 = (bf16[512,1024]{1,0:T(8,128)(2,1)S(1)}, bf16[512,1024]{1,0:T(8,128)(2,1)}, u32[]{:S(2)}) copy-start(bf16[512,1024]{1,0:T(8,128)(2,1)} %all-gather.3.cloned.1.call-done) | copy-start | bytes 3145732
  45.5 9.2 %collective-permute-start.1 = (bf16[512,256]{1,0:T(8,128)(2,1)S(1)}, bf16[512,256]{1,0:T(8,128)(2,1)S(1)}, u32[]{:S(2)}, u32[]{:S(2)}) collective-permute-start(bf16[512,256]{1,0:T(8,128)(2,1)S(1)} %get-tuple-element.22), channel_id=1, source_target_pairs={{0,4},{4,8},{8,12},{12,16},{16,20},{20,24},{24,28},{28,32},{32,36}... | collective-permute-start | bytes 786440 | tf_op jit(solution)/shard_map/ppermute | solution.py:13
  49.1 11.1 %collective-permute-start = (bf16[512,256]{1,0:T(8,128)(2,1)S(1)}, bf16[512,256]{1,0:T(8,128)(2,1)S(1)}, u32[]{:S(2)}, u32[]{:S(2)}) collective-permute-start(bf16[512,256]{1,0:T(8,128)(2,1)S(1)} %get-tuple-element.32), channel_id=1, source_target_pairs={{0,4},{4,8},{8,12},{12,16},{16,20},{20,24},{24,28},{28,32},{32,36}... | collective-permute-start | bytes 786440 | tf_op jit(solution)/shard_map/ppermute | solution.py:13
  70.7 39.8 %copy-start.5 = (bf16[512,256]{1,0:T(8,128)(2,1)S(1)}, bf16[512,256]{1,0:T(8,128)(2,1)}, u32[]{:S(2)}) copy-start(bf16[512,256]{1,0:T(8,128)(2,1)} %param.7) | copy-start | bytes 786436
  70.7 41.5 %copy-start.4 = (bf16[1024,3,256]{2,0,1:T(8,128)(2,1)S(1)}, bf16[1024,3,256]{2,0,1:T(8,128)(2,1)}, u32[]{:S(2)}) copy-start(bf16[1024,3,256]{2,0,1:T(8,128)(2,1)} %param.12) | copy-start | bytes 4718596
  72.2 66.8 %all-gather.5.cloned.1.call-start = ((), (), s32[]{:S(2)}) async-start(), calls=%async_computation.8 | async-start | bytes 1310720 | tf_op jit(solution)/shard_map/all_gather | solution.py:95
  112.2 30.0 %copy-start.8 = (f32[1024]{0:T(1024)S(1)}, f32[1024]{0:T(1024)}, u32[]{:S(2)}) copy-start(f32[1024]{0:T(1024)} %param.11) | copy-start | bytes 12292
  139.0 3.2 %copy-start.2 = (bf16[512,1024]{1,0:T(8,128)(2,1)S(1)}, bf16[512,1024]{1,0:T(8,128)(2,1)}, u32[]{:S(2)}) copy-start(bf16[512,1024]{1,0:T(8,128)(2,1)} %all-gather.5.cloned.1.call-done) | copy-start | bytes 3145732
  145.6 32.8 %all-to-all-start.1 = ((bf16[1,128,4,256]{3,2,0,1:T(4,128)(2,1)}), bf16[1,128,4,256]{3,2,0,1:T(4,128)(2,1)S(1)}, u32[]{:S(2)}, u32[]{:S(2)}) async-start(bf16[1,128,4,256]{3,2,0,1:T(4,128)(2,1)} %bitcast.9), calls=%async_computation.2 | async-start | bytes 524288 | tf_op jit(solution)/shard_map/all_to_all | solution.py:99
  178.3 20.4 %all-to-all-start.2 = ((bf16[1,128,4,256]{3,2,0,1:T(4,128)(2,1)}), bf16[1,128,4,256]{3,2,0,1:T(4,128)(2,1)S(1)}, u32[]{:S(2)}, u32[]{:S(2)}) async-start(bf16[1,128,4,256]{3,2,0,1:T(4,128)(2,1)} %bitcast.11), calls=%async_computation.3 | async-start | bytes 524288 | tf_op jit(solution)/shard_map/all_to_all | solution.py:106
  198.7 23.0 %all-to-all-start = ((bf16[1,128,4,256]{3,2,0,1:T(4,128)(2,1)}), bf16[1,128,4,256]{3,2,0,1:T(4,128)(2,1)S(1)}, u32[]{:S(2)}, u32[]{:S(2)}) async-start(bf16[1,128,4,256]{3,2,0,1:T(4,128)(2,1)} %bitcast.7), calls=%async_computation.1 | async-start | bytes 524288 | tf_op jit(solution)/shard_map/all_to_all | solution.py:113
  207.1 57.5 %reduce-scatter.5.cloned.1.call-start = ((), (), s32[]{:S(2)}) async-start(), calls=%async_computation.9 | async-start | bytes 1310720 | tf_op jit(solution)/shard_map/reduce_scatter | solution.py:132
  221.9 22.0 %copy-start.6 = (bf16[256,1024]{1,0:T(8,128)(2,1)S(1)}, bf16[256,1024]{1,0:T(8,128)(2,1)}, u32[]{:S(2)}) copy-start(bf16[256,1024]{1,0:T(8,128)(2,1)} %param.13) | copy-start | bytes 1572868
  222.5 42.0 %copy-start.3 = (bf16[512,256]{1,0:T(8,128)(2,1)S(1)}, bf16[512,256]{1,0:T(8,128)(2,1)}, u32[]{:S(2)}) copy-start(bf16[512,256]{1,0:T(8,128)(2,1)} %add_convert_fusion.1) | copy-start | bytes 786436
Sparse Core Ops, SparseCore 0:
  9.5 31.6 all-gather.2
  72.3 38.1 reduce-scatter.2
  112.8 26.2 all-gather.4
  245.5 18.9 reduce-scatter.4
where the time goes:
time: 273 us
  waiting for transfers between devices  163 us (60%)
  starting transfers between devices  39 us (14%)
  blocking collectives  21.3 us (8%)
  matrix products  17.9 us (7%)
  between operations  13.4 us (5%)
  other arithmetic  10.6 us (4%)
  local copies, waits for them, and re-layouts  7.42 us (3%)
    reduce_scatter x1, waiting for transfers between devices, row_layer(): lax.psum_scatter(term.astype(jnp.bfloat16), 'head', scatter_dimension=1,...  38.2 us
    all_gather x1, waiting for transfers between devices, row_layer(): full = lax.all_gather(source, 'head', axis=1, tiled=True)  32.1 us
    all_gather x1, waiting for transfers between devices, col_layer(): full = lax.all_gather(hidden, 'head', axis=1, tiled=True)  25 us
    all_to_all x1, blocking collectives, col_layer(): lax.all_to_all(result.reshape(rows, 1, items, width), 'seq', split_axis=0...  21.3 us
    reduce_scatter x1, waiting for transfers between devices, col_layer(): lax.psum_scatter(term.astype(jnp.bfloat16), 'head', scatter_dimension=1,...  19.1 us
    all_to_all x1, starting transfers between devices, col_layer(): lax.all_to_all(query.reshape(rows_here, peers, per_dev, width), 'seq', sp...  17.2 us
    all_to_all x1, waiting for transfers between devices, col_layer(): lax.all_to_all(query.reshape(rows_here, peers, per_dev, width), 'seq', sp...  14.8 us
    all_to_all x1, waiting for transfers between devices, col_layer(): lax.all_to_all(values.reshape(rows_here, peers, per_dev, width), 'seq', s...  13.2 us
  transfers between devices with their start and end apart: 9, of which 9 were waited for; matrix products, arithmetic and copies ran while one was open for 3% of the time, Pallas kernels for 0%

commit v1 on v0

v1 whole, which is shorter than its diff:
```python
import functools

import jax
import jax.numpy as jnp
from jax import lax
from jax.experimental import pallas as pl
from jax.experimental.pallas import tpu as pltpu
from jax.sharding import Mesh, PartitionSpec as P

COLS = 512
HEAD_DIM = 64
SEQ = ("yh", "z", "x")
HEAD = ("yl", "c")
GROUP = 256
PARTS = 4
HEADS_HERE = GROUP // HEAD_DIM
MIB = 1 << 20
VMEM = pl.BlockSpec(memory_space=pltpu.VMEM)
SMEM = pl.BlockSpec(memory_space=pltpu.SMEM)


def dot(a, b):
    return jnp.dot(a, b, preferred_element_type=jnp.float32)


def dot_t(a, b):
    return lax.dot_general(a, b, (((1,), (1,)), ((), ())), preferred_element_type=jnp.float32)


def normed_pieces(pieces, gains):
    flat = [p.astype(jnp.float32) for p in pieces]
    width = sum(p.shape[1] for p in pieces)
    mean = sum(jnp.sum(p, axis=-1, keepdims=True) for p in flat) / width
    flat = [p - mean for p in flat]
    var = sum(jnp.sum(p * p, axis=-1, keepdims=True) for p in flat) / width
    scale = lax.rsqrt(var + 1e-05)
    return [(p * scale * g).astype(jnp.bfloat16) for p, g in zip(flat, gains)]


def row_project_kernel(place, near, far, gain, weight, query, kv):
    first = [place[0], place[1]]
    block = 256

    def step(i):
        rows = pl.ds(pl.multiple_of(i * block, block), block)
        order = [first[0], first[0] + 1, first[1], first[1] + 1]
        pieces = [near[0, rows, :], near[1, rows, :], far[0, rows, :], far[1, rows, :]]
        normed = normed_pieces(pieces, [gain[n] for n in order])
        total = sum(dot(p, weight[n]) for p, n in zip(normed, order)).astype(jnp.bfloat16)
        query[rows, :] = total[:, :GROUP]
        kv[0, rows, :] = total[:, GROUP : 2 * GROUP]
        kv[1, rows, :] = total[:, 2 * GROUP :]

    pl.loop(0, COLS // block)(step)


def row_project(place, near, far, gain, weight):
    return pl.pallas_call(
        row_project_kernel,
        out_shape=(
            jax.ShapeDtypeStruct((COLS, GROUP), jnp.bfloat16),
            jax.ShapeDtypeStruct((2, COLS, GROUP), jnp.bfloat16),
        ),
        in_specs=[SMEM, VMEM, VMEM, VMEM, VMEM],
        out_specs=(VMEM, VMEM),
        compiler_params=pltpu.CompilerParams(vmem_limit_bytes=24 * MIB),
        cost_estimate=pl.CostEstimate(
            flops=2 * COLS * 1024 * 768, bytes_accessed=4 * MIB, transcendentals=COLS
        ),
        name="row_project",
    )(place, near, far, gain, weight)


def head_mask(rows, head):
    lane = lax.broadcasted_iota(jnp.int32, (rows, GROUP), 1)
    return (lane >= head * HEAD_DIM) & (lane < (head + 1) * HEAD_DIM)


def row_attend_kernel(place, query, kv, before, out):
    block = 256
    blocked = jnp.where(place[2] > 0, 0.0, -1e30).astype(jnp.float32)
    row = lax.broadcasted_iota(jnp.int32, (block, block), 0)
    col = lax.broadcasted_iota(jnp.int32, (block, block), 1)
    late, early = col > row, col <= row
    scale = HEAD_DIM ** (-0.5)
    for half in range(2):
        rows = slice(half * block, (half + 1) * block)
        if half == 0:
            keys = [before[0, :block], before[0, block:], kv[0, :block]]
            vals = [before[1, :block], before[1, block:], kv[1, :block]]
        else:
            keys = [before[0, block:], kv[0, :block], kv[0, block:]]
            vals = [before[1, block:], kv[1, :block], kv[1, block:]]
        q = query[rows, :]
        total = jnp.zeros((block, GROUP), jnp.float32)
        for head in range(HEADS_HERE):
            mask = head_mask(block, head)
            qh = jnp.where(mask, q * jnp.bfloat16(scale), jnp.bfloat16(0))
            s0, s1, s2 = [dot_t(qh, k) for k in keys]
            s0 = jnp.where(late, s0, -1e30) + blocked
            if half == 0:
                s1 = s1 + blocked
            s2 = jnp.where(early, s2, -1e30)
            peak = jnp.max(jnp.maximum(jnp.maximum(s0, s1), s2), axis=-1, keepdims=True)
            p = [jnp.exp(s - peak) for s in (s0, s1, s2)]
            norm = jnp.sum(p[0] + p[1] + p[2], axis=-1, keepdims=True)
            acc = sum(dot(w.astype(jnp.bfloat16), v) for w, v in zip(p, vals))
            total = jnp.where(mask, acc / norm, total)
        out[rows, :] = total.astype(jnp.bfloat16)


def row_attend(place, query, kv, before):
    return pl.pallas_call(
        row_attend_kernel,
        out_shape=jax.ShapeDtypeStruct((COLS, GROUP), jnp.bfloat16),
        in_specs=[SMEM, VMEM, VMEM, VMEM],
        out_specs=VMEM,
        compiler_params=pltpu.CompilerParams(vmem_limit_bytes=24 * MIB),
        cost_estimate=pl.CostEstimate(
            flops=4 * COLS * 768 * 1024, bytes_accessed=2 * MIB, transcendentals=4 * COLS * 768
        ),
        name="row_attend",
    )(place, query, kv, before)


ROW_OUT, COL_QKV, COL_OUT, WEIGHT_ROWS = 0, 1024, 4096, 5120


def pack_weights(row_out, col_qkv, col_out):
    def blocks(w):
        return w.reshape(GROUP, PARTS, GROUP).transpose(1, 0, 2).reshape(PARTS * GROUP, GROUP)

    return jnp.concatenate(
        [blocks(row_out), col_qkv.transpose(1, 0, 2).reshape(3 * 1024, GROUP), blocks(col_out)], axis=0
    )


def row_out_kernel(place, att, near, far, w0, w1, w2, w3, out):
    rows = pl.ds(pl.multiple_of(place[3] * 128, 128), 128)
    groups = [place[0] + place[4], place[0] + 1 - place[4], place[1] + place[4], place[1] + 1 - place[4]]
    parts = [att[g] for g in groups]

    def resid(n):
        use_near = (n // 2) * 2 == place[0]
        return jnp.where(use_near, near[n % 2, rows, :], far[n % 2, rows, :])

    for n in range(PARTS):
        total = sum(
            dot(p, w[ROW_OUT + n * GROUP : ROW_OUT + (n + 1) * GROUP, :])
            for p, w in zip(parts, (w0, w1, w2, w3))
        )
        out[:, n * GROUP : (n + 1) * GROUP] = (resid(n).astype(jnp.float32) + total).astype(jnp.bfloat16)


def row_output(place, att, near, far, weights):
    weights = [w[ROW_OUT : ROW_OUT + 1024] for w in weights]
    return pl.pallas_call(
        row_out_kernel,
        out_shape=jax.ShapeDtypeStruct((128, 1024), jnp.bfloat16),
        in_specs=[SMEM] + [VMEM] * 7,
        out_specs=VMEM,
        compiler_params=pltpu.CompilerParams(vmem_limit_bytes=24 * MIB),
        cost_estimate=pl.CostEstimate(
            flops=2 * 128 * 1024 * 1024, bytes_accessed=4 * MIB, transcendentals=0
        ),
        name="row_output",
    )(place, att, near, far, *weights)


def col_layer_kernel(hidden, gain, w0, w1, w2, w3, out):
    h = hidden[...]
    pieces = [h[:, n * GROUP : (n + 1) * GROUP] for n in range(PARTS)]
    normed = normed_pieces(pieces, [gain[n] for n in range(PARTS)])
    normed = jnp.concatenate(normed, axis=1)
    rows = h.shape[0]
    allowed = lax.broadcasted_iota(jnp.int32, (rows, rows), 0) >= lax.broadcasted_iota(
        jnp.int32, (rows, rows), 1
    )
    scale = HEAD_DIM ** (-0.5)
    atts = []
    for w in (w0, w1, w2, w3):
        q, k, v = [
            dot(normed, w[COL_QKV + i * 1024 : COL_QKV + (i + 1) * 1024, :]).astype(jnp.bfloat16)
            for i in range(3)
        ]
        total = jnp.zeros((rows, GROUP), jnp.float32)
        for head in range(HEADS_HERE):
            mask = head_mask(rows, head)
            qh = jnp.where(mask, q * jnp.bfloat16(scale), jnp.bfloat16(0))
            s = jnp.where(allowed, dot_t(qh, k), -1e30)
            p = jnp.exp(s - jnp.max(s, axis=-1, keepdims=True))
            norm = jnp.sum(p, axis=-1, keepdims=True)
            total = jnp.where(mask, dot(p.astype(jnp.bfloat16), v) / norm, total)
        atts.append(total.astype(jnp.bfloat16))
    for n in range(PARTS):
        total = sum(
            dot(a, w[COL_OUT + n * GROUP : COL_OUT + (n + 1) * GROUP, :])
            for a, w in zip(atts, (w0, w1, w2, w3))
        )
        out[n] = (pieces[n].astype(jnp.float32) + total).astype(jnp.bfloat16)


def col_layer(hidden, gain, weights):
    return pl.pallas_call(
        col_layer_kernel,
        out_shape=jax.ShapeDtypeStruct((PARTS, 128, GROUP), jnp.bfloat16),
        in_specs=[VMEM] * 6,
        out_specs=VMEM,
        compiler_params=pltpu.CompilerParams(vmem_limit_bytes=40 * MIB),
        cost_estimate=pl.CostEstimate(
            flops=2 * 128 * 1024 * 4096, bytes_accessed=10 * MIB, transcendentals=16 * 128 * 128
        ),
        name="col_layer",
    )(hidden, gain, *weights)


def on_device(inputs, row_gain, row_qkv, row_out, col_gain, col_qkv, col_out):
    yl, core = lax.axis_index("yl"), lax.axis_index("c")
    place = jnp.stack(
        [yl * 2, (1 - yl) * 2, lax.axis_index(SEQ), yl * 2 + core, core, core]
    ).astype(jnp.int32)

    with jax.named_scope("gather_inputs"):
        other = lax.ppermute(inputs, "yl", [(0, 1), (1, 0)])
        near = lax.all_gather(inputs, "c", axis=0)
        far = lax.all_gather(other, "c", axis=0)

    with jax.named_scope("gather_weights"):
        mine = pack_weights(row_out, col_qkv, col_out)
        route = []
        for yh in range(4):
            a, b = yh * 4, yh * 4 + 2
            route += [(a, b), (b, a)]
            a, b = yh * 4 + 3, ((yh + 1) % 4) * 4 + 1
            route += [(a, b), (b, a)]
        mine, far = lax.optimization_barrier((mine, far))
        theirs = lax.ppermute(mine, ("yh", "yl", "c"), route)
        mine_swapped = lax.ppermute(mine, "c", [(0, 1), (1, 0)])
        theirs_swapped = lax.ppermute(theirs, "c", [(0, 1), (1, 0)])
        weights = [mine, mine_swapped, theirs, theirs_swapped]

    query, kv = row_project(
        place, near, far, row_gain.reshape(PARTS, 1, GROUP), row_qkv.reshape(PARTS, GROUP, 3 * GROUP)
    )
    before = lax.ppermute(kv, SEQ, [(i, i + 1) for i in range(127)])
    att = row_attend(place, query, kv, before)
    att = lax.all_to_all(att.reshape(PARTS, 128, GROUP), HEAD, 0, 0, tiled=True)
    hidden = row_output(place, att, near, far, weights)
    hidden = lax.all_to_all(hidden.reshape(128, 8, 128), SEQ, 0, 0, tiled=True)
    mixed = col_layer(hidden.reshape(128, 1024), col_gain.reshape(PARTS, 1, GROUP), weights)
    mixed = lax.all_to_all(mixed.reshape(512, 2, 128), HEAD + SEQ, 0, 0, tiled=True)
    return mixed.reshape(512, GROUP)


def solution(mesh):
    fine = Mesh(mesh.devices.reshape(4, 8, 4, 2, 2), SEQ + HEAD)
    return jax.shard_map(
        on_device,
        mesh=fine,
        in_specs=(
            P(SEQ, HEAD),
            P(),
            P(None, None, HEAD),
            P(HEAD, None),
            P(),
            P(None, None, HEAD),
            P(HEAD, None),
        ),
        out_specs=P(SEQ, HEAD),
        check_vma=False,
    )
```

time: 273 us -> 183 us (0.67)
  waiting for transfers between devices: 163 us -> 42.5 us
  blocking collectives: 21.3 us -> 82.4 us
  starting transfers between devices: 39 us -> 15.9 us
  local copies, waits for them, and re-layouts: 7.42 us -> 27.3 us
  matrix products: 17.9 us -> 0 us
  Pallas kernels: 0 us -> 13.6 us
  between operations: 13.4 us -> 0.16 us
  other arithmetic: 10.6 us -> 0.17 us
    reduce_scatter x2 -> x0, waiting for transfers between devices: 57.4 us -> none  [the longest x1 38.2 us: row_layer(): lax.psum_scatter(term.astype(jnp.bfloat16), 'head', scatter_dimension=1,...]
    all_gather x2 -> x0, waiting for transfers between devices: 57.1 us -> none  [the longest x1 32.1 us: row_layer(): full = lax.all_gather(source, 'head', axis=1, tiled=True)]
    all_to_all x1 -> x2, blocking collectives: 21.3 us -> 71.1 us  [the longest x1 44.5 us: on_device(): hidden = lax.all_to_all(hidden.reshape(128, 8, 128), SEQ, 0, 0, tiled=True)]
    all_to_all x3 -> x1, waiting for transfers between devices: 41.1 us -> 0.01 us  [on_device(): att = lax.all_to_all(att.reshape(PARTS, 128, GROUP), HEAD, 0, 0, tiled=True)]
    ppermute x2 -> x5, waiting for transfers between devices: 6.88 us -> 42.5 us  [the longest x1 29.5 us: on_device(): theirs = lax.ppermute(mine, ('yh', 'yl', 'c'), route)]
    all_to_all x3 -> x1, starting transfers between devices: 32.1 us -> 4.06 us  [on_device(): att = lax.all_to_all(att.reshape(PARTS, 128, GROUP), HEAD, 0, 0, tiled=True)]
    pallas_call x0 -> x4, Pallas kernels: none -> 13.6 us  [the longest x1 7.18 us: col_layer(): pl.pallas_call(col_layer_kernel, out_shape=jax.ShapeDtypeStruct((PARTS, 1...]
    dot_general x7 -> x0, matrix products: 12 us -> none  [the longest x1 4.83 us: one_row(): jnp.einsum('hqk,khe->qhe', weights, vals_row, preferred_element_type=jnp....]
  transfers between devices with their start and end apart: 9 -> 6, of which waited for: 9 -> 3; matrix products, arithmetic and copies ran while one was open for 3% -> 10% of each run, Pallas kernels for 0% -> 3%
where the time goes in v1:
time: 183 us; the launch traced here: 182 us
  blocking collectives  82.4 us (45%)
  waiting for transfers between devices  42.5 us (23%)
  local copies, waits for them, and re-layouts  27.3 us (15%)
  starting transfers between devices  15.9 us (9%)
  Pallas kernels  13.6 us (7%)
    all_to_all x1, blocking collectives, on_device(): hidden = lax.all_to_all(hidden.reshape(128, 8, 128), SEQ, 0, 0, tiled=True)  44.5 us
    ppermute x1, waiting for transfers between devices, on_device(): theirs = lax.ppermute(mine, ('yh', 'yl', 'c'), route)  29.5 us
    all_to_all x1, blocking collectives, on_device(): lax.all_to_all(mixed.reshape(512, 2, 128), HEAD + SEQ, 0, 0, tiled=True)  26.6 us
    ppermute x1, waiting for transfers between devices, on_device(): before = lax.ppermute(kv, SEQ, [(i, i + 1) for i in range(127)])  11.4 us
    reshape x2, local copies, waits for them, and re-layouts, on_device(): row_qkv.reshape(PARTS, GROUP, 3 * GROUP)  9.47 us
    all_gather x1, blocking collectives, on_device(): far = lax.all_gather(other, 'c', axis=0)  9.15 us
    unnamed x27, local copies, waits for them, and re-layouts  8.98 us
    pallas_call x1, Pallas kernels, col_layer(): pl.pallas_call(col_layer_kernel, out_shape=jax.ShapeDtypeStruct((PARTS, 1...  7.18 us
  transfers between devices with their start and end apart: 6, of which 3 were waited for; matrix products, arithmetic and copies ran while one was open for 10% of the time, Pallas kernels for 3%

profile of v1, /device:TPU:1, one launch (start us, length us, event | category | flops | bytes accessed | tf_op | source)
XLA Modules:
  0.0 182.1 jit_solution(16708070439834648520)
XLA Ops:
  0.0 4.2 %collective-permute-start = (bf16[512,256]{1,0:T(8,128)(2,1)}, bf16[512,256]{1,0:T(8,128)(2,1)S(1)}, u32[]{:S(2)}, u32[]{:S(2)}) collective-permute-start(bf16[512,256]{1,0:T(8,128)(2,1)} %param.7), channel_id=1, source_target_pairs={{0,2},{2,0},{1,3},{3,1},{4,6},{6,4},{5,7},{7,5},{8,10},{10,8},{9,1... | collective-permute-start | bytes 786440 | tf_op jit(solution)/shard_map/gather_inputs/ppermute | solution.py:224
  4.2 1.1 copy.27
  5.2 1.1 copy.26
  6.5 1.6 collective-permute-done
  8.1 9.2 %all-gather.1 = bf16[1024,256]{1,0:T(8,128)(2,1)S(1)} all-gather(bf16[512,256]{1,0:T(8,128)(2,1)S(1)} %collective-permute-done), channel_id=3, replica_groups=mesh['yh'=4,'z'=8,'x'=4,'yl'=2,'c'=2] {'c'}, dimensions={0}, use_global_device_ids=true | all-gather | bytes 786432 | tf_op jit(solution)/shard_map/gather_inputs/all_gather | solution.py:226
  17.3 1.9 %collective-permute-start.3 = (bf16[5120,256]{1,0:T(8,128)(2,1)S(1)}, bf16[5120,256]{1,0:T(8,128)(2,1)}, u32[]{:S(2)}, u32[]{:S(2)}) collective-permute-start(bf16[5120,256]{1,0:T(8,128)(2,1)S(1)} %pad_maximum_fusion.w0), channel_id=1, source_target_pairs={{0,2},{2,0},{3,129},{129,3},{128,130},{130,128},{131,257},{257,131... | collective-permute-start | bytes 7864328 | tf_op jit(solution)/shard_map/gather_weights/ppermute | solution.py:237
  19.2 2.3 %collective-permute-start.2 = (bf16[5120,256]{1,0:T(8,128)(2,1)S(1)}, bf16[5120,256]{1,0:T(8,128)(2,1)}, u32[]{:S(2)}, u32[]{:S(2)}) collective-permute-start(bf16[5120,256]{1,0:T(8,128)(2,1)S(1)} %pad_maximum_fusion.w0), channel_id=1, source_target_pairs={{0,1},{1,0},{2,3},{3,2},{4,5},{5,4},{6,7},{7,6},{8,9},{9,8},{10,11... | collective-permute-start | bytes 7864328 | tf_op jit(solution)/shard_map/gather_weights/ppermute | solution.py:238
  21.5 29.5 %collective-permute-done.3.w2 = bf16[5120,256]{1,0:T(8,128)(2,1)} collective-permute-done((bf16[5120,256]{1,0:T(8,128)(2,1)S(1)}, bf16[5120,256]{1,0:T(8,128)(2,1)}, u32[]{:S(2)}, u32[]{:S(2)}) %collective-permute-start.3) | collective-permute-done | bytes 2621472 | tf_op jit(solution)/shard_map/gather_weights/ppermute | solution.py:237
  51.0 2.2 %collective-permute-start.4 = (bf16[5120,256]{1,0:T(8,128)(2,1)}, bf16[5120,256]{1,0:T(8,128)(2,1)}, u32[]{:S(2)}, u32[]{:S(2)}) collective-permute-start(bf16[5120,256]{1,0:T(8,128)(2,1)} %collective-permute-done.3.w2), channel_id=1, source_target_pairs={{0,1},{1,0},{2,3},{3,2},{4,5},{5,4},{6,7},{7,6},{8,9},{9,8},{10,11... | collective-permute-start | bytes 7864328 | tf_op jit(solution)/shard_map/gather_weights/ppermute | solution.py:239
  53.2 4.2 %copy.15 = bf16[1024,3,256]{2,1,0:T(4,128)(2,1)} copy(bf16[1024,3,256]{2,0,1:T(8,128)(2,1)} %param.9) | data formatting | bytes 3145728 | tf_op jit(solution)/shard_map/reshape | solution.py:243
  57.4 5.3 %reshape.54.weight = bf16[4,256,768]{2,1,0:T(8,128)(2,1)} reshape(bf16[1024,3,256]{2,1,0:T(4,128)(2,1)} %copy.15) | data formatting | bytes 3145728 | tf_op jit(solution)/shard_map/reshape | solution.py:243
  62.8 2.2 %all-gather = bf16[1024,256]{1,0:T(8,128)(2,1)S(1)} all-gather(bf16[512,256]{1,0:T(8,128)(2,1)S(1)} %copy-done.11), channel_id=2, replica_groups=mesh['yh'=4,'z'=8,'x'=4,'yl'=2,'c'=2] {'c'}, dimensions={0}, use_global_device_ids=true | all-gather | bytes 786432 | tf_op jit(solution)/shard_map/gather_inputs/all_gather | solution.py:225
  64.9 1.4 copy-done.6
  66.4 2.3 %row_project.1 = (bf16[512,256]{1,0:T(8,128)(2,1)S(1)}, bf16[2,512,256]{2,1,0:T(8,128)(2,1)S(1)}) custom-call(s32[6]{0:T(128)S(1)} %stack.24.place, bf16[2,512,256]{2,1,0:T(8,128)(2,1)S(1)} %bitcast.39, bf16[2,512,256]{2,1,0:T(8,128)(2,1)S(1)} %bitcast.37, f32[4,1,256]{2,1,0:T(1,128)S(1)} %bitcast.45, bf16[4,256,768]{2,1,0:T(8,128)(2,1)S(1)} %copy-done.6), custom_call_target="tpu_custom_call" | custom-call | flops 805306368 | bytes 4194304 | tf_op jit(solution)/shard_map/row_project/pallas_call | solution.py:58
  69.5 1.3 collective-permute-start.1
  70.8 11.4 %collective-permute-done.1.before = bf16[2,512,256]{2,1,0:T(8,128)(2,1)S(1)} collective-permute-done((bf16[2,512,256]{2,1,0:T(8,128)(2,1)S(1)}, bf16[2,512,256]{2,1,0:T(8,128)(2,1)S(1)}, u32[]{:S(2)}, u32[]{:S(2)}) %collective-permute-start.1) | collective-permute-done | bytes 524320 | tf_op jit(solution)/shard_map/ppermute | solution.py:245
  82.2 3.1 %row_attend.1 = bf16[512,256]{1,0:T(8,128)(2,1)S(1)} custom-call(s32[6]{0:T(128)S(1)} %stack.24.place, bf16[512,256]{1,0:T(8,128)(2,1)S(1)} %get-tuple-element.10.query, bf16[2,512,256]{2,1,0:T(8,128)(2,1)S(1)} %get-tuple-element.11.kv, bf16[2,512,256]{2,1,0:T(8,128)(2,1)S(1)} %collective-permute-done.1.before), custom_call_target="tpu_custom_call" | custom-call | flops 1610612736 | bytes 2097152 | tf_op jit(solution)/shard_map/row_attend/pallas_call | solution.py:113
  86.0 4.1 %all-to-all-start = ((bf16[4,128,256]{2,1,0:T(8,128)(2,1)}), bf16[4,128,256]{2,1,0:T(8,128)(2,1)S(1)}, u32[]{:S(2)}, u32[]{:S(2)}) async-start(bf16[4,128,256]{2,1,0:T(8,128)(2,1)} %bitcast.43), calls=%async_computation | async-start | bytes 524288 | tf_op jit(solution)/shard_map/all_to_all | solution.py:247
  91.0 1.9 %slice.17.w2 = bf16[1024,256]{1,0:T(8,128)(2,1)} slice(bf16[5120,256]{1,0:T(8,128)(2,1)} %collective-permute-done.3.w2), slice={[0:1024], [0:256]} | slice | bytes 1048576 | tf_op jit(solution)/shard_map/slice | solution.py:156
  92.8 1.9 %slice.16.w1 = bf16[1024,256]{1,0:T(8,128)(2,1)} slice(bf16[5120,256]{1,0:T(8,128)(2,1)} %collective-permute-done.2.w1), slice={[0:1024], [0:256]} | slice | bytes 1048576 | tf_op jit(solution)/shard_map/slice | solution.py:156
  94.7 1.9 %slice.18.w3 = bf16[1024,256]{1,0:T(8,128)(2,1)} slice(bf16[5120,256]{1,0:T(8,128)(2,1)} %collective-permute-done.4.w3), slice={[0:1024], [0:256]} | slice | bytes 1048576 | tf_op jit(solution)/shard_map/slice | solution.py:156
  102.9 44.5 %all_to_all.15 = bf16[128,8,128]{2,1,0:T(8,128)(2,1)S(1)} all-to-all(bf16[128,8,128]{2,1,0:T(8,128)(2,1)S(1)} %bitcast.49), channel_id=1, replica_groups=mesh['yh'=4,'z'=8,'x'=4,'yl'=2,'c'=2] {'yh','z','x'}, dimensions={0} | all-to-all | bytes 524288 | tf_op jit(solution)/shard_map/all_to_all | solution.py:249
  147.5 7.2 %col_layer.1 = bf16[4,128,256]{2,1,0:T(8,128)(2,1)S(1)} custom-call(bf16[128,1024]{1,0:T(8,128)(2,1)S(1)} %bitcast.41, f32[4,1,256]{2,1,0:T(1,128)S(1)} %bitcast.44, bf16[5120,256]{1,0:T(8,128)(2,1)S(1)} %pad_maximum_fusion.w0, bf16[5120,256]{1,0:T(8,128)(2,1)} %collective-permute-done.2.w1, bf16[5120,256]{1,0:T(8,128)(2,1)} %collective-permute-done.3.w2, ...), custom_call_target="tpu_custom_call" | custom-call | flops 1073741824 | bytes 10485760 | tf_op jit(solution)/shard_map/col_layer/pallas_call | solution.py:204
  154.7 26.6 %all_to_all.16 = bf16[512,2,128]{2,1,0:T(2,128)(2,1)S(1)} all-to-all(bf16[512,2,128]{2,1,0:T(2,128)(2,1)S(1)} %reshape.50), channel_id=1, replica_groups=mesh['yh'=4,'z'=8,'x'=4,'yl'=2,'c'=2] {'yl','c','yh','z','x'}, dimensions={0} | all-to-all | bytes 524288 | tf_op jit(solution)/shard_map/all_to_all | solution.py:251
  (34 shorter events, 9.8 us)
Async XLA Ops:
  0.0 6.3 %copy-start.10 = (bf16[1024,3,256]{2,0,1:T(8,128)(2,1)S(1)}, bf16[1024,3,256]{2,0,1:T(8,128)(2,1)}, u32[]{:S(2)}) copy-start(bf16[1024,3,256]{2,0,1:T(8,128)(2,1)} %param.12) | copy-start | bytes 4718596
  0.0 8.1 %collective-permute-start = (bf16[512,256]{1,0:T(8,128)(2,1)}, bf16[512,256]{1,0:T(8,128)(2,1)S(1)}, u32[]{:S(2)}, u32[]{:S(2)}) collective-permute-start(bf16[512,256]{1,0:T(8,128)(2,1)} %param.7), channel_id=1, source_target_pairs={{0,2},{2,0},{1,3},{3,1},{4,6},{6,4},{5,7},{7,5},{8,10},{10,8},{9,1... | collective-permute-start | bytes 786440 | tf_op jit(solution)/shard_map/gather_inputs/ppermute | solution.py:224
  17.3 33.7 %collective-permute-start.3 = (bf16[5120,256]{1,0:T(8,128)(2,1)S(1)}, bf16[5120,256]{1,0:T(8,128)(2,1)}, u32[]{:S(2)}, u32[]{:S(2)}) collective-permute-start(bf16[5120,256]{1,0:T(8,128)(2,1)S(1)} %pad_maximum_fusion.w0), channel_id=1, source_target_pairs={{0,2},{2,0},{3,129},{129,3},{128,130},{130,128},{131,257},{257,131... | collective-permute-start | bytes 7864328 | tf_op jit(solution)/shard_map/gather_weights/ppermute | solution.py:237
  19.2 73.7 %collective-permute-start.2 = (bf16[5120,256]{1,0:T(8,128)(2,1)S(1)}, bf16[5120,256]{1,0:T(8,128)(2,1)}, u32[]{:S(2)}, u32[]{:S(2)}) collective-permute-start(bf16[5120,256]{1,0:T(8,128)(2,1)S(1)} %pad_maximum_fusion.w0), channel_id=1, source_target_pairs={{0,1},{1,0},{2,3},{3,2},{4,5},{5,4},{6,7},{7,6},{8,9},{9,8},{10,11... | collective-permute-start | bytes 7864328 | tf_op jit(solution)/shard_map/gather_weights/ppermute | solution.py:238
  51.0 43.8 %collective-permute-start.4 = (bf16[5120,256]{1,0:T(8,128)(2,1)}, bf16[5120,256]{1,0:T(8,128)(2,1)}, u32[]{:S(2)}, u32[]{:S(2)}) collective-permute-start(bf16[5120,256]{1,0:T(8,128)(2,1)} %collective-permute-done.3.w2), channel_id=1, source_target_pairs={{0,1},{1,0},{2,3},{3,2},{4,5},{5,4},{6,7},{7,6},{8,9},{9,8},{10,11... | collective-permute-start | bytes 7864328 | tf_op jit(solution)/shard_map/gather_weights/ppermute | solution.py:239
  57.4 5.4 %copy-start.11 = (bf16[512,256]{1,0:T(8,128)(2,1)S(1)}, bf16[512,256]{1,0:T(8,128)(2,1)}, u32[]{:S(2)}) copy-start(bf16[512,256]{1,0:T(8,128)(2,1)} %param.7) | copy-start | bytes 786436
  57.4 7.6 %copy-start.9 = (f32[1024]{0:T(1024)S(1)}, f32[1024]{0:T(1024)}, u32[]{:S(2)}) copy-start(f32[1024]{0:T(1024)} %param.8) | copy-start | bytes 12292
  64.9 1.4 copy-start.6
  68.7 0.8 copy-start
  69.5 12.7 %collective-permute-start.1 = (bf16[2,512,256]{2,1,0:T(8,128)(2,1)S(1)}, bf16[2,512,256]{2,1,0:T(8,128)(2,1)S(1)}, u32[]{:S(2)}, u32[]{:S(2)}) collective-permute-start(bf16[2,512,256]{2,1,0:T(8,128)(2,1)S(1)} %get-tuple-element.11.kv), channel_id=1, source_target_pairs={{0,4},{4,8},{8,12},{12,16},{16,20},{20,24},{24,28},{28,32},{32,36}... | collective-permute-start | bytes 1572872 | tf_op jit(solution)/shard_map/ppermute | solution.py:245
  85.3 0.7 copy-start.7
  86.0 10.6 %all-to-all-start = ((bf16[4,128,256]{2,1,0:T(8,128)(2,1)}), bf16[4,128,256]{2,1,0:T(8,128)(2,1)S(1)}, u32[]{:S(2)}, u32[]{:S(2)}) async-start(bf16[4,128,256]{2,1,0:T(8,128)(2,1)} %bitcast.43), calls=%async_computation | async-start | bytes 524288 | tf_op jit(solution)/shard_map/all_to_all | solution.py:247
  96.6 1.0 copy-start.1
  97.7 1.0 copy-start.2
  98.7 1.0 copy-start.3
  99.8 1.0 copy-start.4
  100.8 1.0 copy-start.5
  101.8 45.6 %copy-start.8 = (f32[1024]{0:T(1024)S(1)}, f32[1024]{0:T(1024)}, u32[]{:S(2)}) copy-start(f32[1024]{0:T(1024)} %param.11) | copy-start | bytes 12292

commit v2 on v1

v2 whole, which is shorter than its diff:
```python
import functools

import jax
import jax.numpy as jnp
from jax import lax
from jax.experimental import pallas as pl
from jax.experimental.pallas import tpu as pltpu
from jax.sharding import Mesh, PartitionSpec as P

COLS = 512
HEAD_DIM = 64
SEQ = ("yh", "z", "x")
HEAD = ("yl", "c")
GROUP = 256
PARTS = 4
HEADS_HERE = GROUP // HEAD_DIM
MIB = 1 << 20
VMEM = pl.BlockSpec(memory_space=pltpu.VMEM)
SMEM = pl.BlockSpec(memory_space=pltpu.SMEM)


def dot(a, b):
    return jnp.dot(a, b, preferred_element_type=jnp.float32)


def dot_t(a, b):
    return lax.dot_general(a, b, (((1,), (1,)), ((), ())), preferred_element_type=jnp.float32)


def normed_pieces(pieces, gains):
    flat = [p.astype(jnp.float32) for p in pieces]
    width = sum(p.shape[1] for p in pieces)
    mean = sum(jnp.sum(p, axis=-1, keepdims=True) for p in flat) / width
    flat = [p - mean for p in flat]
    var = sum(jnp.sum(p * p, axis=-1, keepdims=True) for p in flat) / width
    scale = lax.rsqrt(var + 1e-05)
    return [(p * scale * g).astype(jnp.bfloat16) for p, g in zip(flat, gains)]


def project(normed, order, weight, which):
    return sum(dot(p, weight[which, n]) for p, n in zip(normed, order)).astype(jnp.bfloat16)


def head_mask(rows, head):
    lane = lax.broadcasted_iota(jnp.int32, (rows, GROUP), 1)
    return (lane >= head * HEAD_DIM) & (lane < (head + 1) * HEAD_DIM)


def one_head(query, head):
    return jnp.where(head_mask(query.shape[0], head), query, jnp.bfloat16(0))


def triangle(block):
    row = lax.broadcasted_iota(jnp.int32, (block, block), 0)
    col = lax.broadcasted_iota(jnp.int32, (block, block), 1)
    return row, col


def attend_blocks(query, keys, vals, adjust):
    rows = query.shape[0]
    peak_all = norm_all = acc_all = jnp.zeros((rows, GROUP), jnp.float32)
    for head in range(HEADS_HERE):
        mask = head_mask(rows, head)
        qh = one_head(query, head)
        scores = [f(dot_t(qh, k)) for k, f in zip(keys, adjust)]
        peak = functools.reduce(jnp.maximum, scores)
        peak = jnp.max(peak, axis=-1, keepdims=True)
        expo = [jnp.exp(s - peak) for s in scores]
        norm = jnp.sum(sum(expo[1:], expo[0]), axis=-1, keepdims=True)
        acc = sum(dot(w.astype(jnp.bfloat16), v) for w, v in zip(expo, vals))
        peak_all = jnp.where(mask, peak, peak_all)
        norm_all = jnp.where(mask, norm, norm_all)
        acc_all = jnp.where(mask, acc, acc_all)
    return peak_all, norm_all, acc_all


BLOCK = 256
SCALE = HEAD_DIM ** (-0.5)


def row_own_kernel(place, near, far, gain, weight, query, peak, norm, acc, resid, kv):
    order = [place[0], place[0] + 1, place[1], place[1] + 1]
    mine = pl.ds(pl.multiple_of(place[3] * 128, 128), 128)
    for n, piece in zip(order, (near[0, mine], near[1, mine], far[0, mine], far[1, mine])):
        resid[n] = piece
    row, col = triangle(BLOCK)
    for i in range(COLS // BLOCK):
        rows = slice(i * BLOCK, (i + 1) * BLOCK)
        pieces = [near[0, rows], near[1, rows], far[0, rows], far[1, rows]]
        normed = normed_pieces(pieces, [gain[n] for n in order])
        query[rows] = project(normed, order, weight, 0) * jnp.bfloat16(SCALE)
        kv[0, rows] = project(normed, order, weight, 1)
        kv[1, rows] = project(normed, order, weight, 2)
    for i in range(COLS // BLOCK):
        rows = slice(i * BLOCK, (i + 1) * BLOCK)
        parts = [slice(j * BLOCK, (j + 1) * BLOCK) for j in range(i + 1)]
        adjust = [lambda s: s] * i + [lambda s: jnp.where(col <= row, s, -1e30)]
        peak[rows], norm[rows], acc[rows] = attend_blocks(
            query[rows], [kv[0, p] for p in parts], [kv[1, p] for p in parts], adjust
        )


def row_own(place, near, far, gain, weight):
    return pl.pallas_call(
        row_own_kernel,
        out_shape=(
            jax.ShapeDtypeStruct((COLS, GROUP), jnp.bfloat16),
            *[jax.ShapeDtypeStruct((COLS, GROUP), jnp.float32)] * 3,
            jax.ShapeDtypeStruct((PARTS, 128, GROUP), jnp.bfloat16),
        ),
        in_specs=[SMEM, VMEM, VMEM, VMEM, VMEM],
        out_specs=(VMEM,) * 5,
        scratch_shapes=[pltpu.VMEM((2, COLS, GROUP), jnp.bfloat16)],
        compiler_params=pltpu.CompilerParams(vmem_limit_bytes=16 * MIB),
        cost_estimate=pl.CostEstimate(
            flops=2 * COLS * 1024 * 768 + 4 * COLS * 384 * 1024,
            bytes_accessed=5 * MIB,
            transcendentals=4 * COLS * 384,
        ),
        name="row_own",
    )(place, near, far, gain, weight)


def row_halo_kernel(place, near, far, gain, weight, query, peak, norm, acc, out, kv):
    order = [place[0], place[0] + 1, place[1], place[1] + 1]
    row, col = triangle(BLOCK)
    blocked = jnp.where(place[2] > 0, 0.0, -1e30).astype(jnp.float32)
    blocks = COLS // BLOCK
    for i in range(blocks):
        rows = slice(i * BLOCK, (i + 1) * BLOCK)
        pieces = [near[0, rows], near[1, rows], far[0, rows], far[1, rows]]
        normed = normed_pieces(pieces, [gain[n] for n in order])
        kv[0, rows] = project(normed, order, weight, 1)
        kv[1, rows] = project(normed, order, weight, 2)
    for i in range(blocks):
        rows = slice(i * BLOCK, (i + 1) * BLOCK)
        parts = [slice(j * BLOCK, (j + 1) * BLOCK) for j in range(i, blocks)]
        adjust = [lambda s: jnp.where(col > row, s, -1e30) + blocked] + [lambda s: s + blocked] * (blocks - 1 - i)
        peak2, norm2, acc2 = attend_blocks(
            query[rows], [kv[0, p] for p in parts], [kv[1, p] for p in parts], adjust
        )
        top = jnp.maximum(peak[rows], peak2)
        one, two = jnp.exp(peak[rows] - top), jnp.exp(peak2 - top)
        att = (acc[rows] * one + acc2 * two) / (norm[rows] * one + norm2 * two)
        att = att.astype(jnp.bfloat16)
        for j in range(BLOCK // 128):
            out[i * BLOCK // 128 + j] = att[j * 128 : (j + 1) * 128]


def row_halo(place, near, far, gain, weight, state):
    return pl.pallas_call(
        row_halo_kernel,
        out_shape=jax.ShapeDtypeStruct((PARTS, 128, GROUP), jnp.bfloat16),
        in_specs=[SMEM] + [VMEM] * 8,
        out_specs=VMEM,
        scratch_shapes=[pltpu.VMEM((2, COLS, GROUP), jnp.bfloat16)],
        compiler_params=pltpu.CompilerParams(vmem_limit_bytes=16 * MIB),
        cost_estimate=pl.CostEstimate(
            flops=2 * COLS * 1024 * 512 + 4 * COLS * 384 * 1024,
            bytes_accessed=5 * MIB,
            transcendentals=4 * COLS * 384,
        ),
        name="row_halo",
    )(place, near, far, gain, weight, *state)


OUT_ROWS, COL_ROWS = 1024, 4096


def column_blocks(w):
    return w.reshape(GROUP, PARTS, GROUP).transpose(1, 0, 2).reshape(PARTS * GROUP, GROUP)


ANY = pl.BlockSpec(memory_space=pl.ANY)


def row_out_kernel(place, att, resid, weights, swapped, out, held, sem):
    copies = [pltpu.make_async_copy(w, held.at[i], sem.at[i]) for i, w in enumerate((weights, swapped))]
    for copy in copies:
        copy.start()
    groups = [place[0] + place[4], place[1] + place[4], place[0] + 1 - place[4], place[1] + 1 - place[4]]
    parts = [att[g] for g in groups]
    for copy in copies:
        copy.wait()
    for n in range(PARTS):
        cols = slice(n * GROUP, (n + 1) * GROUP)
        total = 0
        for i, p in enumerate(parts):
            first = (i % 2) * OUT_ROWS + n * GROUP
            total = total + dot(p, held[i // 2, first : first + GROUP, :])
        out[:, cols] = (resid[n].astype(jnp.float32) + total).astype(jnp.bfloat16)


def row_output(place, att, resid, weights, swapped):
    return pl.pallas_call(
        row_out_kernel,
        out_shape=jax.ShapeDtypeStruct((128, 1024), jnp.bfloat16),
        in_specs=[SMEM, VMEM, VMEM, ANY, ANY],
        out_specs=VMEM,
        scratch_shapes=[pltpu.VMEM((2, 2 * OUT_ROWS, GROUP), jnp.bfloat16), pltpu.SemaphoreType.DMA((2,))],
        compiler_params=pltpu.CompilerParams(vmem_limit_bytes=10 * MIB),
        cost_estimate=pl.CostEstimate(
            flops=2 * 128 * 1024 * 1024, bytes_accessed=4 * MIB, transcendentals=0
        ),
        name="row_output",
    )(place, att, resid, weights, swapped)


def col_layer_kernel(hidden, gain, w0, w1, w2, w3, out, held, sem):
    copies = [
        pltpu.make_async_copy(w, held.at[i], sem.at[i]) for i, w in enumerate((w0, w1, w2, w3))
    ]
    for copy in copies:
        copy.start()
    h = hidden[...]
    pieces = [h[:, n * GROUP : (n + 1) * GROUP] for n in range(PARTS)]
    normed = normed_pieces(pieces, [gain[n] for n in range(PARTS)])
    normed = jnp.concatenate(normed, axis=1)
    row, col = triangle(h.shape[0])
    atts = []
    for i, copy in enumerate(copies):
        copy.wait()
        q, k, v = [
            dot(normed, held[i, j * 1024 : (j + 1) * 1024, :]).astype(jnp.bfloat16) for j in range(3)
        ]
        _, norm, acc = attend_blocks(
            q * jnp.bfloat16(SCALE), [k], [v], [lambda s: jnp.where(col <= row, s, -1e30)]
        )
        atts.append((acc / norm).astype(jnp.bfloat16))
    for n in range(PARTS):
        rows = slice(3 * 1024 + n * GROUP, 3 * 1024 + (n + 1) * GROUP)
        total = sum(dot(a, held[i, rows, :]) for i, a in enumerate(atts))
        out[n] = (pieces[n].astype(jnp.float32) + total).astype(jnp.bfloat16)


def col_layer(hidden, gain, weights):
    return pl.pallas_call(
        col_layer_kernel,
        out_shape=jax.ShapeDtypeStruct((PARTS, 128, GROUP), jnp.bfloat16),
        in_specs=[VMEM] * 2 + [ANY] * 4,
        out_specs=VMEM,
        scratch_shapes=[pltpu.VMEM((PARTS, COL_ROWS, GROUP), jnp.bfloat16), pltpu.SemaphoreType.DMA((PARTS,))],
        compiler_params=pltpu.CompilerParams(vmem_limit_bytes=20 * MIB),
        cost_estimate=pl.CostEstimate(
            flops=2 * 128 * 1024 * 4096, bytes_accessed=10 * MIB, transcendentals=16 * 128 * 128
        ),
        name="col_layer",
    )(hidden, gain, *weights)


SWAP = [(0, 1), (1, 0)]


def after(value, *others):
    return lax.optimization_barrier((value, *others))[0]


def cross_route():
    route = []
    for yh in range(4):
        a, b = yh * 4, yh * 4 + 2
        route += [(a, b), (b, a)]
        a, b = yh * 4 + 3, ((yh + 1) % 4) * 4 + 1
        route += [(a, b), (b, a)]
    return route


def on_device(inputs, row_gain, row_qkv, row_out, col_gain, col_qkv, col_out):
    yl, core = lax.axis_index("yl"), lax.axis_index("c")
    place = jnp.stack([yl * 2, (1 - yl) * 2, lax.axis_index(SEQ), yl * 2 + core, core]).astype(jnp.int32)
    row_gain = row_gain.reshape(PARTS, 1, GROUP)
    row_qkv = row_qkv.transpose(1, 0, 2).reshape(3, PARTS, GROUP, GROUP)
    everywhere = ("yh", "yl", "c")

    other = lax.ppermute(inputs, "yl", SWAP)
    before = lax.ppermute(inputs, SEQ, [(i, i + 1) for i in range(127)])
    near = lax.all_gather(inputs, "c", axis=0)
    far = lax.all_gather(after(other, near), "c", axis=0)
    before_other = lax.ppermute(after(before, far), "yl", SWAP)

    out_mine = column_blocks(row_out)
    col_mine = jnp.concatenate([col_qkv.transpose(1, 0, 2).reshape(3 * 1024, GROUP), column_blocks(col_out)])
    out_mine = after(out_mine, far)
    out_theirs = lax.ppermute(out_mine, everywhere, cross_route())
    col_mine = after(col_mine, before, far)
    col_theirs = lax.ppermute(col_mine, everywhere, cross_route())
    col_swapped = lax.ppermute(col_mine, "c", SWAP)

    *state, resid = row_own(place, near, far, row_gain, row_qkv)
    before_near = lax.all_gather(after(before, resid), "c", axis=0)
    before_far = lax.all_gather(after(before_other, before_near), "c", axis=0)
    out_both = jnp.concatenate([out_mine, after(out_theirs, before_far)])
    out_swapped = lax.ppermute(out_both, "c", SWAP)
    att = row_halo(place, before_near, before_far, row_gain, row_qkv, state)
    att = lax.all_to_all(att, HEAD, 0, 0, tiled=True)
    hidden = row_output(place, att, resid, out_both, out_swapped)
    col_theirs = after(col_theirs, hidden)
    col_theirs_swapped = lax.ppermute(col_theirs, "c", SWAP)
    hidden = lax.all_to_all(hidden.reshape(128, 8, 128), SEQ, 0, 0, tiled=True)
    mixed = col_layer(
        hidden.reshape(128, 1024),
        col_gain.reshape(PARTS, 1, GROUP),
        [col_mine, col_swapped, col_theirs, col_theirs_swapped],
    )
    mixed = lax.all_to_all(mixed.reshape(512, 2, 128), HEAD + SEQ, 0, 0, tiled=True)
    return mixed.reshape(512, GROUP)


def solution(mesh):
    fine = Mesh(mesh.devices.reshape(4, 8, 4, 2, 2), SEQ + HEAD)
    return jax.shard_map(
        on_device,
        mesh=fine,
        in_specs=(
            P(SEQ, HEAD),
            P(),
            P(None, None, HEAD),
            P(HEAD, None),
            P(),
            P(None, None, HEAD),
            P(HEAD, None),
        ),
        out_specs=P(SEQ, HEAD),
        check_vma=False,
    )
```

time: 183 us -> 152 us (0.83)
  waiting for transfers between devices: 42.5 us -> 9.61 us
  starting transfers between devices: 15.9 us -> 36.8 us
  local copies, waits for them, and re-layouts: 27.3 us -> 7.08 us
    ppermute x5 -> x8, waiting for transfers between devices: 42.5 us -> 6.4 us  [the longest x1 6.38 us: on_device(): out_theirs = lax.ppermute(out_mine, everywhere, cross_route())]
    ppermute x5 -> x8, starting transfers between devices: 11.9 us -> 32.8 us  [the longest x1 13.1 us: on_device(): col_theirs = lax.ppermute(col_mine, everywhere, cross_route())]
    reshape x4 -> x2, local copies, waits for them, and re-layouts: 11.6 us -> 2.95 us  [column_blocks(): w.reshape(GROUP, PARTS, GROUP).transpose(1, 0, 2)]
    all_to_all x1, blocking collectives: 44.5 us -> 36.7 us  [on_device(): hidden = lax.all_to_all(hidden.reshape(128, 8, 128), SEQ, 0, 0, tiled=True)]
    slice x4 -> x0, local copies, waits for them, and re-layouts: 6.53 us -> none  [row_output(): weights = [w[ROW_OUT:ROW_OUT + 1024] for w in weights]]
    unnamed x27 -> x22, local copies, waits for them, and re-layouts: 8.98 us -> 3.94 us
    all_gather x1 -> x3, blocking collectives: 9.15 us -> 13.9 us  [the longest x1 7.76 us: on_device(): before_far = lax.all_gather(after(before_other, before_near), 'c', axis=0)]
    all_to_all x1, waiting for transfers between devices: 0.01 us -> 3.21 us  [on_device(): att = lax.all_to_all(att, HEAD, 0, 0, tiled=True)]
  transfers between devices with their start and end apart: 6 -> 9, of which waited for: 3 -> 2; matrix products, arithmetic and copies ran while one was open for 10% -> 3% of each run, Pallas kernels for 3% -> 6%
where the time goes in v2:
time: 152 us; the launch traced here: 151 us
  blocking collectives  82.1 us (54%)
  starting transfers between devices  36.8 us (24%)
  Pallas kernels  13.7 us (9%)
  waiting for transfers between devices  9.61 us (6%)
  local copies, waits for them, and re-layouts  7.08 us (5%)
  other arithmetic  1.59 us (1%)
    all_to_all x1, blocking collectives, on_device(): hidden = lax.all_to_all(hidden.reshape(128, 8, 128), SEQ, 0, 0, tiled=True)  36.7 us
    all_to_all x1, blocking collectives, on_device(): lax.all_to_all(mixed.reshape(512, 2, 128), HEAD + SEQ, 0, 0, tiled=True)  26.7 us
    ppermute x1, starting transfers between devices, on_device(): col_theirs = lax.ppermute(col_mine, everywhere, cross_route())  13.1 us
    all_gather x1, blocking collectives, on_device(): before_far = lax.all_gather(after(before_other, before_near), 'c', axis=0)  7.76 us
    ppermute x1, waiting for transfers between devices, on_device(): out_theirs = lax.ppermute(out_mine, everywhere, cross_route())  6.38 us
    pallas_call x1, Pallas kernels, col_layer(): pl.pallas_call(col_layer_kernel, out_shape=jax.ShapeDtypeStruct((PARTS, 1...  4.98 us
    all_gather x1, blocking collectives, on_device(): near = lax.all_gather(inputs, 'c', axis=0)  4.75 us
    ppermute x1, starting transfers between devices, on_device(): out_theirs = lax.ppermute(out_mine, everywhere, cross_route())  4.03 us
  transfers between devices with their start and end apart: 9, of which 2 were waited for; matrix products, arithmetic and copies ran while one was open for 3% of the time, Pallas kernels for 6%

profile of v2, /device:TPU:1, one launch (start us, length us, event | category | flops | bytes accessed | tf_op | source)
XLA Modules:
  0.0 151.1 jit_solution(14517123997964366706)
XLA Ops:
  0.0 4.0 %collective-permute-start = (bf16[512,256]{1,0:T(8,128)(2,1)}, bf16[512,256]{1,0:T(8,128)(2,1)S(1)}, u32[]{:S(2)}, u32[]{:S(2)}) collective-permute-start(bf16[512,256]{1,0:T(8,128)(2,1)} %param.7), channel_id=1, source_target_pairs={{0,4},{4,8},{8,12},{12,16},{16,20},{20,24},{24,28},{28,32},{32,36}... | collective-permute-start | bytes 786440 | tf_op jit(solution)/shard_map/ppermute | solution.py:276
  4.0 3.2 %collective-permute-start.1 = (bf16[512,256]{1,0:T(8,128)(2,1)}, bf16[512,256]{1,0:T(8,128)(2,1)S(1)}, u32[]{:S(2)}, u32[]{:S(2)}) collective-permute-start(bf16[512,256]{1,0:T(8,128)(2,1)} %param.7), channel_id=1, source_target_pairs={{0,2},{2,0},{1,3},{3,1},{4,6},{6,4},{5,7},{7,5},{8,10},{10,8},{9,1... | collective-permute-start | bytes 786440 | tf_op jit(solution)/shard_map/ppermute | solution.py:275
  8.3 1.6 %pad_maximum_fusion.w0 = bf16[4096,256]{1,0:T(8,128)(2,1)S(1)} fusion(bf16[1024,256]{1,0:T(8,128)(2,1)S(1)} %bitcast.54, bf16[3072,256]{1,0:T(8,128)(2,1)} %bitcast.55), kind=kLoop, calls=%fused_computation | loop fusion | flops 4194304 | bytes 4194304 | tf_op jit(solution)/shard_map/concatenate | solution.py:282
  9.9 4.7 %all-gather = bf16[1024,256]{1,0:T(8,128)(2,1)S(1)} all-gather(bf16[512,256]{1,0:T(8,128)(2,1)S(1)} %copy-done.8), channel_id=2, replica_groups=mesh['yh'=4,'z'=8,'x'=4,'yl'=2,'c'=2] {'c'}, dimensions={0}, use_global_device_ids=true | all-gather | bytes 786432 | tf_op jit(solution)/shard_map/all_gather | solution.py:277
  14.6 3.8 %all-gather.1 = bf16[1024,256]{1,0:T(8,128)(2,1)S(1)} all-gather(bf16[512,256]{1,0:T(8,128)(2,1)S(1)} %collective-permute-done.1), channel_id=3, replica_groups=mesh['yh'=4,'z'=8,'x'=4,'yl'=2,'c'=2] {'c'}, dimensions={0}, use_global_device_ids=true | all-gather | bytes 786432 | tf_op jit(solution)/shard_map/all_gather | solution.py:278
  18.5 13.1 %collective-permute-start.6 = (bf16[4096,256]{1,0:T(8,128)(2,1)S(1)}, bf16[4096,256]{1,0:T(8,128)(2,1)}, u32[]{:S(2)}, u32[]{:S(2)}) collective-permute-start(bf16[4096,256]{1,0:T(8,128)(2,1)S(1)} %pad_maximum_fusion.w0), channel_id=1, source_target_pairs={{0,2},{2,0},{3,129},{129,3},{128,130},{130,128},{131,257},{257,131... | collective-permute-start | bytes 6291464 | tf_op jit(solution)/shard_map/ppermute | solution.py:286
  31.5 1.9 %copy.20 = bf16[32,4,8,256]{3,2,0,1:T(8,128)(2,1)} copy(bf16[32,4,8,256]{3,2,1,0:T(8,128)(2,1)} %bitcast.60) | data formatting | bytes 1048576 | tf_op jit(solution)/shard_map/reshape | solution.py:171
  33.5 1.9 %collective-permute-start.2 = (bf16[512,256]{1,0:T(8,128)(2,1)S(1)}, bf16[512,256]{1,0:T(8,128)(2,1)S(1)}, u32[]{:S(2)}, u32[]{:S(2)}) collective-permute-start(bf16[512,256]{1,0:T(8,128)(2,1)S(1)} %collective-permute-done), channel_id=1, source_target_pairs={{0,2},{2,0},{1,3},{3,1},{4,6},{6,4},{5,7},{7,5},{8,10},{10,8},{9,1... | collective-permute-start | bytes 786440 | tf_op jit(solution)/shard_map/ppermute | solution.py:279
  35.4 4.0 %collective-permute-start.3 = (bf16[1024,256]{1,0:T(8,128)(2,1)}, bf16[1024,256]{1,0:T(8,128)(2,1)S(1)}, u32[]{:S(2)}, u32[]{:S(2)}) collective-permute-start(bf16[1024,256]{1,0:T(8,128)(2,1)} %bitcast.52), channel_id=1, source_target_pairs={{0,2},{2,0},{3,129},{129,3},{128,130},{130,128},{131,257},{257,131... | collective-permute-start | bytes 1572872 | tf_op jit(solution)/shard_map/ppermute | solution.py:284
  39.5 1.4 copy-done.4
  40.9 3.1 %row_own.1 = (bf16[512,256]{1,0:T(8,128)(2,1)S(1)}, f32[512,256]{1,0:T(8,128)S(1)}, f32[512,256]{1,0:T(8,128)S(1)}, f32[512,256]{1,0:T(8,128)S(1)}, bf16[4,128,256]{2,1,0:T(8,128)(2,1)S(1)}) custom-call(s32[5]{0:T(128)S(1)} %stack.23.place, bf16[2,512,256]{2,1,0:T(8,128)(2,1)S(1)} %bitcast.43, bf16[2,512,256]{2,1,0:T(8,128)(2,1)S(1)} %bitcast.44, ...), custom_call_target="tpu_custom_call" | custom-call | flops 1610612736 | bytes 5242880 | tf_op jit(solution)/shard_map/row_own/pallas_call | solution.py:104
  44.1 2.3 %all-gather.2 = bf16[1024,256]{1,0:T(8,128)(2,1)S(1)} all-gather(bf16[512,256]{1,0:T(8,128)(2,1)S(1)} %collective-permute-done), channel_id=4, replica_groups=mesh['yh'=4,'z'=8,'x'=4,'yl'=2,'c'=2] {'c'}, dimensions={0}, use_global_device_ids=true | all-gather | bytes 786432 | tf_op jit(solution)/shard_map/all_gather | solution.py:290
  46.4 7.8 %all-gather.3 = bf16[1024,256]{1,0:T(8,128)(2,1)S(1)} all-gather(bf16[512,256]{1,0:T(8,128)(2,1)S(1)} %collective-permute-done.2), channel_id=5, replica_groups=mesh['yh'=4,'z'=8,'x'=4,'yl'=2,'c'=2] {'c'}, dimensions={0}, use_global_device_ids=true | all-gather | bytes 786432 | tf_op jit(solution)/shard_map/all_gather | solution.py:291
  54.2 6.4 %collective-permute-done.3 = bf16[1024,256]{1,0:T(8,128)(2,1)S(1)} collective-permute-done((bf16[1024,256]{1,0:T(8,128)(2,1)}, bf16[1024,256]{1,0:T(8,128)(2,1)S(1)}, u32[]{:S(2)}, u32[]{:S(2)}) %collective-permute-start.3) | collective-permute-done | bytes 524320 | tf_op jit(solution)/shard_map/ppermute | solution.py:284
  60.6 1.9 %collective-permute-start.4 = (bf16[2048,256]{1,0:T(8,128)(2,1)S(1)}, bf16[2048,256]{1,0:T(8,128)(2,1)}, u32[]{:S(2)}, u32[]{:S(2)}) collective-permute-start(bf16[2048,256]{1,0:T(8,128)(2,1)S(1)} %constant_dynamic-update-slice_fusion.weights), channel_id=1, source_target_pairs={{0,1},{1,0},{2,3},{3,2},{4,5},{5,4},{6,7},{7,6},{8,9},{9,8},{10,11... | collective-permute-start | bytes 3145736 | tf_op jit(solution)/shard_map/ppermute | solution.py:293
  62.5 3.3 %row_halo.1 = bf16[4,128,256]{2,1,0:T(8,128)(2,1)S(1)} custom-call(s32[5]{0:T(128)S(1)} %stack.23.place, bf16[2,512,256]{2,1,0:T(8,128)(2,1)S(1)} %bitcast.45, bf16[2,512,256]{2,1,0:T(8,128)(2,1)S(1)} %bitcast.46, f32[4,1,256]{2,1,0:T(1,128)S(1)} %bitcast.51, bf16[3,4,256,256]{3,2,1,0:T(8,128)(2,1)S(1)} %bitcast.49, ...), custom_call_target="tpu_custom_call" | custom-call | flops 1342177280 | bytes 5242880 | tf_op jit(solution)/shard_map/row_halo/pallas_call | solution.py:151
  66.5 4.0 %all-to-all-start = ((bf16[4,128,256]{2,1,0:T(8,128)(2,1)}), bf16[4,128,256]{2,1,0:T(8,128)(2,1)S(1)}, u32[]{:S(2)}, u32[]{:S(2)}) async-start(bf16[4,128,256]{2,1,0:T(8,128)(2,1)} %copy-done.2), calls=%async_computation | async-start | bytes 524288 | tf_op jit(solution)/shard_map/all_to_all | solution.py:295
  70.5 1.9 %collective-permute-start.5 = (bf16[4096,256]{1,0:T(8,128)(2,1)S(1)}, bf16[4096,256]{1,0:T(8,128)(2,1)}, u32[]{:S(2)}, u32[]{:S(2)}) collective-permute-start(bf16[4096,256]{1,0:T(8,128)(2,1)S(1)} %pad_maximum_fusion.w0), channel_id=1, source_target_pairs={{0,1},{1,0},{2,3},{3,2},{4,5},{5,4},{6,7},{7,6},{8,9},{9,8},{10,11... | collective-permute-start | bytes 6291464 | tf_op jit(solution)/shard_map/ppermute | solution.py:287
  72.5 3.2 %all-to-all-done.att = bf16[4,128,256]{2,1,0:T(8,128)(2,1)S(1)} async-done(((bf16[4,128,256]{2,1,0:T(8,128)(2,1)}), bf16[4,128,256]{2,1,0:T(8,128)(2,1)S(1)}, u32[]{:S(2)}, u32[]{:S(2)}) %all-to-all-start) | async-done | bytes 262176 | tf_op jit(solution)/shard_map/all_to_all | solution.py:295
  76.7 2.3 %row_output.1 = bf16[128,1024]{1,0:T(8,128)(2,1)S(1)} custom-call(s32[5]{0:T(128)S(1)} %stack.23.place, bf16[4,128,256]{2,1,0:T(8,128)(2,1)S(1)} %all-to-all-done.att, bf16[4,128,256]{2,1,0:T(8,128)(2,1)S(1)} %copy-done.1, bf16[2048,256]{1,0:T(8,128)(2,1)S(1)} %constant_dynamic-update-slice_fusion.weights, bf16[2048,256]{1,0:T(8,128)(2,1)} %collective-permute-done.4.swapped), custom_call_target="tpu_custom_call" | custom-call | flops 268435456 | bytes 4194304 | tf_op jit(solution)/shard_map/row_output/pallas_call | solution.py:195
  79.0 2.8 %collective-permute-start.7 = (bf16[4096,256]{1,0:T(8,128)(2,1)}, bf16[4096,256]{1,0:T(8,128)(2,1)S(1)}, u32[]{:S(2)}, u32[]{:S(2)}) collective-permute-start(bf16[4096,256]{1,0:T(8,128)(2,1)} %collective-permute-done.6.w2), channel_id=1, source_target_pairs={{0,1},{1,0},{2,3},{3,2},{4,5},{5,4},{6,7},{7,6},{8,9},{9,8},{10,11... | collective-permute-start | bytes 6291464 | tf_op jit(solution)/shard_map/ppermute | solution.py:298
  81.8 36.7 %all_to_all.15 = bf16[128,8,128]{2,1,0:T(8,128)(2,1)S(1)} all-to-all(bf16[128,8,128]{2,1,0:T(8,128)(2,1)S(1)} %bitcast.56), channel_id=1, replica_groups=mesh['yh'=4,'z'=8,'x'=4,'yl'=2,'c'=2] {'yh','z','x'}, dimensions={0} | all-to-all | bytes 524288 | tf_op jit(solution)/shard_map/all_to_all | solution.py:299
  118.6 5.0 %col_layer.1 = bf16[4,128,256]{2,1,0:T(8,128)(2,1)S(1)} custom-call(bf16[128,1024]{1,0:T(8,128)(2,1)S(1)} %bitcast.42, f32[4,1,256]{2,1,0:T(1,128)S(1)} %bitcast.47, bf16[4096,256]{1,0:T(8,128)(2,1)S(1)} %pad_maximum_fusion.w0, bf16[4096,256]{1,0:T(8,128)(2,1)} %collective-permute-done.5.w1, bf16[4096,256]{1,0:T(8,128)(2,1)} %collective-permute-done.6.w2, ...), custom_call_target="tpu_custom_call" | custom-call | flops 1073741824 | bytes 10485760 | tf_op jit(solution)/shard_map/col_layer/pallas_call | solution.py:237
  123.7 26.7 %all_to_all.16 = bf16[512,2,128]{2,1,0:T(2,128)(2,1)S(1)} all-to-all(bf16[512,2,128]{2,1,0:T(2,128)(2,1)S(1)} %reshape.46), channel_id=1, replica_groups=mesh['yh'=4,'z'=8,'x'=4,'yl'=2,'c'=2] {'yl','c','yh','z','x'}, dimensions={0} | all-to-all | bytes 524288 | tf_op jit(solution)/shard_map/all_to_all | solution.py:305
  (32 shorter events, 3.8 us)
Async XLA Ops:
  0.0 18.5 %collective-permute-start = (bf16[512,256]{1,0:T(8,128)(2,1)}, bf16[512,256]{1,0:T(8,128)(2,1)S(1)}, u32[]{:S(2)}, u32[]{:S(2)}) collective-permute-start(bf16[512,256]{1,0:T(8,128)(2,1)} %param.7), channel_id=1, source_target_pairs={{0,4},{4,8},{8,12},{12,16},{16,20},{20,24},{24,28},{28,32},{32,36}... | collective-permute-start | bytes 786440 | tf_op jit(solution)/shard_map/ppermute | solution.py:276
  4.0 10.7 %collective-permute-start.1 = (bf16[512,256]{1,0:T(8,128)(2,1)}, bf16[512,256]{1,0:T(8,128)(2,1)S(1)}, u32[]{:S(2)}, u32[]{:S(2)}) collective-permute-start(bf16[512,256]{1,0:T(8,128)(2,1)} %param.7), channel_id=1, source_target_pairs={{0,2},{2,0},{1,3},{3,1},{4,6},{6,4},{5,7},{7,5},{8,10},{10,8},{9,1... | collective-permute-start | bytes 786440 | tf_op jit(solution)/shard_map/ppermute | solution.py:275
  8.3 1.6 %copy-start.8 = (bf16[512,256]{1,0:T(8,128)(2,1)S(1)}, bf16[512,256]{1,0:T(8,128)(2,1)}, u32[]{:S(2)}) copy-start(bf16[512,256]{1,0:T(8,128)(2,1)} %param.7) | copy-start | bytes 786436
  9.9 29.6 %copy-start.6 = (f32[1024]{0:T(1024)S(1)}, f32[1024]{0:T(1024)}, u32[]{:S(2)}) copy-start(f32[1024]{0:T(1024)} %param.8) | copy-start | bytes 12292
  18.5 60.5 %collective-permute-start.6 = (bf16[4096,256]{1,0:T(8,128)(2,1)S(1)}, bf16[4096,256]{1,0:T(8,128)(2,1)}, u32[]{:S(2)}, u32[]{:S(2)}) collective-permute-start(bf16[4096,256]{1,0:T(8,128)(2,1)S(1)} %pad_maximum_fusion.w0), channel_id=1, source_target_pairs={{0,2},{2,0},{3,129},{129,3},{128,130},{130,128},{131,257},{257,131... | collective-permute-start | bytes 6291464 | tf_op jit(solution)/shard_map/ppermute | solution.py:286
  33.5 12.9 %collective-permute-start.2 = (bf16[512,256]{1,0:T(8,128)(2,1)S(1)}, bf16[512,256]{1,0:T(8,128)(2,1)S(1)}, u32[]{:S(2)}, u32[]{:S(2)}) collective-permute-start(bf16[512,256]{1,0:T(8,128)(2,1)S(1)} %collective-permute-done), channel_id=1, source_target_pairs={{0,2},{2,0},{1,3},{3,1},{4,6},{6,4},{5,7},{7,5},{8,10},{10,8},{9,1... | collective-permute-start | bytes 786440 | tf_op jit(solution)/shard_map/ppermute | solution.py:279
  35.4 25.1 %collective-permute-start.3 = (bf16[1024,256]{1,0:T(8,128)(2,1)}, bf16[1024,256]{1,0:T(8,128)(2,1)S(1)}, u32[]{:S(2)}, u32[]{:S(2)}) collective-permute-start(bf16[1024,256]{1,0:T(8,128)(2,1)} %bitcast.52), channel_id=1, source_target_pairs={{0,2},{2,0},{3,129},{129,3},{128,130},{130,128},{131,257},{257,131... | collective-permute-start | bytes 1572872 | tf_op jit(solution)/shard_map/ppermute | solution.py:284
  39.5 1.4 copy-start.4
  40.9 3.2 %copy-start.7 = (bf16[32,4,8,256]{3,2,0,1:T(8,128)(2,1)S(1)}, bf16[32,4,8,256]{3,2,0,1:T(8,128)(2,1)}, u32[]{:S(2)}) copy-start(bf16[32,4,8,256]{3,2,0,1:T(8,128)(2,1)} %copy.20) | copy-start | bytes 1572868
  44.0 16.6 %copy-start = (bf16[4,128,256]{2,1,0:T(8,128)(2,1)}, bf16[4,128,256]{2,1,0:T(8,128)(2,1)S(1)}, u32[]{:S(2)}) copy-start(bf16[4,128,256]{2,1,0:T(8,128)(2,1)S(1)} %get-tuple-element.19.resid) | copy-start | bytes 786436
  44.0 18.5 %copy-start.5 = (bf16[1024,3,256]{2,0,1:T(8,128)(2,1)S(1)}, bf16[1024,3,256]{2,0,1:T(8,128)(2,1)}, u32[]{:S(2)}) copy-start(bf16[1024,3,256]{2,0,1:T(8,128)(2,1)} %param.9) | copy-start | bytes 4718596
  60.6 15.1 %collective-permute-start.4 = (bf16[2048,256]{1,0:T(8,128)(2,1)S(1)}, bf16[2048,256]{1,0:T(8,128)(2,1)}, u32[]{:S(2)}, u32[]{:S(2)}) collective-permute-start(bf16[2048,256]{1,0:T(8,128)(2,1)S(1)} %constant_dynamic-update-slice_fusion.weights), channel_id=1, source_target_pairs={{0,1},{1,0},{2,3},{3,2},{4,5},{5,4},{6,7},{7,6},{8,9},{9,8},{10,11... | collective-permute-start | bytes 3145736 | tf_op jit(solution)/shard_map/ppermute | solution.py:293
  65.8 0.7 copy-start.2
  66.5 52.1 %copy-start.3 = (f32[1024]{0:T(1024)S(1)}, f32[1024]{0:T(1024)}, u32[]{:S(2)}) copy-start(f32[1024]{0:T(1024)} %param.11) | copy-start | bytes 12292
  66.5 9.2 %all-to-all-start = ((bf16[4,128,256]{2,1,0:T(8,128)(2,1)}), bf16[4,128,256]{2,1,0:T(8,128)(2,1)S(1)}, u32[]{:S(2)}, u32[]{:S(2)}) async-start(bf16[4,128,256]{2,1,0:T(8,128)(2,1)} %copy-done.2), calls=%async_computation | async-start | bytes 524288 | tf_op jit(solution)/shard_map/all_to_all | solution.py:295
  70.5 48.1 %collective-permute-start.5 = (bf16[4096,256]{1,0:T(8,128)(2,1)S(1)}, bf16[4096,256]{1,0:T(8,128)(2,1)}, u32[]{:S(2)}, u32[]{:S(2)}) collective-permute-start(bf16[4096,256]{1,0:T(8,128)(2,1)S(1)} %pad_maximum_fusion.w0), channel_id=1, source_target_pairs={{0,1},{1,0},{2,3},{3,2},{4,5},{5,4},{6,7},{7,6},{8,9},{9,8},{10,11... | collective-permute-start | bytes 6291464 | tf_op jit(solution)/shard_map/ppermute | solution.py:287
  75.7 1.0 copy-start.1
  79.0 39.6 %collective-permute-start.7 = (bf16[4096,256]{1,0:T(8,128)(2,1)}, bf16[4096,256]{1,0:T(8,128)(2,1)S(1)}, u32[]{:S(2)}, u32[]{:S(2)}) collective-permute-start(bf16[4096,256]{1,0:T(8,128)(2,1)} %collective-permute-done.6.w2), channel_id=1, source_target_pairs={{0,1},{1,0},{2,3},{3,2},{4,5},{5,4},{6,7},{7,6},{8,9},{9,8},{10,11... | collective-permute-start | bytes 6291464 | tf_op jit(solution)/shard_map/ppermute | solution.py:298

commit v3 on v2

v3 whole, which is shorter than its diff:
```python
import functools

import jax
import jax.numpy as jnp
from jax import lax
from jax.experimental import pallas as pl
from jax.experimental.pallas import tpu as pltpu
from jax.sharding import Mesh, PartitionSpec as P

COLS = 512
HEAD_DIM = 64
SEQ = ("yh", "z", "x")
HEAD = ("yl", "c")
GROUP = 256
PARTS = 4
HEADS_HERE = GROUP // HEAD_DIM
MIB = 1 << 20
VMEM = pl.BlockSpec(memory_space=pltpu.VMEM)
SMEM = pl.BlockSpec(memory_space=pltpu.SMEM)
ANY = pl.BlockSpec(memory_space=pl.ANY)


def dot(a, b):
    return jnp.dot(a, b, preferred_element_type=jnp.float32)


def dot_t(a, b):
    return lax.dot_general(a, b, (((1,), (1,)), ((), ())), preferred_element_type=jnp.float32)


def normed_pieces(pieces, gains):
    flat = [p.astype(jnp.float32) for p in pieces]
    width = sum(p.shape[1] for p in pieces)
    mean = sum(jnp.sum(p, axis=-1, keepdims=True) for p in flat) / width
    flat = [p - mean for p in flat]
    var = sum(jnp.sum(p * p, axis=-1, keepdims=True) for p in flat) / width
    scale = lax.rsqrt(var + 1e-05)
    return [(p * scale * g).astype(jnp.bfloat16) for p, g in zip(flat, gains)]


def project(normed, order, weight, which):
    return sum(dot(p, weight[which, n]) for p, n in zip(normed, order)).astype(jnp.bfloat16)


def head_mask(rows, head):
    lane = lax.broadcasted_iota(jnp.int32, (rows, GROUP), 1)
    return (lane >= head * HEAD_DIM) & (lane < (head + 1) * HEAD_DIM)


def one_head(query, head):
    return jnp.where(head_mask(query.shape[0], head), query, jnp.bfloat16(0))


def triangle(block):
    row = lax.broadcasted_iota(jnp.int32, (block, block), 0)
    col = lax.broadcasted_iota(jnp.int32, (block, block), 1)
    return row, col


def attend_blocks(query, keys, vals, adjust):
    rows = query.shape[0]
    peak_all = norm_all = acc_all = jnp.zeros((rows, GROUP), jnp.float32)
    for head in range(HEADS_HERE):
        mask = head_mask(rows, head)
        qh = one_head(query, head)
        scores = [f(dot_t(qh, k)) for k, f in zip(keys, adjust)]
        peak = functools.reduce(jnp.maximum, scores)
        peak = jnp.max(peak, axis=-1, keepdims=True)
        expo = [jnp.exp(s - peak) for s in scores]
        norm = jnp.sum(sum(expo[1:], expo[0]), axis=-1, keepdims=True)
        acc = sum(dot(w.astype(jnp.bfloat16), v) for w, v in zip(expo, vals))
        peak_all = jnp.where(mask, peak, peak_all)
        norm_all = jnp.where(mask, norm, norm_all)
        acc_all = jnp.where(mask, acc, acc_all)
    return peak_all, norm_all, acc_all


BLOCK = 256
SCALE = HEAD_DIM ** (-0.5)


def row_own_kernel(place, near, far, gain, weight, query, peak, norm, acc, kv):
    order = [place[0], place[0] + 1, place[1], place[1] + 1]
    row, col = triangle(BLOCK)
    for i in range(COLS // BLOCK):
        rows = slice(i * BLOCK, (i + 1) * BLOCK)
        pieces = [near[0, rows], near[1, rows], far[0, rows], far[1, rows]]
        normed = normed_pieces(pieces, [gain[n] for n in order])
        query[rows] = project(normed, order, weight, 0)
        kv[0, rows] = project(normed, order, weight, 1)
        kv[1, rows] = project(normed, order, weight, 2)
    for i in range(COLS // BLOCK):
        rows = slice(i * BLOCK, (i + 1) * BLOCK)
        parts = [slice(j * BLOCK, (j + 1) * BLOCK) for j in range(i + 1)]
        adjust = [lambda s: s] * i + [lambda s: jnp.where(col <= row, s, -1e30)]
        peak[rows], norm[rows], acc[rows] = attend_blocks(
            query[rows], [kv[0, p] for p in parts], [kv[1, p] for p in parts], adjust
        )


def row_own(place, near, far, gain, weight):
    return pl.pallas_call(
        row_own_kernel,
        out_shape=(
            jax.ShapeDtypeStruct((COLS, GROUP), jnp.bfloat16),
            *[jax.ShapeDtypeStruct((COLS, GROUP), jnp.float32)] * 3,
        ),
        in_specs=[SMEM, VMEM, VMEM, VMEM, VMEM],
        out_specs=(VMEM,) * 4,
        scratch_shapes=[
            pltpu.VMEM((2, COLS, GROUP), jnp.bfloat16),
        ],
        compiler_params=pltpu.CompilerParams(vmem_limit_bytes=16 * MIB),
        cost_estimate=pl.CostEstimate(flops=1, bytes_accessed=1, transcendentals=0),
        name="row_own",
    )(place, near, far, gain, weight)


def row_halo_kernel(place, near, far, gain, weight, query, peak, norm, acc, source, out, kv):
    order = [place[0], place[0] + 1, place[1], place[1] + 1]
    row, col = triangle(BLOCK)
    blocked = jnp.where(place[2] > 0, 0.0, -1e30).astype(jnp.float32)
    blocks = COLS // BLOCK
    for i in range(blocks):
        rows = slice(i * BLOCK, (i + 1) * BLOCK)
        pieces = [near[0, rows], near[1, rows], far[0, rows], far[1, rows]]
        normed = normed_pieces(pieces, [gain[n] for n in order])
        kv[0, rows] = project(normed, order, weight, 1)
        kv[1, rows] = project(normed, order, weight, 2)
    for i in range(blocks):
        rows = slice(i * BLOCK, (i + 1) * BLOCK)
        parts = [slice(j * BLOCK, (j + 1) * BLOCK) for j in range(i, blocks)]
        adjust = [lambda s: jnp.where(col > row, s, -1e30) + blocked] + [lambda s: s + blocked] * (blocks - 1 - i)
        peak2, norm2, acc2 = attend_blocks(
            query[rows], [kv[0, p] for p in parts], [kv[1, p] for p in parts], adjust
        )
        top = jnp.maximum(peak[rows], peak2)
        one, two = jnp.exp(peak[rows] - top), jnp.exp(peak2 - top)
        att = (acc[rows] * one + acc2 * two) / (norm[rows] * one + norm2 * two)
        out[rows, :GROUP] = att.astype(jnp.bfloat16)
        out[rows, GROUP:] = source[rows]


def row_halo(place, near, far, gain, weight, state, source):
    return pl.pallas_call(
        row_halo_kernel,
        out_shape=jax.ShapeDtypeStruct((COLS, 2 * GROUP), jnp.bfloat16),
        in_specs=[SMEM] + [VMEM] * 9,
        out_specs=VMEM,
        scratch_shapes=[
            pltpu.VMEM((2, COLS, GROUP), jnp.bfloat16),
        ],
        compiler_params=pltpu.CompilerParams(vmem_limit_bytes=16 * MIB),
        cost_estimate=pl.CostEstimate(flops=1, bytes_accessed=1, transcendentals=0),
        name="row_halo",
    )(place, near, far, gain, weight, *state, source)


QKV_AT, OUT_AT, WEIGHT_ROWS = 1024, 4096, 5120


def column_blocks(w):
    return w.reshape(GROUP, PARTS, GROUP).transpose(1, 0, 2).reshape(PARTS * GROUP, GROUP)


def col_layer_kernel(place, moved, gain, w0, w1, w2, w3, out, held, sem):
    arrays = (w0, w1, w2, w3)
    groups = [place[0] + place[3], place[0] + 1 - place[3], place[1] + place[3], place[1] + 1 - place[3]]
    first = [pltpu.make_async_copy(w.at[:QKV_AT], held.at[i, :QKV_AT], sem.at[0, i]) for i, w in enumerate(arrays)]
    rest = [pltpu.make_async_copy(w.at[QKV_AT:], held.at[i, QKV_AT:], sem.at[1, i]) for i, w in enumerate(arrays)]
    for copy in first + rest:
        copy.start()

    def add_projected(pieces, atts, at):
        result = []
        for n in range(PARTS):
            rows = slice(at + n * GROUP, at + (n + 1) * GROUP)
            total = sum(dot(a, held[i, rows, :]) for i, a in enumerate(atts))
            result.append((pieces[n].astype(jnp.float32) + total).astype(jnp.bfloat16))
        return result

    atts = [moved[g, :, :GROUP] for g in groups]
    for copy in first:
        copy.wait()
    pieces = add_projected([moved[n, :, GROUP:] for n in range(PARTS)], atts, 0)
    normed = normed_pieces(pieces, [gain[n] for n in range(PARTS)])
    normed = jnp.concatenate(normed, axis=1)
    row, col = triangle(normed.shape[0])
    atts = []
    for i, copy in enumerate(rest):
        copy.wait()
        q, k, v = [
            dot(normed, held[i, QKV_AT + j * 1024 : QKV_AT + (j + 1) * 1024, :]).astype(jnp.bfloat16)
            for j in range(3)
        ]
        _, norm, acc = attend_blocks(
            q * jnp.bfloat16(SCALE), [k], [v], [lambda s: jnp.where(col <= row, s, -1e30)]
        )
        atts.append((acc / norm).astype(jnp.bfloat16))
    for n, piece in enumerate(add_projected(pieces, atts, OUT_AT)):
        out[n] = piece


def col_layer(place, moved, gain, weights):
    return pl.pallas_call(
        col_layer_kernel,
        out_shape=jax.ShapeDtypeStruct((PARTS, 128, GROUP), jnp.bfloat16),
        in_specs=[SMEM, VMEM, VMEM] + [ANY] * 4,
        out_specs=VMEM,
        scratch_shapes=[pltpu.VMEM((PARTS, WEIGHT_ROWS, GROUP), jnp.bfloat16), pltpu.SemaphoreType.DMA((2, PARTS))],
        compiler_params=pltpu.CompilerParams(vmem_limit_bytes=20 * MIB),
        cost_estimate=pl.CostEstimate(flops=1, bytes_accessed=1, transcendentals=0),
        name="col_layer",
    )(place, moved, gain, *weights)


SWAP = [(0, 1), (1, 0)]


def after(value, *others):
    return lax.optimization_barrier((value, *others))[0]


def cross_route(outer):
    route = []
    for yh in range(4):
        for core in range(2):
            a = yh * 4 + 2 + core
            b = ((yh + 1) % 4 if core in outer else yh) * 4 + core
            route += [(a, b), (b, a)]
    return route


def on_device(inputs, row_gain, row_qkv, row_out, col_gain, col_qkv, col_out):
    yl, core = lax.axis_index("yl"), lax.axis_index("c")
    place = jnp.stack([yl * 2, (1 - yl) * 2, lax.axis_index(SEQ), core]).astype(jnp.int32)
    row_gain = row_gain.reshape(PARTS, 1, GROUP)
    row_qkv = row_qkv.transpose(1, 0, 2).reshape(3, PARTS, GROUP, GROUP)
    row_qkv = row_qkv * jnp.array([SCALE, 1, 1], jnp.bfloat16)[:, None, None, None]

    other = lax.ppermute(inputs, "yl", SWAP)
    before = lax.ppermute(inputs, SEQ, [(i, i + 1) for i in range(127)])
    near = lax.all_gather(inputs, "c", axis=0)
    far = lax.all_gather(after(other, near), "c", axis=0)
    before_other = lax.ppermute(after(before, far), "yl", SWAP)

    mine = jnp.concatenate(
        [column_blocks(row_out), col_qkv.transpose(1, 0, 2).reshape(3 * 1024, GROUP), column_blocks(col_out)]
    )
    mine, row_qkv = lax.optimization_barrier((mine, row_qkv, before, other, near))[:2]
    theirs = lax.ppermute(mine, ("yh", "yl", "c"), cross_route((1,)))

    state = row_own(place, near, far, row_gain, row_qkv)
    mine_swapped = lax.ppermute(after(mine, state[0]), "c", SWAP)
    before_near = lax.all_gather(after(before, state[0]), "c", axis=0)
    before_far = lax.all_gather(after(before_other, before_near), "c", axis=0)
    sent = row_halo(place, before_near, before_far, row_gain, row_qkv, state, inputs)
    theirs_swapped = lax.ppermute(after(theirs, sent), "c", SWAP)

    moved = lax.all_to_all(sent.reshape(COLS, 4, 128), HEAD + SEQ, 0, 0, tiled=True)
    mixed = col_layer(
        place,
        moved.reshape(PARTS, 128, 2 * GROUP),
        col_gain.reshape(PARTS, 1, GROUP),
        [mine, mine_swapped, theirs, theirs_swapped],
    )
    mixed = lax.all_to_all(mixed.reshape(COLS, 2, 128), HEAD + SEQ, 0, 0, tiled=True)
    return mixed.reshape(COLS, GROUP)


def solution(mesh):
    fine = Mesh(mesh.devices.reshape(4, 8, 4, 2, 2), SEQ + HEAD)
    return jax.shard_map(
        on_device,
        mesh=fine,
        in_specs=(
            P(SEQ, HEAD),
            P(),
            P(None, None, HEAD),
            P(HEAD, None),
            P(),
            P(None, None, HEAD),
            P(HEAD, None),
        ),
        out_specs=P(SEQ, HEAD),
        check_vma=False,
    )
```

time: 152 us -> 148 us (0.974)
  blocking collectives: 82.1 us -> 98.5 us
  waiting for transfers between devices: 9.61 us -> 0.02 us
  starting transfers between devices: 36.8 us -> 28.5 us
  local copies, waits for them, and re-layouts: 7.08 us -> 5.56 us
    all_to_all x2, blocking collectives: 63.4 us -> 73.9 us  [the longest x1 47 us: on_device(): lax.all_to_all(sent.reshape(COLS, 4, 128), HEAD + SEQ, 0, 0, tiled=True)]
    ppermute x5 -> x3, waiting for transfers between devices: 6.39 us -> 0.01 us  [the longest x1 0.01 us: on_device(): theirs = lax.ppermute(mine, ('yh', 'yl', 'c'), cross_route((1,)))]
    all_gather x1, blocking collectives: 7.76 us -> 12.3 us  [on_device(): before_far = lax.all_gather(after(before_other, before_near), 'c', axis=0)]
    ppermute x5 -> x3, starting transfers between devices: 23.7 us -> 19.3 us  [the longest x1 14.9 us: on_device(): theirs = lax.ppermute(mine, ('yh', 'yl', 'c'), cross_route((1,)))]
    all_to_all x1 -> x0, starting transfers between devices: 4 us -> none  [on_device(): att = lax.all_to_all(att, HEAD, 0, 0, tiled=True)]
    all_to_all x1 -> x0, waiting for transfers between devices: 3.21 us -> none  [on_device(): att = lax.all_to_all(att, HEAD, 0, 0, tiled=True)]
    all_gather x1, blocking collectives: 2.31 us -> 5.12 us  [on_device(): before_near = lax.all_gather(after(before, state[0]), 'c', axis=0)]
    unnamed x22 -> x13, local copies, waits for them, and re-layouts: 3.94 us -> 1.13 us
  transfers between devices with their start and end apart: 9 -> 6, of which waited for: 2 -> 0; matrix products, arithmetic and copies ran while one was open for 3% -> 4% of each run, Pallas kernels for 6% -> 4%
where the time goes in v3:
time: 148 us
  blocking collectives  98.5 us (67%)
  starting transfers between devices  28.5 us (19%)
  Pallas kernels  13.2 us (9%)
  local copies, waits for them, and re-layouts  5.56 us (4%)
  other arithmetic  1.93 us (1%)
    all_to_all x1, blocking collectives, on_device(): lax.all_to_all(sent.reshape(COLS, 4, 128), HEAD + SEQ, 0, 0, tiled=True)  47 us
    all_to_all x1, blocking collectives, on_device(): lax.all_to_all(mixed.reshape(COLS, 2, 128), HEAD + SEQ, 0, 0, tiled=True)  27 us
    ppermute x1, starting transfers between devices, on_device(): theirs = lax.ppermute(mine, ('yh', 'yl', 'c'), cross_route((1,)))  14.9 us
    all_gather x1, blocking collectives, on_device(): before_far = lax.all_gather(after(before_other, before_near), 'c', axis=0)  12.3 us
    pallas_call x1, Pallas kernels, col_layer(): pl.pallas_call(col_layer_kernel, out_shape=jax.ShapeDtypeStruct((PARTS, 1...  6.89 us
    all_gather x1, blocking collectives, on_device(): before_near = lax.all_gather(after(before, state[0]), 'c', axis=0)  5.12 us
    all_gather x1, blocking collectives, on_device(): near = lax.all_gather(inputs, 'c', axis=0)  4.96 us
    ppermute x1, starting transfers between devices, on_device(): before = lax.ppermute(inputs, SEQ, [(i, i + 1) for i in range(127)])  4.08 us
  transfers between devices with their start and end apart: 6, of which 0 were waited for; matrix products, arithmetic and copies ran while one was open for 4% of the time, Pallas kernels for 4%

profile of v3, /device:TPU:1, one launch (start us, length us, event | category | flops | bytes accessed | tf_op | source)
XLA Modules:
  0.0 147.9 jit_solution(13965487209545266758)
XLA Ops:
  0.0 4.1 %collective-permute-start = (bf16[512,256]{1,0:T(8,128)(2,1)}, bf16[512,256]{1,0:T(8,128)(2,1)S(1)}, u32[]{:S(2)}, u32[]{:S(2)}) collective-permute-start(bf16[512,256]{1,0:T(8,128)(2,1)} %source.1), channel_id=1, source_target_pairs={{0,4},{4,8},{8,12},{12,16},{16,20},{20,24},{24,28},{28,32},{32,36}... | collective-permute-start | bytes 786440 | tf_op jit(solution)/shard_map/ppermute | solution.py:242
  4.1 3.2 %collective-permute-start.1 = (bf16[512,256]{1,0:T(8,128)(2,1)}, bf16[512,256]{1,0:T(8,128)(2,1)S(1)}, u32[]{:S(2)}, u32[]{:S(2)}) collective-permute-start(bf16[512,256]{1,0:T(8,128)(2,1)} %source.1), channel_id=1, source_target_pairs={{0,2},{2,0},{1,3},{3,1},{4,6},{6,4},{5,7},{7,5},{8,10},{10,8},{9,1... | collective-permute-start | bytes 786440 | tf_op jit(solution)/shard_map/ppermute | solution.py:241
  7.3 5.0 %all-gather = bf16[1024,256]{1,0:T(8,128)(2,1)S(1)} all-gather(bf16[512,256]{1,0:T(8,128)(2,1)} %source.1), channel_id=2, replica_groups=mesh['yh'=4,'z'=8,'x'=4,'yl'=2,'c'=2] {'c'}, dimensions={0}, use_global_device_ids=true | all-gather | bytes 786432 | tf_op jit(solution)/shard_map/all_gather | solution.py:243
  12.3 1.1 copy.18
  13.3 1.1 copy.17
  14.5 1.7 %pad_maximum_fusion.w0 = bf16[5120,256]{1,0:T(8,128)(2,1)} fusion(bf16[1024,256]{1,0:T(8,128)(2,1)S(1)} %bitcast.42, bf16[3072,256]{1,0:T(8,128)(2,1)S(1)} %bitcast.43, bf16[1024,256]{1,0:T(8,128)(2,1)S(1)} %bitcast.41), kind=kLoop, calls=%fused_computation | loop fusion | flops 7864320 | bytes 5242880 | tf_op jit(solution)/shard_map/concatenate | solution.py:247
  16.1 0.4 copy-done.4
  16.5 0.2 broadcast_multiply_fusion.weight
  16.7 14.9 %collective-permute-start.4 = (bf16[5120,256]{1,0:T(8,128)(2,1)}, bf16[5120,256]{1,0:T(8,128)(2,1)}, u32[]{:S(2)}, u32[]{:S(2)}) collective-permute-start(bf16[5120,256]{1,0:T(8,128)(2,1)} %pad_maximum_fusion.w0), channel_id=1, source_target_pairs={{2,0},{0,2},{3,129},{129,3},{130,128},{128,130},{131,257},{257,131... | collective-permute-start | bytes 7864328 | tf_op jit(solution)/shard_map/ppermute | solution.py:251
  31.7 2.2 %all-gather.1 = bf16[1024,256]{1,0:T(8,128)(2,1)S(1)} all-gather(bf16[512,256]{1,0:T(8,128)(2,1)S(1)} %collective-permute-done.1), channel_id=3, replica_groups=mesh['yh'=4,'z'=8,'x'=4,'yl'=2,'c'=2] {'c'}, dimensions={0}, use_global_device_ids=true | all-gather | bytes 786432 | tf_op jit(solution)/shard_map/all_gather | solution.py:244
  33.8 1.9 %collective-permute-start.2 = (bf16[512,256]{1,0:T(8,128)(2,1)S(1)}, bf16[512,256]{1,0:T(8,128)(2,1)S(1)}, u32[]{:S(2)}, u32[]{:S(2)}) collective-permute-start(bf16[512,256]{1,0:T(8,128)(2,1)S(1)} %collective-permute-done), channel_id=1, source_target_pairs={{0,2},{2,0},{1,3},{3,1},{4,6},{6,4},{5,7},{7,5},{8,10},{10,8},{9,1... | collective-permute-start | bytes 786440 | tf_op jit(solution)/shard_map/ppermute | solution.py:245
  35.8 0.1 pad_add_fusion.place
  35.8 3.1 %row_own.1 = (bf16[512,256]{1,0:T(8,128)(2,1)S(1)}, f32[512,256]{1,0:T(8,128)S(1)}, f32[512,256]{1,0:T(8,128)S(1)}, f32[512,256]{1,0:T(8,128)S(1)}) custom-call(s32[4]{0:T(128)S(1)} %pad_add_fusion.place, bf16[2,512,256]{2,1,0:T(8,128)(2,1)S(1)} %bitcast.36, bf16[2,512,256]{2,1,0:T(8,128)(2,1)S(1)} %bitcast.37, f32[4,1,256]{2,1,0:T(1,128)S(1)} %bitcast.38, ...), custom_call_target="tpu_custom_call" | custom-call | flops 1 | bytes 1 | tf_op jit(solution)/shard_map/row_own/pallas_call | solution.py:102
  38.9 2.0 %collective-permute-start.3 = (bf16[5120,256]{1,0:T(8,128)(2,1)}, bf16[5120,256]{1,0:T(8,128)(2,1)}, u32[]{:S(2)}, u32[]{:S(2)}) collective-permute-start(bf16[5120,256]{1,0:T(8,128)(2,1)} %pad_maximum_fusion.w0), channel_id=1, source_target_pairs={{0,1},{1,0},{2,3},{3,2},{4,5},{5,4},{6,7},{7,6},{8,9},{9,8},{10,11... | collective-permute-start | bytes 7864328 | tf_op jit(solution)/shard_map/ppermute | solution.py:254
  41.0 5.1 %all-gather.2 = bf16[1024,256]{1,0:T(8,128)(2,1)S(1)} all-gather(bf16[512,256]{1,0:T(8,128)(2,1)S(1)} %collective-permute-done), channel_id=4, replica_groups=mesh['yh'=4,'z'=8,'x'=4,'yl'=2,'c'=2] {'c'}, dimensions={0}, use_global_device_ids=true | all-gather | bytes 786432 | tf_op jit(solution)/shard_map/all_gather | solution.py:255
  46.1 12.3 %all-gather.3 = bf16[1024,256]{1,0:T(8,128)(2,1)S(1)} all-gather(bf16[512,256]{1,0:T(8,128)(2,1)S(1)} %collective-permute-done.2), channel_id=5, replica_groups=mesh['yh'=4,'z'=8,'x'=4,'yl'=2,'c'=2] {'c'}, dimensions={0}, use_global_device_ids=true | all-gather | bytes 786432 | tf_op jit(solution)/shard_map/all_gather | solution.py:256
  58.4 3.3 %row_halo.1 = bf16[512,512]{1,0:T(8,128)(2,1)S(1)} custom-call(s32[4]{0:T(128)S(1)} %pad_add_fusion.place, bf16[2,512,256]{2,1,0:T(8,128)(2,1)S(1)} %bitcast.34, bf16[2,512,256]{2,1,0:T(8,128)(2,1)S(1)} %bitcast.35, f32[4,1,256]{2,1,0:T(1,128)S(1)} %bitcast.39, bf16[3,4,256,256]{3,2,1,0:T(8,128)(2,1)S(1)} %broadcast_multiply_fusion.weight, ...), custom_call_target="tpu_custom_call" | custom-call | flops 1 | bytes 1 | tf_op jit(solution)/shard_map/row_halo/pallas_call | solution.py:145
  61.7 2.3 %collective-permute-start.5 = (bf16[5120,256]{1,0:T(8,128)(2,1)}, bf16[5120,256]{1,0:T(8,128)(2,1)S(1)}, u32[]{:S(2)}, u32[]{:S(2)}) collective-permute-start(bf16[5120,256]{1,0:T(8,128)(2,1)} %collective-permute-done.4.w2), channel_id=1, source_target_pairs={{0,1},{1,0},{2,3},{3,2},{4,5},{5,4},{6,7},{7,6},{8,9},{9,8},{10,11... | collective-permute-start | bytes 7864328 | tf_op jit(solution)/shard_map/ppermute | solution.py:258
  64.0 1.0 reshape.44
  65.0 47.0 %all_to_all.10 = bf16[512,4,128]{2,1,0:T(4,128)(2,1)} all-to-all(bf16[512,4,128]{2,1,0:T(4,128)(2,1)} %reshape.44), channel_id=1, replica_groups=mesh['yh'=4,'z'=8,'x'=4,'yl'=2,'c'=2] {'yl','c','yh','z','x'}, dimensions={0} | all-to-all | bytes 1048576 | tf_op jit(solution)/shard_map/all_to_all | solution.py:260
  111.9 1.2 reshape.45.moved
  113.2 6.9 %col_layer.1 = bf16[4,128,256]{2,1,0:T(8,128)(2,1)S(1)} custom-call(s32[4]{0:T(128)S(1)} %pad_add_fusion.place, bf16[4,128,512]{2,1,0:T(8,128)(2,1)S(1)} %reshape.45.moved, f32[4,1,256]{2,1,0:T(1,128)S(1)} %bitcast.40, bf16[5120,256]{1,0:T(8,128)(2,1)} %pad_maximum_fusion.w0, bf16[5120,256]{1,0:T(8,128)(2,1)} %collective-permute-done.3.w1, ...), custom_call_target="tpu_custom_call" | custom-call | flops 1 | bytes 1 | tf_op jit(solution)/shard_map/col_layer/pallas_call | solution.py:205
  120.2 27.0 %all_to_all.11 = bf16[512,2,128]{2,1,0:T(2,128)(2,1)S(1)} all-to-all(bf16[512,2,128]{2,1,0:T(2,128)(2,1)S(1)} %reshape.47), channel_id=1, replica_groups=mesh['yh'=4,'z'=8,'x'=4,'yl'=2,'c'=2] {'yl','c','yh','z','x'}, dimensions={0} | all-to-all | bytes 524288 | tf_op jit(solution)/shard_map/all_to_all | solution.py:267
  147.1 0.7 copy.19
  (18 shorter events, 0.1 us)
Async XLA Ops:
  0.0 14.4 %copy-start.3 = (bf16[1024,3,256]{2,0,1:T(8,128)(2,1)S(1)}, bf16[1024,3,256]{2,0,1:T(8,128)(2,1)}, u32[]{:S(2)}) copy-start(bf16[1024,3,256]{2,0,1:T(8,128)(2,1)} %param.13) | copy-start | bytes 4718596
  0.0 16.7 %collective-permute-start = (bf16[512,256]{1,0:T(8,128)(2,1)}, bf16[512,256]{1,0:T(8,128)(2,1)S(1)}, u32[]{:S(2)}, u32[]{:S(2)}) collective-permute-start(bf16[512,256]{1,0:T(8,128)(2,1)} %source.1), channel_id=1, source_target_pairs={{0,4},{4,8},{8,12},{12,16},{16,20},{20,24},{24,28},{28,32},{32,36}... | collective-permute-start | bytes 786440 | tf_op jit(solution)/shard_map/ppermute | solution.py:242
  4.1 12.6 %collective-permute-start.1 = (bf16[512,256]{1,0:T(8,128)(2,1)}, bf16[512,256]{1,0:T(8,128)(2,1)S(1)}, u32[]{:S(2)}, u32[]{:S(2)}) collective-permute-start(bf16[512,256]{1,0:T(8,128)(2,1)} %source.1), channel_id=1, source_target_pairs={{0,2},{2,0},{1,3},{3,1},{4,6},{6,4},{5,7},{7,5},{8,10},{10,8},{9,1... | collective-permute-start | bytes 786440 | tf_op jit(solution)/shard_map/ppermute | solution.py:241
  14.4 2.1 %copy-start.4 = (bf16[1024,3,256]{2,0,1:T(8,128)(2,1)S(1)}, bf16[1024,3,256]{2,0,1:T(8,128)(2,1)}, u32[]{:S(2)}) copy-start(bf16[1024,3,256]{2,0,1:T(8,128)(2,1)} %param.10) | copy-start | bytes 4718596
  14.4 2.1 %copy-start.5 = (bf16[3]{0:T(256)(128)(2,1)S(1)}, bf16[3]{0:T(256)(128)(2,1)}, u32[]{:S(2)}) copy-start(bf16[3]{0:T(256)(128)(2,1)} %constant.30.clone) | copy-start | bytes 22
  16.1 19.7 %copy-start.1 = (f32[1024]{0:T(1024)S(1)}, f32[1024]{0:T(1024)}, u32[]{:S(2)}) copy-start(f32[1024]{0:T(1024)} %param.9) | copy-start | bytes 12292
  16.7 41.7 %copy-start = (bf16[512,256]{1,0:T(8,128)(2,1)S(1)}, bf16[512,256]{1,0:T(8,128)(2,1)}, u32[]{:S(2)}) copy-start(bf16[512,256]{1,0:T(8,128)(2,1)} %source.1) | copy-start | bytes 786436
  16.7 45.0 %collective-permute-start.4 = (bf16[5120,256]{1,0:T(8,128)(2,1)}, bf16[5120,256]{1,0:T(8,128)(2,1)}, u32[]{:S(2)}, u32[]{:S(2)}) collective-permute-start(bf16[5120,256]{1,0:T(8,128)(2,1)} %pad_maximum_fusion.w0), channel_id=1, source_target_pairs={{2,0},{0,2},{3,129},{129,3},{130,128},{128,130},{131,257},{257,131... | collective-permute-start | bytes 7864328 | tf_op jit(solution)/shard_map/ppermute | solution.py:251
  33.8 12.3 %collective-permute-start.2 = (bf16[512,256]{1,0:T(8,128)(2,1)S(1)}, bf16[512,256]{1,0:T(8,128)(2,1)S(1)}, u32[]{:S(2)}, u32[]{:S(2)}) collective-permute-start(bf16[512,256]{1,0:T(8,128)(2,1)S(1)} %collective-permute-done), channel_id=1, source_target_pairs={{0,2},{2,0},{1,3},{3,1},{4,6},{6,4},{5,7},{7,5},{8,10},{10,8},{9,1... | collective-permute-start | bytes 786440 | tf_op jit(solution)/shard_map/ppermute | solution.py:245
  38.9 74.3 %collective-permute-start.3 = (bf16[5120,256]{1,0:T(8,128)(2,1)}, bf16[5120,256]{1,0:T(8,128)(2,1)}, u32[]{:S(2)}, u32[]{:S(2)}) collective-permute-start(bf16[5120,256]{1,0:T(8,128)(2,1)} %pad_maximum_fusion.w0), channel_id=1, source_target_pairs={{0,1},{1,0},{2,3},{3,2},{4,5},{5,4},{6,7},{7,6},{8,9},{9,8},{10,11... | collective-permute-start | bytes 7864328 | tf_op jit(solution)/shard_map/ppermute | solution.py:254
  61.7 51.5 %copy-start.2 = (f32[1024]{0:T(1024)S(1)}, f32[1024]{0:T(1024)}, u32[]{:S(2)}) copy-start(f32[1024]{0:T(1024)} %param.12) | copy-start | bytes 12292
  61.7 51.5 %collective-permute-start.5 = (bf16[5120,256]{1,0:T(8,128)(2,1)}, bf16[5120,256]{1,0:T(8,128)(2,1)S(1)}, u32[]{:S(2)}, u32[]{:S(2)}) collective-permute-start(bf16[5120,256]{1,0:T(8,128)(2,1)} %collective-permute-done.4.w2), channel_id=1, source_target_pairs={{0,1},{1,0},{2,3},{3,2},{4,5},{5,4},{6,7},{7,6},{8,9},{9,8},{10,11... | collective-permute-start | bytes 7864328 | tf_op jit(solution)/shard_map/ppermute | solution.py:258

commit v4 on v3

--- a/solution.py
+++ b/solution.py
@@ -241,23 +241,25 @@
     other = lax.ppermute(inputs, "yl", SWAP)
     before = lax.ppermute(inputs, SEQ, [(i, i + 1) for i in range(127)])
     near = lax.all_gather(inputs, "c", axis=0)
-    far = lax.all_gather(after(other, near), "c", axis=0)
-    before_other = lax.ppermute(after(before, far), "yl", SWAP)
+    other, before = lax.optimization_barrier((other, before, near))[:2]
+    before_other = lax.ppermute(before, "yl", SWAP)
+    far = lax.all_gather(other, "c", axis=0)
+    before_near = lax.all_gather(after(before, far), "c", axis=0)
+    before_far = lax.all_gather(after(before_other, before_near), "c", axis=0)
 
     mine = jnp.concatenate(
         [column_blocks(row_out), col_qkv.transpose(1, 0, 2).reshape(3 * 1024, GROUP), column_blocks(col_out)]
     )
-    mine, row_qkv = lax.optimization_barrier((mine, row_qkv, before, other, near))[:2]
+    mine, row_qkv = lax.optimization_barrier((mine, row_qkv, near))[:2]
+    mine = after(mine, before_far)
     theirs = lax.ppermute(mine, ("yh", "yl", "c"), cross_route((1,)))
-
-    state = row_own(place, near, far, row_gain, row_qkv)
-    mine_swapped = lax.ppermute(after(mine, state[0]), "c", SWAP)
-    before_near = lax.all_gather(after(before, state[0]), "c", axis=0)
-    before_far = lax.all_gather(after(before_other, before_near), "c", axis=0)
+    mine_swapped = lax.ppermute(mine, "c", SWAP)
+
+    state = row_own(place, near, after(far, before_far), row_gain, row_qkv)
     sent = row_halo(place, before_near, before_far, row_gain, row_qkv, state, inputs)
-    theirs_swapped = lax.ppermute(after(theirs, sent), "c", SWAP)
 
     moved = lax.all_to_all(sent.reshape(COLS, 4, 128), HEAD + SEQ, 0, 0, tiled=True)
+    theirs_swapped = lax.ppermute(after(theirs, moved), "c", SWAP)
     mixed = col_layer(
         place,
         moved.reshape(PARTS, 128, 2 * GROUP),

time: 148 us -> 134 us (0.905)
  blocking collectives: 98.5 us -> 39.4 us
  starting transfers between devices: 28.5 us -> 52.4 us
  waiting for transfers between devices: 0.02 us -> 19.8 us
    all_to_all x1 -> x0, blocking collectives: 47 us -> none  [on_device(): lax.all_to_all(sent.reshape(COLS, 4, 128), HEAD + SEQ, 0, 0, tiled=True)]
    all_to_all x0 -> x1, starting transfers between devices: none -> 15.2 us  [on_device(): lax.all_to_all(sent.reshape(COLS, 4, 128), HEAD + SEQ, 0, 0, tiled=True)]
    all_to_all x0 -> x1, waiting for transfers between devices: none -> 14.8 us  [on_device(): lax.all_to_all(sent.reshape(COLS, 4, 128), HEAD + SEQ, 0, 0, tiled=True)]
    all_gather x1, blocking collectives: 12.3 us -> 2.68 us  [on_device(): before_far = lax.all_gather(after(before_other, before_near), 'c', axis=0)]
    ppermute x3, starting transfers between devices: 6.24 us -> 15.4 us  [the longest x1 6.28 us: on_device(): mine_swapped = lax.ppermute(mine, 'c', SWAP)]
    ppermute x3, waiting for transfers between devices: 0.01 us -> 5.02 us  [the longest x1 3.42 us: on_device(): theirs_swapped = lax.ppermute(after(theirs, moved), 'c', SWAP)]
    all_gather x2, blocking collectives: 7.31 us -> 4.76 us  [the longest x1 2.59 us: on_device(): far = lax.all_gather(other, 'c', axis=0)]
  transfers between devices with their start and end apart: 6 -> 7, of which waited for: 0 -> 3; matrix products, arithmetic and copies ran while one was open for 4% -> 5% of each run, Pallas kernels for 4% -> 5%
where the time goes in v4:
time: 134 us
  starting transfers between devices  52.4 us (39%)
  blocking collectives  39.4 us (29%)
  waiting for transfers between devices  19.8 us (15%)
  Pallas kernels  13.2 us (10%)
  local copies, waits for them, and re-layouts  6.61 us (5%)
  other arithmetic  1.92 us (1%)
    all_to_all x1, blocking collectives, on_device(): lax.all_to_all(mixed.reshape(COLS, 2, 128), HEAD + SEQ, 0, 0, tiled=True)  27 us
    all_to_all x1, starting transfers between devices, on_device(): lax.all_to_all(sent.reshape(COLS, 4, 128), HEAD + SEQ, 0, 0, tiled=True)  15.2 us
    all_to_all x1, waiting for transfers between devices, on_device(): lax.all_to_all(sent.reshape(COLS, 4, 128), HEAD + SEQ, 0, 0, tiled=True)  14.8 us
    ppermute x1, starting transfers between devices, on_device(): theirs = lax.ppermute(mine, ('yh', 'yl', 'c'), cross_route((1,)))  14.5 us
    pallas_call x1, Pallas kernels, col_layer(): pl.pallas_call(col_layer_kernel, out_shape=jax.ShapeDtypeStruct((PARTS, 1...  6.89 us
    ppermute x1, starting transfers between devices, on_device(): mine_swapped = lax.ppermute(mine, 'c', SWAP)  6.28 us
    ppermute x1, starting transfers between devices, on_device(): theirs_swapped = lax.ppermute(after(theirs, moved), 'c', SWAP)  5.34 us
    all_gather x1, blocking collectives, on_device(): near = lax.all_gather(inputs, 'c', axis=0)  4.96 us
  transfers between devices with their start and end apart: 7, of which 3 were waited for; matrix products, arithmetic and copies ran while one was open for 5% of the time, Pallas kernels for 5%

profile of v4, /device:TPU:1, one launch (start us, length us, event | category | flops | bytes accessed | tf_op | source)
XLA Modules:
  0.0 133.6 jit_solution(16992925572956230344)
XLA Ops:
  0.0 4.1 %collective-permute-start.1 = (bf16[512,256]{1,0:T(8,128)(2,1)}, bf16[512,256]{1,0:T(8,128)(2,1)S(1)}, u32[]{:S(2)}, u32[]{:S(2)}) collective-permute-start(bf16[512,256]{1,0:T(8,128)(2,1)} %source.1), channel_id=1, source_target_pairs={{0,4},{4,8},{8,12},{12,16},{16,20},{20,24},{24,28},{28,32},{32,36}... | collective-permute-start | bytes 786440 | tf_op jit(solution)/shard_map/ppermute | solution.py:242
  4.1 3.2 %collective-permute-start = (bf16[512,256]{1,0:T(8,128)(2,1)}, bf16[512,256]{1,0:T(8,128)(2,1)S(1)}, u32[]{:S(2)}, u32[]{:S(2)}) collective-permute-start(bf16[512,256]{1,0:T(8,128)(2,1)} %source.1), channel_id=1, source_target_pairs={{0,2},{2,0},{1,3},{3,1},{4,6},{6,4},{5,7},{7,5},{8,10},{10,8},{9,1... | collective-permute-start | bytes 786440 | tf_op jit(solution)/shard_map/ppermute | solution.py:241
  7.3 5.0 %all-gather = bf16[1024,256]{1,0:T(8,128)(2,1)S(1)} all-gather(bf16[512,256]{1,0:T(8,128)(2,1)} %source.1), channel_id=2, replica_groups=mesh['yh'=4,'z'=8,'x'=4,'yl'=2,'c'=2] {'c'}, dimensions={0}, use_global_device_ids=true | all-gather | bytes 786432 | tf_op jit(solution)/shard_map/all_gather | solution.py:243
  12.3 1.1 copy.18
  13.3 1.1 copy.17
  14.5 1.7 %pad_maximum_fusion.w0 = bf16[5120,256]{1,0:T(8,128)(2,1)} fusion(bf16[1024,256]{1,0:T(8,128)(2,1)S(1)} %bitcast.42, bf16[3072,256]{1,0:T(8,128)(2,1)S(1)} %bitcast.43, bf16[1024,256]{1,0:T(8,128)(2,1)S(1)} %bitcast.41), kind=kLoop, calls=%fused_computation | loop fusion | flops 7864320 | bytes 5242880 | tf_op jit(solution)/shard_map/concatenate | solution.py:250
  16.7 3.8 %collective-permute-start.2 = (bf16[512,256]{1,0:T(8,128)(2,1)S(1)}, bf16[512,256]{1,0:T(8,128)(2,1)S(1)}, u32[]{:S(2)}, u32[]{:S(2)}) collective-permute-start(bf16[512,256]{1,0:T(8,128)(2,1)S(1)} %collective-permute-done.1), channel_id=1, source_target_pairs={{0,2},{2,0},{1,3},{3,1},{4,6},{6,4},{5,7},{7,5},{8,10},{10,8},{9,1... | collective-permute-start | bytes 786440 | tf_op jit(solution)/shard_map/ppermute | solution.py:245
  20.5 2.6 %all-gather.1 = bf16[1024,256]{1,0:T(8,128)(2,1)} all-gather(bf16[512,256]{1,0:T(8,128)(2,1)S(1)} %collective-permute-done), channel_id=3, replica_groups=mesh['yh'=4,'z'=8,'x'=4,'yl'=2,'c'=2] {'c'}, dimensions={0}, use_global_device_ids=true | all-gather | bytes 786432 | tf_op jit(solution)/shard_map/all_gather | solution.py:246
  23.1 2.2 %all-gather.2 = bf16[1024,256]{1,0:T(8,128)(2,1)S(1)} all-gather(bf16[512,256]{1,0:T(8,128)(2,1)S(1)} %collective-permute-done.1), channel_id=4, replica_groups=mesh['yh'=4,'z'=8,'x'=4,'yl'=2,'c'=2] {'c'}, dimensions={0}, use_global_device_ids=true | all-gather | bytes 786432 | tf_op jit(solution)/shard_map/all_gather | solution.py:247
  25.3 1.6 %collective-permute-done.2 = bf16[512,256]{1,0:T(8,128)(2,1)S(1)} collective-permute-done((bf16[512,256]{1,0:T(8,128)(2,1)S(1)}, bf16[512,256]{1,0:T(8,128)(2,1)S(1)}, u32[]{:S(2)}, u32[]{:S(2)}) %collective-permute-start.2) | collective-permute-done | bytes 262176 | tf_op jit(solution)/shard_map/ppermute | solution.py:245
  26.9 2.7 %all-gather.3 = bf16[1024,256]{1,0:T(8,128)(2,1)S(1)} all-gather(bf16[512,256]{1,0:T(8,128)(2,1)S(1)} %collective-permute-done.2), channel_id=5, replica_groups=mesh['yh'=4,'z'=8,'x'=4,'yl'=2,'c'=2] {'c'}, dimensions={0}, use_global_device_ids=true | all-gather | bytes 786432 | tf_op jit(solution)/shard_map/all_gather | solution.py:248
  29.6 14.5 %collective-permute-start.4 = (bf16[5120,256]{1,0:T(8,128)(2,1)}, bf16[5120,256]{1,0:T(8,128)(2,1)}, u32[]{:S(2)}, u32[]{:S(2)}) collective-permute-start(bf16[5120,256]{1,0:T(8,128)(2,1)} %pad_maximum_fusion.w0), channel_id=1, source_target_pairs={{2,0},{0,2},{3,129},{129,3},{130,128},{128,130},{131,257},{257,131... | collective-permute-start | bytes 7864328 | tf_op jit(solution)/shard_map/ppermute | solution.py:255
  44.2 1.0 copy-done
  45.2 3.1 %row_own.1 = (bf16[512,256]{1,0:T(8,128)(2,1)S(1)}, f32[512,256]{1,0:T(8,128)S(1)}, f32[512,256]{1,0:T(8,128)S(1)}, f32[512,256]{1,0:T(8,128)S(1)}) custom-call(s32[4]{0:T(128)S(1)} %pad_add_fusion.place, bf16[2,512,256]{2,1,0:T(8,128)(2,1)S(1)} %bitcast.36, bf16[2,512,256]{2,1,0:T(8,128)(2,1)S(1)} %bitcast.37, f32[4,1,256]{2,1,0:T(1,128)S(1)} %bitcast.38, ...), custom_call_target="tpu_custom_call" | custom-call | flops 1 | bytes 1 | tf_op jit(solution)/shard_map/row_own/pallas_call | solution.py:102
  48.3 3.2 %row_halo.1 = bf16[512,512]{1,0:T(8,128)(2,1)S(1)} custom-call(s32[4]{0:T(128)S(1)} %pad_add_fusion.place, bf16[2,512,256]{2,1,0:T(8,128)(2,1)S(1)} %bitcast.34, bf16[2,512,256]{2,1,0:T(8,128)(2,1)S(1)} %bitcast.35, f32[4,1,256]{2,1,0:T(1,128)S(1)} %bitcast.39, bf16[3,4,256,256]{3,2,1,0:T(8,128)(2,1)S(1)} %broadcast_multiply_fusion.weight, ...), custom_call_target="tpu_custom_call" | custom-call | flops 1 | bytes 1 | tf_op jit(solution)/shard_map/row_halo/pallas_call | solution.py:145
  51.5 1.0 reshape.44
  52.5 15.2 %all-to-all-start = ((bf16[512,4,128]{2,1,0:T(4,128)(2,1)}), bf16[512,4,128]{2,1,0:T(4,128)(2,1)}, u32[]{:S(2)}, u32[]{:S(2)}) async-start(bf16[512,4,128]{2,1,0:T(4,128)(2,1)} %reshape.44), calls=%async_computation | async-start | bytes 1048576 | tf_op jit(solution)/shard_map/all_to_all | solution.py:261
  67.7 6.3 %collective-permute-start.3 = (bf16[5120,256]{1,0:T(8,128)(2,1)}, bf16[5120,256]{1,0:T(8,128)(2,1)S(1)}, u32[]{:S(2)}, u32[]{:S(2)}) collective-permute-start(bf16[5120,256]{1,0:T(8,128)(2,1)} %pad_maximum_fusion.w0), channel_id=1, source_target_pairs={{0,1},{1,0},{2,3},{3,2},{4,5},{5,4},{6,7},{7,6},{8,9},{9,8},{10,11... | collective-permute-start | bytes 7864328 | tf_op jit(solution)/shard_map/ppermute | solution.py:256
  74.0 14.8 %all-to-all-done = bf16[512,4,128]{2,1,0:T(4,128)(2,1)} async-done(((bf16[512,4,128]{2,1,0:T(4,128)(2,1)}), bf16[512,4,128]{2,1,0:T(4,128)(2,1)}, u32[]{:S(2)}, u32[]{:S(2)}) %all-to-all-start) | async-done | bytes 524320 | tf_op jit(solution)/shard_map/all_to_all | solution.py:261
  88.8 5.3 %collective-permute-start.5 = (bf16[5120,256]{1,0:T(8,128)(2,1)}, bf16[5120,256]{1,0:T(8,128)(2,1)}, u32[]{:S(2)}, u32[]{:S(2)}) collective-permute-start(bf16[5120,256]{1,0:T(8,128)(2,1)} %collective-permute-done.4.w2), channel_id=1, source_target_pairs={{0,1},{1,0},{2,3},{3,2},{4,5},{5,4},{6,7},{7,6},{8,9},{9,8},{10,11... | collective-permute-start | bytes 7864328 | tf_op jit(solution)/shard_map/ppermute | solution.py:262
  94.2 1.2 reshape.45.moved
  95.4 3.4 %collective-permute-done.5.w3 = bf16[5120,256]{1,0:T(8,128)(2,1)} collective-permute-done((bf16[5120,256]{1,0:T(8,128)(2,1)}, bf16[5120,256]{1,0:T(8,128)(2,1)}, u32[]{:S(2)}, u32[]{:S(2)}) %collective-permute-start.5) | collective-permute-done | bytes 2621472 | tf_op jit(solution)/shard_map/ppermute | solution.py:262
  98.9 6.9 %col_layer.1 = bf16[4,128,256]{2,1,0:T(8,128)(2,1)S(1)} custom-call(s32[4]{0:T(128)S(1)} %pad_add_fusion.place, bf16[4,128,512]{2,1,0:T(8,128)(2,1)S(1)} %reshape.45.moved, f32[4,1,256]{2,1,0:T(1,128)S(1)} %bitcast.40, bf16[5120,256]{1,0:T(8,128)(2,1)} %pad_maximum_fusion.w0, bf16[5120,256]{1,0:T(8,128)(2,1)S(1)} %collective-permute-done.3.w1, ...), custom_call_target="tpu_custom_call" | custom-call | flops 1 | bytes 1 | tf_op jit(solution)/shard_map/col_layer/pallas_call | solution.py:205
  105.8 27.0 %all_to_all.10 = bf16[512,2,128]{2,1,0:T(2,128)(2,1)S(1)} all-to-all(bf16[512,2,128]{2,1,0:T(2,128)(2,1)S(1)} %reshape.47), channel_id=1, replica_groups=mesh['yh'=4,'z'=8,'x'=4,'yl'=2,'c'=2] {'yl','c','yh','z','x'}, dimensions={0} | all-to-all | bytes 524288 | tf_op jit(solution)/shard_map/all_to_all | solution.py:269
  (21 shorter events, 1.5 us)
Async XLA Ops:
  0.0 14.4 %copy-start.4 = (bf16[1024,3,256]{2,0,1:T(8,128)(2,1)S(1)}, bf16[1024,3,256]{2,0,1:T(8,128)(2,1)}, u32[]{:S(2)}) copy-start(bf16[1024,3,256]{2,0,1:T(8,128)(2,1)} %param.13) | copy-start | bytes 4718596
  0.0 16.7 %collective-permute-start.1 = (bf16[512,256]{1,0:T(8,128)(2,1)}, bf16[512,256]{1,0:T(8,128)(2,1)S(1)}, u32[]{:S(2)}, u32[]{:S(2)}) collective-permute-start(bf16[512,256]{1,0:T(8,128)(2,1)} %source.1), channel_id=1, source_target_pairs={{0,4},{4,8},{8,12},{12,16},{16,20},{20,24},{24,28},{28,32},{32,36}... | collective-permute-start | bytes 786440 | tf_op jit(solution)/shard_map/ppermute | solution.py:242
  4.1 12.6 %collective-permute-start = (bf16[512,256]{1,0:T(8,128)(2,1)}, bf16[512,256]{1,0:T(8,128)(2,1)S(1)}, u32[]{:S(2)}, u32[]{:S(2)}) collective-permute-start(bf16[512,256]{1,0:T(8,128)(2,1)} %source.1), channel_id=1, source_target_pairs={{0,2},{2,0},{1,3},{3,1},{4,6},{6,4},{5,7},{7,5},{8,10},{10,8},{9,1... | collective-permute-start | bytes 786440 | tf_op jit(solution)/shard_map/ppermute | solution.py:241
  14.4 2.1 %copy-start.5 = (bf16[1024,3,256]{2,0,1:T(8,128)(2,1)S(1)}, bf16[1024,3,256]{2,0,1:T(8,128)(2,1)}, u32[]{:S(2)}) copy-start(bf16[1024,3,256]{2,0,1:T(8,128)(2,1)} %param.10) | copy-start | bytes 4718596
  14.4 2.1 %copy-start.6 = (bf16[3]{0:T(256)(128)(2,1)S(1)}, bf16[3]{0:T(256)(128)(2,1)}, u32[]{:S(2)}) copy-start(bf16[3]{0:T(256)(128)(2,1)} %constant.30.clone) | copy-start | bytes 22
  16.5 27.6 %copy-start.2 = (f32[1024]{0:T(1024)S(1)}, f32[1024]{0:T(1024)}, u32[]{:S(2)}) copy-start(f32[1024]{0:T(1024)} %param.9) | copy-start | bytes 12292
  16.7 31.6 %copy-start.1 = (bf16[512,256]{1,0:T(8,128)(2,1)S(1)}, bf16[512,256]{1,0:T(8,128)(2,1)}, u32[]{:S(2)}) copy-start(bf16[512,256]{1,0:T(8,128)(2,1)} %source.1) | copy-start | bytes 786436
  16.7 10.1 %collective-permute-start.2 = (bf16[512,256]{1,0:T(8,128)(2,1)S(1)}, bf16[512,256]{1,0:T(8,128)(2,1)S(1)}, u32[]{:S(2)}, u32[]{:S(2)}) collective-permute-start(bf16[512,256]{1,0:T(8,128)(2,1)S(1)} %collective-permute-done.1), channel_id=1, source_target_pairs={{0,2},{2,0},{1,3},{3,1},{4,6},{6,4},{5,7},{7,5},{8,10},{10,8},{9,1... | collective-permute-start | bytes 786440 | tf_op jit(solution)/shard_map/ppermute | solution.py:245
  29.6 59.3 %collective-permute-start.4 = (bf16[5120,256]{1,0:T(8,128)(2,1)}, bf16[5120,256]{1,0:T(8,128)(2,1)}, u32[]{:S(2)}, u32[]{:S(2)}) collective-permute-start(bf16[5120,256]{1,0:T(8,128)(2,1)} %pad_maximum_fusion.w0), channel_id=1, source_target_pairs={{2,0},{0,2},{3,129},{129,3},{130,128},{128,130},{131,257},{257,131... | collective-permute-start | bytes 7864328 | tf_op jit(solution)/shard_map/ppermute | solution.py:255
  44.1 1.0 copy-start
  51.5 47.3 %copy-start.3 = (f32[1024]{0:T(1024)S(1)}, f32[1024]{0:T(1024)}, u32[]{:S(2)}) copy-start(f32[1024]{0:T(1024)} %param.12) | copy-start | bytes 12292
  52.5 36.3 %all-to-all-start = ((bf16[512,4,128]{2,1,0:T(4,128)(2,1)}), bf16[512,4,128]{2,1,0:T(4,128)(2,1)}, u32[]{:S(2)}, u32[]{:S(2)}) async-start(bf16[512,4,128]{2,1,0:T(4,128)(2,1)} %reshape.44), calls=%async_computation | async-start | bytes 1048576 | tf_op jit(solution)/shard_map/all_to_all | solution.py:261
  67.7 27.7 %collective-permute-start.3 = (bf16[5120,256]{1,0:T(8,128)(2,1)}, bf16[5120,256]{1,0:T(8,128)(2,1)S(1)}, u32[]{:S(2)}, u32[]{:S(2)}) collective-permute-start(bf16[5120,256]{1,0:T(8,128)(2,1)} %pad_maximum_fusion.w0), channel_id=1, source_target_pairs={{0,1},{1,0},{2,3},{3,2},{4,5},{5,4},{6,7},{7,6},{8,9},{9,8},{10,11... | collective-permute-start | bytes 7864328 | tf_op jit(solution)/shard_map/ppermute | solution.py:256
  88.8 10.0 %collective-permute-start.5 = (bf16[5120,256]{1,0:T(8,128)(2,1)}, bf16[5120,256]{1,0:T(8,128)(2,1)}, u32[]{:S(2)}, u32[]{:S(2)}) collective-permute-start(bf16[5120,256]{1,0:T(8,128)(2,1)} %collective-permute-done.4.w2), channel_id=1, source_target_pairs={{0,1},{1,0},{2,3},{3,2},{4,5},{5,4},{6,7},{7,6},{8,9},{9,8},{10,11... | collective-permute-start | bytes 7864328 | tf_op jit(solution)/shard_map/ppermute | solution.py:262

commit v5 on v3

--- a/solution.py
+++ b/solution.py
@@ -159,8 +159,30 @@
 QKV_AT, OUT_AT, WEIGHT_ROWS = 1024, 4096, 5120
 
 
-def column_blocks(w):
-    return w.reshape(GROUP, PARTS, GROUP).transpose(1, 0, 2).reshape(PARTS * GROUP, GROUP)
+def pack_kernel(row_out, col_qkv, col_out, packed, sem):
+    pairs = [(col_qkv, packed.at[QKV_AT:OUT_AT])]
+    for source, at in ((row_out, 0), (col_out, OUT_AT)):
+        for n in range(PARTS):
+            rows = slice(at + n * GROUP, at + (n + 1) * GROUP)
+            pairs.append((source.at[:, n * GROUP : (n + 1) * GROUP], packed.at[rows]))
+    copies = [pltpu.make_async_copy(a, b, sem.at[i]) for i, (a, b) in enumerate(pairs)]
+    for copy in copies:
+        copy.start()
+    for copy in copies:
+        copy.wait()
+
+
+def pack_weights(row_out, col_qkv, col_out):
+    return pl.pallas_call(
+        pack_kernel,
+        out_shape=jax.ShapeDtypeStruct((WEIGHT_ROWS, GROUP), jnp.bfloat16),
+        in_specs=[ANY] * 3,
+        out_specs=ANY,
+        scratch_shapes=[pltpu.SemaphoreType.DMA((2 * PARTS + 1,))],
+        compiler_params=pltpu.CompilerParams(vmem_limit_bytes=MIB),
+        cost_estimate=pl.CostEstimate(flops=1, bytes_accessed=1, transcendentals=0),
+        name="pack_weights",
+    )(row_out, col_qkv, col_out)
 
 
 def col_layer_kernel(place, moved, gain, w0, w1, w2, w3, out, held, sem):
@@ -240,24 +262,23 @@
 
     other = lax.ppermute(inputs, "yl", SWAP)
     before = lax.ppermute(inputs, SEQ, [(i, i + 1) for i in range(127)])
+    before_other = lax.ppermute(
+        inputs, SEQ + ("yl",), [(2 * i + j, 2 * i + 3 - j) for i in range(127) for j in range(2)]
+    )
     near = lax.all_gather(inputs, "c", axis=0)
-    far = lax.all_gather(after(other, near), "c", axis=0)
-    before_other = lax.ppermute(after(before, far), "yl", SWAP)
-
-    mine = jnp.concatenate(
-        [column_blocks(row_out), col_qkv.transpose(1, 0, 2).reshape(3 * 1024, GROUP), column_blocks(col_out)]
-    )
-    mine, row_qkv = lax.optimization_barrier((mine, row_qkv, before, other, near))[:2]
+    mine = pack_weights(row_out, col_qkv.transpose(1, 0, 2).reshape(3 * 1024, GROUP), col_out)
+    mine, row_qkv, other = lax.optimization_barrier((mine, row_qkv, other, near))[:3]
+    far = lax.all_gather(other, "c", axis=0)
+    state = row_own(place, near, far, row_gain, row_qkv)
+    mine = after(mine, before, before_other, state[0])
     theirs = lax.ppermute(mine, ("yh", "yl", "c"), cross_route((1,)))
-
-    state = row_own(place, near, far, row_gain, row_qkv)
-    mine_swapped = lax.ppermute(after(mine, state[0]), "c", SWAP)
     before_near = lax.all_gather(after(before, state[0]), "c", axis=0)
     before_far = lax.all_gather(after(before_other, before_near), "c", axis=0)
     sent = row_halo(place, before_near, before_far, row_gain, row_qkv, state, inputs)
-    theirs_swapped = lax.ppermute(after(theirs, sent), "c", SWAP)
+    mine_swapped = lax.ppermute(after(mine, sent), "c", SWAP)
 
     moved = lax.all_to_all(sent.reshape(COLS, 4, 128), HEAD + SEQ, 0, 0, tiled=True)
+    theirs_swapped = lax.ppermute(after(theirs, moved), "c", SWAP)
     mixed = col_layer(
         place,
         moved.reshape(PARTS, 128, 2 * GROUP),

time: 148 us -> 138 us (0.932)
  blocking collectives: 98.5 us -> 38.8 us
  starting transfers between devices: 28.5 us -> 55.8 us
  waiting for transfers between devices: 0.02 us -> 23 us
  local copies, waits for them, and re-layouts: 5.56 us -> 3.42 us
  Pallas kernels: 13.2 us -> 14.8 us
    all_to_all x1 -> x0, blocking collectives: 47 us -> none  [on_device(): lax.all_to_all(sent.reshape(COLS, 4, 128), HEAD + SEQ, 0, 0, tiled=True)]
    all_to_all x0 -> x1, waiting for transfers between devices: none -> 19.2 us  [on_device(): lax.all_to_all(sent.reshape(COLS, 4, 128), HEAD + SEQ, 0, 0, tiled=True)]
    all_to_all x0 -> x1, starting transfers between devices: none -> 15.6 us  [on_device(): lax.all_to_all(sent.reshape(COLS, 4, 128), HEAD + SEQ, 0, 0, tiled=True)]
    all_gather x1, blocking collectives: 12.3 us -> 2.17 us  [on_device(): before_far = lax.all_gather(after(before_other, before_near), 'c', axis=0)]
    ppermute x1, starting transfers between devices: 14.9 us -> 21.7 us  [on_device(): theirs = lax.ppermute(mine, ('yh', 'yl', 'c'), cross_route((1,)))]
    ppermute x3, starting transfers between devices: 6.24 us -> 11.4 us  [the longest x1 6.28 us: on_device(): mine_swapped = lax.ppermute(after(mine, sent), 'c', SWAP)]
    ppermute x3, waiting for transfers between devices: 0.01 us -> 3.79 us  [the longest x1 3.78 us: on_device(): theirs_swapped = lax.ppermute(after(theirs, moved), 'c', SWAP)]
    all_gather x1, blocking collectives: 5.12 us -> 2.18 us  [on_device(): before_near = lax.all_gather(after(before, state[0]), 'c', axis=0)]
  transfers between devices with their start and end apart: 6 -> 7, of which waited for: 0 -> 2; matrix products, arithmetic and copies ran while one was open for 4% -> 3% of each run, Pallas kernels for 4% -> 6%
where the time goes in v5:
time: 138 us
  starting transfers between devices  55.8 us (40%)
  blocking collectives  38.8 us (28%)
  waiting for transfers between devices  23 us (17%)
  Pallas kernels  14.8 us (11%)
  local copies, waits for them, and re-layouts  3.42 us (2%)
  other arithmetic  1.81 us (1%)
    all_to_all x1, blocking collectives, on_device(): lax.all_to_all(mixed.reshape(COLS, 2, 128), HEAD + SEQ, 0, 0, tiled=True)  28.9 us
    ppermute x1, starting transfers between devices, on_device(): theirs = lax.ppermute(mine, ('yh', 'yl', 'c'), cross_route((1,)))  21.7 us
    all_to_all x1, waiting for transfers between devices, on_device(): lax.all_to_all(sent.reshape(COLS, 4, 128), HEAD + SEQ, 0, 0, tiled=True)  19.2 us
    all_to_all x1, starting transfers between devices, on_device(): lax.all_to_all(sent.reshape(COLS, 4, 128), HEAD + SEQ, 0, 0, tiled=True)  15.6 us
    pallas_call x1, Pallas kernels, col_layer(): pl.pallas_call(col_layer_kernel, out_shape=jax.ShapeDtypeStruct((PARTS, 1...  6.89 us
    ppermute x1, starting transfers between devices, on_device(): mine_swapped = lax.ppermute(after(mine, sent), 'c', SWAP)  6.28 us
    ppermute x1, starting transfers between devices, on_device(): other = lax.ppermute(inputs, 'yl', SWAP)  4.02 us
    ppermute x1, waiting for transfers between devices, on_device(): theirs_swapped = lax.ppermute(after(theirs, moved), 'c', SWAP)  3.78 us
  transfers between devices with their start and end apart: 7, of which 2 were waited for; matrix products, arithmetic and copies ran while one was open for 3% of the time, Pallas kernels for 6%

profile of v5, /device:TPU:1, one launch (start us, length us, event | category | flops | bytes accessed | tf_op | source)
XLA Modules:
  0.0 137.8 jit_solution(16180768572337856543)
XLA Ops:
  0.0 4.0 %collective-permute-start.1 = (bf16[512,256]{1,0:T(8,128)(2,1)}, bf16[512,256]{1,0:T(8,128)(2,1)S(1)}, u32[]{:S(2)}, u32[]{:S(2)}) collective-permute-start(bf16[512,256]{1,0:T(8,128)(2,1)} %source.1), channel_id=1, source_target_pairs={{0,2},{2,0},{1,3},{3,1},{4,6},{6,4},{5,7},{7,5},{8,10},{10,8},{9,1... | collective-permute-start | bytes 786440 | tf_op jit(solution)/shard_map/ppermute | solution.py:263
  4.0 3.1 %collective-permute-start = (bf16[512,256]{1,0:T(8,128)(2,1)}, bf16[512,256]{1,0:T(8,128)(2,1)S(1)}, u32[]{:S(2)}, u32[]{:S(2)}) collective-permute-start(bf16[512,256]{1,0:T(8,128)(2,1)} %source.1), channel_id=1, source_target_pairs={{0,4},{4,8},{8,12},{12,16},{16,20},{20,24},{24,28},{28,32},{32,36}... | collective-permute-start | bytes 786440 | tf_op jit(solution)/shard_map/ppermute | solution.py:264
  7.2 3.0 %collective-permute-start.2 = (bf16[512,256]{1,0:T(8,128)(2,1)}, bf16[512,256]{1,0:T(8,128)(2,1)S(1)}, u32[]{:S(2)}, u32[]{:S(2)}) collective-permute-start(bf16[512,256]{1,0:T(8,128)(2,1)} %source.1), channel_id=1, source_target_pairs={{0,6},{2,4},{4,10},{6,8},{8,14},{10,12},{12,18},{14,16},{16,22},{1... | collective-permute-start | bytes 786440 | tf_op jit(solution)/shard_map/ppermute | solution.py:265
  10.2 1.7 %broadcast_multiply_fusion.weight = bf16[3,4,256,256]{3,2,1,0:T(8,128)(2,1)S(1)} fusion(bf16[3,4,256,256]{3,2,1,0:T(8,128)(2,1)} %bitcast.28, bf16[3]{0:T(256)(128)(2,1)} %constant.30.clone), kind=kLoop, calls=%fused_computation | loop fusion | flops 786432 | bytes 3145734 | tf_op jit(solution)/shard_map/mul | solution.py:261
  12.0 0.1 copy-done
  12.2 0.2 copy-done.3
  12.4 1.6 %pack_weights.1.w0 = bf16[5120,256]{1,0:T(8,128)(2,1)} custom-call(bf16[256,1024]{1,0:T(8,128)(2,1)S(1)} %copy-done.2, bf16[3072,256]{1,0:T(8,128)(2,1)S(1)} %bitcast.24, bf16[256,1024]{1,0:T(8,128)(2,1)S(1)} %copy-done.3), custom_call_target="tpu_custom_call" | custom-call | flops 1 | bytes 1 | tf_op jit(solution)/shard_map/pack_weights/pallas_call | solution.py:176
  14.1 3.3 %all-gather = bf16[1024,256]{1,0:T(8,128)(2,1)S(1)} all-gather(bf16[512,256]{1,0:T(8,128)(2,1)S(1)} %copy-done.1), channel_id=2, replica_groups=mesh['yh'=4,'z'=8,'x'=4,'yl'=2,'c'=2] {'c'}, dimensions={0}, use_global_device_ids=true | all-gather | bytes 786432 | tf_op jit(solution)/shard_map/all_gather | solution.py:268
  17.4 2.2 %all-gather.1 = bf16[1024,256]{1,0:T(8,128)(2,1)S(1)} all-gather(bf16[512,256]{1,0:T(8,128)(2,1)S(1)} %collective-permute-done.1), channel_id=3, replica_groups=mesh['yh'=4,'z'=8,'x'=4,'yl'=2,'c'=2] {'c'}, dimensions={0}, use_global_device_ids=true | all-gather | bytes 786432 | tf_op jit(solution)/shard_map/all_gather | solution.py:271
  19.5 3.1 %row_own.1 = (bf16[512,256]{1,0:T(8,128)(2,1)S(1)}, f32[512,256]{1,0:T(8,128)S(1)}, f32[512,256]{1,0:T(8,128)S(1)}, f32[512,256]{1,0:T(8,128)S(1)}) custom-call(s32[4]{0:T(128)S(1)} %pad_add_fusion.place, bf16[2,512,256]{2,1,0:T(8,128)(2,1)S(1)} %bitcast.22, bf16[2,512,256]{2,1,0:T(8,128)(2,1)S(1)} %bitcast.23, f32[4,1,256]{2,1,0:T(1,128)S(1)} %bitcast.25, ...), custom_call_target="tpu_custom_call" | custom-call | flops 1 | bytes 1 | tf_op jit(solution)/shard_map/row_own/pallas_call | solution.py:102
  22.6 21.7 %collective-permute-start.4 = (bf16[5120,256]{1,0:T(8,128)(2,1)}, bf16[5120,256]{1,0:T(8,128)(2,1)}, u32[]{:S(2)}, u32[]{:S(2)}) collective-permute-start(bf16[5120,256]{1,0:T(8,128)(2,1)} %pack_weights.1.w0), channel_id=1, source_target_pairs={{2,0},{0,2},{3,129},{129,3},{130,128},{128,130},{131,257},{257,131... | collective-permute-start | bytes 7864328 | tf_op jit(solution)/shard_map/ppermute | solution.py:274
  44.3 2.2 %all-gather.2 = bf16[1024,256]{1,0:T(8,128)(2,1)S(1)} all-gather(bf16[512,256]{1,0:T(8,128)(2,1)S(1)} %collective-permute-done), channel_id=4, replica_groups=mesh['yh'=4,'z'=8,'x'=4,'yl'=2,'c'=2] {'c'}, dimensions={0}, use_global_device_ids=true | all-gather | bytes 786432 | tf_op jit(solution)/shard_map/all_gather | solution.py:275
  46.5 2.2 %all-gather.3 = bf16[1024,256]{1,0:T(8,128)(2,1)S(1)} all-gather(bf16[512,256]{1,0:T(8,128)(2,1)S(1)} %collective-permute-done.2), channel_id=5, replica_groups=mesh['yh'=4,'z'=8,'x'=4,'yl'=2,'c'=2] {'c'}, dimensions={0}, use_global_device_ids=true | all-gather | bytes 786432 | tf_op jit(solution)/shard_map/all_gather | solution.py:276
  48.7 3.3 %row_halo.1 = bf16[512,512]{1,0:T(8,128)(2,1)S(1)} custom-call(s32[4]{0:T(128)S(1)} %pad_add_fusion.place, bf16[2,512,256]{2,1,0:T(8,128)(2,1)S(1)} %bitcast.20, bf16[2,512,256]{2,1,0:T(8,128)(2,1)S(1)} %bitcast.21, f32[4,1,256]{2,1,0:T(1,128)S(1)} %bitcast.26, bf16[3,4,256,256]{3,2,1,0:T(8,128)(2,1)S(1)} %broadcast_multiply_fusion.weight, ...), custom_call_target="tpu_custom_call" | custom-call | flops 1 | bytes 1 | tf_op jit(solution)/shard_map/row_halo/pallas_call | solution.py:145
  52.0 1.0 reshape.28
  52.9 15.6 %all-to-all-start = ((bf16[512,4,128]{2,1,0:T(4,128)(2,1)}), bf16[512,4,128]{2,1,0:T(4,128)(2,1)}, u32[]{:S(2)}, u32[]{:S(2)}) async-start(bf16[512,4,128]{2,1,0:T(4,128)(2,1)} %reshape.28), calls=%async_computation | async-start | bytes 1048576 | tf_op jit(solution)/shard_map/all_to_all | solution.py:280
  68.6 6.3 %collective-permute-start.3 = (bf16[5120,256]{1,0:T(8,128)(2,1)}, bf16[5120,256]{1,0:T(8,128)(2,1)S(1)}, u32[]{:S(2)}, u32[]{:S(2)}) collective-permute-start(bf16[5120,256]{1,0:T(8,128)(2,1)} %pack_weights.1.w0), channel_id=1, source_target_pairs={{0,1},{1,0},{2,3},{3,2},{4,5},{5,4},{6,7},{7,6},{8,9},{9,8},{10,11... | collective-permute-start | bytes 7864328 | tf_op jit(solution)/shard_map/ppermute | solution.py:278
  74.8 19.2 %all-to-all-done = bf16[512,4,128]{2,1,0:T(4,128)(2,1)} async-done(((bf16[512,4,128]{2,1,0:T(4,128)(2,1)}), bf16[512,4,128]{2,1,0:T(4,128)(2,1)}, u32[]{:S(2)}, u32[]{:S(2)}) %all-to-all-start) | async-done | bytes 524320 | tf_op jit(solution)/shard_map/all_to_all | solution.py:280
  94.0 2.1 %collective-permute-start.5 = (bf16[5120,256]{1,0:T(8,128)(2,1)}, bf16[5120,256]{1,0:T(8,128)(2,1)}, u32[]{:S(2)}, u32[]{:S(2)}) collective-permute-start(bf16[5120,256]{1,0:T(8,128)(2,1)} %collective-permute-done.4.w2), channel_id=1, source_target_pairs={{0,1},{1,0},{2,3},{3,2},{4,5},{5,4},{6,7},{7,6},{8,9},{9,8},{10,11... | collective-permute-start | bytes 7864328 | tf_op jit(solution)/shard_map/ppermute | solution.py:281
  96.1 1.2 reshape.29.moved
  97.4 3.8 %collective-permute-done.5.w3 = bf16[5120,256]{1,0:T(8,128)(2,1)} collective-permute-done((bf16[5120,256]{1,0:T(8,128)(2,1)}, bf16[5120,256]{1,0:T(8,128)(2,1)}, u32[]{:S(2)}, u32[]{:S(2)}) %collective-permute-start.5) | collective-permute-done | bytes 2621472 | tf_op jit(solution)/shard_map/ppermute | solution.py:281
  101.2 6.9 %col_layer.1 = bf16[4,128,256]{2,1,0:T(8,128)(2,1)S(1)} custom-call(s32[4]{0:T(128)S(1)} %pad_add_fusion.place, bf16[4,128,512]{2,1,0:T(8,128)(2,1)S(1)} %reshape.29.moved, f32[4,1,256]{2,1,0:T(1,128)S(1)} %bitcast.27, bf16[5120,256]{1,0:T(8,128)(2,1)} %pack_weights.1.w0, bf16[5120,256]{1,0:T(8,128)(2,1)S(1)} %collective-permute-done.3.w1, ...), custom_call_target="tpu_custom_call" | custom-call | flops 1 | bytes 1 | tf_op jit(solution)/shard_map/col_layer/pallas_call | solution.py:227
  108.1 28.9 %all_to_all.10 = bf16[512,2,128]{2,1,0:T(2,128)(2,1)S(1)} all-to-all(bf16[512,2,128]{2,1,0:T(2,128)(2,1)S(1)} %reshape.31), channel_id=1, replica_groups=mesh['yh'=4,'z'=8,'x'=4,'yl'=2,'c'=2] {'yl','c','yh','z','x'}, dimensions={0} | all-to-all | bytes 524288 | tf_op jit(solution)/shard_map/all_to_all | solution.py:288
  137.1 0.7 copy.11
  (17 shorter events, 0.3 us)
Async XLA Ops:
  0.0 17.4 %collective-permute-start.1 = (bf16[512,256]{1,0:T(8,128)(2,1)}, bf16[512,256]{1,0:T(8,128)(2,1)S(1)}, u32[]{:S(2)}, u32[]{:S(2)}) collective-permute-start(bf16[512,256]{1,0:T(8,128)(2,1)} %source.1), channel_id=1, source_target_pairs={{0,2},{2,0},{1,3},{3,1},{4,6},{6,4},{5,7},{7,5},{8,10},{10,8},{9,1... | collective-permute-start | bytes 786440 | tf_op jit(solution)/shard_map/ppermute | solution.py:263
  4.0 18.6 %collective-permute-start = (bf16[512,256]{1,0:T(8,128)(2,1)}, bf16[512,256]{1,0:T(8,128)(2,1)S(1)}, u32[]{:S(2)}, u32[]{:S(2)}) collective-permute-start(bf16[512,256]{1,0:T(8,128)(2,1)} %source.1), channel_id=1, source_target_pairs={{0,4},{4,8},{8,12},{12,16},{16,20},{20,24},{24,28},{28,32},{32,36}... | collective-permute-start | bytes 786440 | tf_op jit(solution)/shard_map/ppermute | solution.py:264
  7.2 15.5 %collective-permute-start.2 = (bf16[512,256]{1,0:T(8,128)(2,1)}, bf16[512,256]{1,0:T(8,128)(2,1)S(1)}, u32[]{:S(2)}, u32[]{:S(2)}) collective-permute-start(bf16[512,256]{1,0:T(8,128)(2,1)} %source.1), channel_id=1, source_target_pairs={{0,6},{2,4},{4,10},{6,8},{8,14},{10,12},{12,18},{14,16},{16,22},{1... | collective-permute-start | bytes 786440 | tf_op jit(solution)/shard_map/ppermute | solution.py:265
  10.2 1.9 %copy-start = (bf16[1024,3,256]{2,0,1:T(8,128)(2,1)S(1)}, bf16[1024,3,256]{2,0,1:T(8,128)(2,1)}, u32[]{:S(2)}) copy-start(bf16[1024,3,256]{2,0,1:T(8,128)(2,1)} %param.13) | copy-start | bytes 4718596
  10.2 2.0 %copy-start.2 = (bf16[256,1024]{1,0:T(8,128)(2,1)S(1)}, bf16[256,1024]{1,0:T(8,128)(2,1)}, u32[]{:S(2)}) copy-start(bf16[256,1024]{1,0:T(8,128)(2,1)} %row_out.1) | copy-start | bytes 1572868
  10.2 2.1 %copy-start.3 = (bf16[256,1024]{1,0:T(8,128)(2,1)S(1)}, bf16[256,1024]{1,0:T(8,128)(2,1)}, u32[]{:S(2)}) copy-start(bf16[256,1024]{1,0:T(8,128)(2,1)} %col_out.1) | copy-start | bytes 1572868
  12.4 1.7 %copy-start.1 = (bf16[512,256]{1,0:T(8,128)(2,1)S(1)}, bf16[512,256]{1,0:T(8,128)(2,1)}, u32[]{:S(2)}) copy-start(bf16[512,256]{1,0:T(8,128)(2,1)} %source.1) | copy-start | bytes 786436
  14.0 5.6 %copy-start.4 = (f32[1024]{0:T(1024)S(1)}, f32[1024]{0:T(1024)}, u32[]{:S(2)}) copy-start(f32[1024]{0:T(1024)} %param.9) | copy-start | bytes 12292
  22.6 71.4 %collective-permute-start.4 = (bf16[5120,256]{1,0:T(8,128)(2,1)}, bf16[5120,256]{1,0:T(8,128)(2,1)}, u32[]{:S(2)}, u32[]{:S(2)}) collective-permute-start(bf16[5120,256]{1,0:T(8,128)(2,1)} %pack_weights.1.w0), channel_id=1, source_target_pairs={{2,0},{0,2},{3,129},{129,3},{130,128},{128,130},{131,257},{257,131... | collective-permute-start | bytes 7864328 | tf_op jit(solution)/shard_map/ppermute | solution.py:274
  51.9 49.2 %copy-start.5 = (f32[1024]{0:T(1024)S(1)}, f32[1024]{0:T(1024)}, u32[]{:S(2)}) copy-start(f32[1024]{0:T(1024)} %param.12) | copy-start | bytes 12292
  52.9 41.1 %all-to-all-start = ((bf16[512,4,128]{2,1,0:T(4,128)(2,1)}), bf16[512,4,128]{2,1,0:T(4,128)(2,1)}, u32[]{:S(2)}, u32[]{:S(2)}) async-start(bf16[512,4,128]{2,1,0:T(4,128)(2,1)} %reshape.28), calls=%async_computation | async-start | bytes 1048576 | tf_op jit(solution)/shard_map/all_to_all | solution.py:280
  68.6 28.8 %collective-permute-start.3 = (bf16[5120,256]{1,0:T(8,128)(2,1)}, bf16[5120,256]{1,0:T(8,128)(2,1)S(1)}, u32[]{:S(2)}, u32[]{:S(2)}) collective-permute-start(bf16[5120,256]{1,0:T(8,128)(2,1)} %pack_weights.1.w0), channel_id=1, source_target_pairs={{0,1},{1,0},{2,3},{3,2},{4,5},{5,4},{6,7},{7,6},{8,9},{9,8},{10,11... | collective-permute-start | bytes 7864328 | tf_op jit(solution)/shard_map/ppermute | solution.py:278
  94.0 7.1 %collective-permute-start.5 = (bf16[5120,256]{1,0:T(8,128)(2,1)}, bf16[5120,256]{1,0:T(8,128)(2,1)}, u32[]{:S(2)}, u32[]{:S(2)}) collective-permute-start(bf16[5120,256]{1,0:T(8,128)(2,1)} %collective-permute-done.4.w2), channel_id=1, source_target_pairs={{0,1},{1,0},{2,3},{3,2},{4,5},{5,4},{6,7},{7,6},{8,9},{9,8},{10,11... | collective-permute-start | bytes 7864328 | tf_op jit(solution)/shard_map/ppermute | solution.py:281

commit v6 on v5

--- a/solution.py
+++ b/solution.py
@@ -260,20 +260,20 @@
     row_qkv = row_qkv.transpose(1, 0, 2).reshape(3, PARTS, GROUP, GROUP)
     row_qkv = row_qkv * jnp.array([SCALE, 1, 1], jnp.bfloat16)[:, None, None, None]
 
+    before = lax.ppermute(inputs, SEQ, [(i, i + 1) for i in range(127)])
     other = lax.ppermute(inputs, "yl", SWAP)
-    before = lax.ppermute(inputs, SEQ, [(i, i + 1) for i in range(127)])
-    before_other = lax.ppermute(
-        inputs, SEQ + ("yl",), [(2 * i + j, 2 * i + 3 - j) for i in range(127) for j in range(2)]
-    )
     near = lax.all_gather(inputs, "c", axis=0)
     mine = pack_weights(row_out, col_qkv.transpose(1, 0, 2).reshape(3 * 1024, GROUP), col_out)
-    mine, row_qkv, other = lax.optimization_barrier((mine, row_qkv, other, near))[:3]
-    far = lax.all_gather(other, "c", axis=0)
+    mine, row_qkv, before = lax.optimization_barrier((mine, row_qkv, before, near))[:3]
+    before_other = lax.ppermute(before, "yl", SWAP)
+    far = lax.all_gather(after(other, before), "c", axis=0)
+    before_near = lax.all_gather(after(before, far), "c", axis=0)
+    place = after(place, before_near)
     state = row_own(place, near, far, row_gain, row_qkv)
-    mine = after(mine, before, before_other, state[0])
+    before_far = lax.all_gather(after(before_other, state[0]), "c", axis=0)
+
+    mine = after(mine, before_far)
     theirs = lax.ppermute(mine, ("yh", "yl", "c"), cross_route((1,)))
-    before_near = lax.all_gather(after(before, state[0]), "c", axis=0)
-    before_far = lax.all_gather(after(before_other, before_near), "c", axis=0)
     sent = row_halo(place, before_near, before_far, row_gain, row_qkv, state, inputs)
     mine_swapped = lax.ppermute(after(mine, sent), "c", SWAP)
 

time: 138 us -> 135 us (0.978)
  starting transfers between devices: 55.8 us -> 49.2 us
  local copies, waits for them, and re-layouts: 3.42 us -> 7.48 us
  blocking collectives: 38.8 us -> 40.4 us
  other arithmetic: 1.81 us -> 0.25 us
    ppermute x1, starting transfers between devices: 21.7 us -> 15.9 us  [on_device(): theirs = lax.ppermute(mine, ('yh', 'yl', 'c'), cross_route((1,)))]
    all_to_all x1, starting transfers between devices: 15.6 us -> 11.3 us  [on_device(): lax.all_to_all(sent.reshape(COLS, 4, 128), HEAD + SEQ, 0, 0, tiled=True)]
    unnamed x13 -> x17, local copies, waits for them, and re-layouts: 1.15 us -> 5.22 us
    ppermute x1, starting transfers between devices: 2.09 us -> 4.91 us  [on_device(): theirs_swapped = lax.ppermute(after(theirs, moved), 'c', SWAP)]
    all_gather x1, blocking collectives: 3.31 us -> 4.96 us  [on_device(): near = lax.all_gather(inputs, 'c', axis=0)]
    mul x1, other arithmetic: 1.74 us -> 0.17 us  [on_device(): row_qkv * jnp.array([SCALE, 1, 1], jnp.bfloat16)[:, None, None, None]]
  transfers between devices with their start and end apart: 7 -> 7, of which waited for: 2 -> 2; matrix products, arithmetic and copies ran while one was open for 3% -> 2% of each run, Pallas kernels for 6% -> 5%
where the time goes in v6:
time: 135 us; the launch traced here: 134 us
  starting transfers between devices  49.2 us (36%)
  blocking collectives  40.4 us (30%)
  waiting for transfers between devices  23.3 us (17%)
  Pallas kernels  13.7 us (10%)
  local copies, waits for them, and re-layouts  7.48 us (6%)
    all_to_all x1, blocking collectives, on_device(): lax.all_to_all(mixed.reshape(COLS, 2, 128), HEAD + SEQ, 0, 0, tiled=True)  28.4 us
    all_to_all x1, waiting for transfers between devices, on_device(): lax.all_to_all(sent.reshape(COLS, 4, 128), HEAD + SEQ, 0, 0, tiled=True)  19.9 us
    ppermute x1, starting transfers between devices, on_device(): theirs = lax.ppermute(mine, ('yh', 'yl', 'c'), cross_route((1,)))  15.9 us
    all_to_all x1, starting transfers between devices, on_device(): lax.all_to_all(sent.reshape(COLS, 4, 128), HEAD + SEQ, 0, 0, tiled=True)  11.3 us
    pallas_call x1, Pallas kernels, col_layer(): pl.pallas_call(col_layer_kernel, out_shape=jax.ShapeDtypeStruct((PARTS, 1...  6.86 us
    ppermute x1, starting transfers between devices, on_device(): mine_swapped = lax.ppermute(after(mine, sent), 'c', SWAP)  6.28 us
    unnamed x17, local copies, waits for them, and re-layouts  5.22 us
    all_gather x1, blocking collectives, on_device(): near = lax.all_gather(inputs, 'c', axis=0)  4.96 us
  transfers between devices with their start and end apart: 7, of which 2 were waited for; matrix products, arithmetic and copies ran while one was open for 2% of the time, Pallas kernels for 5%

profile of v6, /device:TPU:1, one launch (start us, length us, event | category | flops | bytes accessed | tf_op | source)
XLA Modules:
  0.0 134.5 jit_solution(4020871605380665585)
XLA Ops:
  0.0 4.0 %collective-permute-start = (bf16[512,256]{1,0:T(8,128)(2,1)}, bf16[512,256]{1,0:T(8,128)(2,1)S(1)}, u32[]{:S(2)}, u32[]{:S(2)}) collective-permute-start(bf16[512,256]{1,0:T(8,128)(2,1)} %source.1), channel_id=1, source_target_pairs={{0,4},{4,8},{8,12},{12,16},{16,20},{20,24},{24,28},{28,32},{32,36}... | collective-permute-start | bytes 786440 | tf_op jit(solution)/shard_map/ppermute | solution.py:263
  4.0 3.2 %collective-permute-start.1 = (bf16[512,256]{1,0:T(8,128)(2,1)}, bf16[512,256]{1,0:T(8,128)(2,1)}, u32[]{:S(2)}, u32[]{:S(2)}) collective-permute-start(bf16[512,256]{1,0:T(8,128)(2,1)} %source.1), channel_id=1, source_target_pairs={{0,2},{2,0},{1,3},{3,1},{4,6},{6,4},{5,7},{7,5},{8,10},{10,8},{9,1... | collective-permute-start | bytes 786440 | tf_op jit(solution)/shard_map/ppermute | solution.py:264
  7.2 5.0 %all-gather = bf16[1024,256]{1,0:T(8,128)(2,1)S(1)} all-gather(bf16[512,256]{1,0:T(8,128)(2,1)} %source.1), channel_id=2, replica_groups=mesh['yh'=4,'z'=8,'x'=4,'yl'=2,'c'=2] {'c'}, dimensions={0}, use_global_device_ids=true | all-gather | bytes 786432 | tf_op jit(solution)/shard_map/all_gather | solution.py:265
  12.1 1.4 %copy-done = bf16[1024,3,256]{2,0,1:T(8,128)(2,1)S(1)} copy-done((bf16[1024,3,256]{2,0,1:T(8,128)(2,1)S(1)}, bf16[1024,3,256]{2,0,1:T(8,128)(2,1)}, u32[]{:S(2)}) %copy-start) | copy-done | bytes 1572888
  13.5 1.0 copy-done.2
  14.6 1.0 copy-done.3
  16.1 1.0 copy-done.6
  17.2 3.6 %collective-permute-start.2 = (bf16[512,256]{1,0:T(8,128)(2,1)S(1)}, bf16[512,256]{1,0:T(8,128)(2,1)S(1)}, u32[]{:S(2)}, u32[]{:S(2)}) collective-permute-start(bf16[512,256]{1,0:T(8,128)(2,1)S(1)} %collective-permute-done), channel_id=1, source_target_pairs={{0,2},{2,0},{1,3},{3,1},{4,6},{6,4},{5,7},{7,5},{8,10},{10,8},{9,1... | collective-permute-start | bytes 786440 | tf_op jit(solution)/shard_map/ppermute | solution.py:268
  20.9 2.7 %all-gather.1 = bf16[1024,256]{1,0:T(8,128)(2,1)S(1)} all-gather(bf16[512,256]{1,0:T(8,128)(2,1)} %collective-permute-done.1), channel_id=3, replica_groups=mesh['yh'=4,'z'=8,'x'=4,'yl'=2,'c'=2] {'c'}, dimensions={0}, use_global_device_ids=true | all-gather | bytes 786432 | tf_op jit(solution)/shard_map/all_gather | solution.py:269
  23.6 2.2 %all-gather.2 = bf16[1024,256]{1,0:T(8,128)(2,1)S(1)} all-gather(bf16[512,256]{1,0:T(8,128)(2,1)S(1)} %collective-permute-done), channel_id=4, replica_groups=mesh['yh'=4,'z'=8,'x'=4,'yl'=2,'c'=2] {'c'}, dimensions={0}, use_global_device_ids=true | all-gather | bytes 786432 | tf_op jit(solution)/shard_map/all_gather | solution.py:270
  25.8 3.2 %row_own.1 = (bf16[512,256]{1,0:T(8,128)(2,1)S(1)}, f32[512,256]{1,0:T(8,128)S(1)}, f32[512,256]{1,0:T(8,128)S(1)}, f32[512,256]{1,0:T(8,128)S(1)}) custom-call(s32[4]{0:T(128)S(1)} %pad_add_fusion.place, bf16[2,512,256]{2,1,0:T(8,128)(2,1)S(1)} %bitcast.22, bf16[2,512,256]{2,1,0:T(8,128)(2,1)S(1)} %bitcast.23, f32[4,1,256]{2,1,0:T(1,128)S(1)} %bitcast.25, ...), custom_call_target="tpu_custom_call" | custom-call | flops 1 | bytes 1 | tf_op jit(solution)/shard_map/row_own/pallas_call | solution.py:102
  28.9 2.2 %all-gather.3 = bf16[1024,256]{1,0:T(8,128)(2,1)S(1)} all-gather(bf16[512,256]{1,0:T(8,128)(2,1)S(1)} %collective-permute-done.2), channel_id=5, replica_groups=mesh['yh'=4,'z'=8,'x'=4,'yl'=2,'c'=2] {'c'}, dimensions={0}, use_global_device_ids=true | all-gather | bytes 786432 | tf_op jit(solution)/shard_map/all_gather | solution.py:273
  31.1 15.9 %collective-permute-start.4 = (bf16[5120,256]{1,0:T(8,128)(2,1)S(1)}, bf16[5120,256]{1,0:T(8,128)(2,1)}, u32[]{:S(2)}, u32[]{:S(2)}) collective-permute-start(bf16[5120,256]{1,0:T(8,128)(2,1)S(1)} %pack_weights.1.w0), channel_id=1, source_target_pairs={{2,0},{0,2},{3,129},{129,3},{130,128},{128,130},{131,257},{257,131... | collective-permute-start | bytes 7864328 | tf_op jit(solution)/shard_map/ppermute | solution.py:276
  47.0 3.3 %row_halo.1 = bf16[512,512]{1,0:T(8,128)(2,1)S(1)} custom-call(s32[4]{0:T(128)S(1)} %pad_add_fusion.place, bf16[2,512,256]{2,1,0:T(8,128)(2,1)S(1)} %bitcast.20, bf16[2,512,256]{2,1,0:T(8,128)(2,1)S(1)} %bitcast.21, f32[4,1,256]{2,1,0:T(1,128)S(1)} %bitcast.26, bf16[3,4,256,256]{3,2,1,0:T(8,128)(2,1)S(1)} %broadcast_multiply_fusion.weight, ...), custom_call_target="tpu_custom_call" | custom-call | flops 1 | bytes 1 | tf_op jit(solution)/shard_map/row_halo/pallas_call | solution.py:145
  50.3 1.0 reshape.28
  51.3 11.3 %all-to-all-start = ((bf16[512,4,128]{2,1,0:T(4,128)(2,1)}), bf16[512,4,128]{2,1,0:T(4,128)(2,1)}, u32[]{:S(2)}, u32[]{:S(2)}) async-start(bf16[512,4,128]{2,1,0:T(4,128)(2,1)} %reshape.28), calls=%async_computation | async-start | bytes 1048576 | tf_op jit(solution)/shard_map/all_to_all | solution.py:280
  62.6 6.3 %collective-permute-start.3 = (bf16[5120,256]{1,0:T(8,128)(2,1)S(1)}, bf16[5120,256]{1,0:T(8,128)(2,1)}, u32[]{:S(2)}, u32[]{:S(2)}) collective-permute-start(bf16[5120,256]{1,0:T(8,128)(2,1)S(1)} %pack_weights.1.w0), channel_id=1, source_target_pairs={{0,1},{1,0},{2,3},{3,2},{4,5},{5,4},{6,7},{7,6},{8,9},{9,8},{10,11... | collective-permute-start | bytes 7864328 | tf_op jit(solution)/shard_map/ppermute | solution.py:278
  68.9 19.9 %all-to-all-done = bf16[512,4,128]{2,1,0:T(4,128)(2,1)} async-done(((bf16[512,4,128]{2,1,0:T(4,128)(2,1)}), bf16[512,4,128]{2,1,0:T(4,128)(2,1)}, u32[]{:S(2)}, u32[]{:S(2)}) %all-to-all-start) | async-done | bytes 524320 | tf_op jit(solution)/shard_map/all_to_all | solution.py:280
  88.8 4.9 %collective-permute-start.5 = (bf16[5120,256]{1,0:T(8,128)(2,1)}, bf16[5120,256]{1,0:T(8,128)(2,1)}, u32[]{:S(2)}, u32[]{:S(2)}) collective-permute-start(bf16[5120,256]{1,0:T(8,128)(2,1)} %collective-permute-done.4.w2), channel_id=1, source_target_pairs={{0,1},{1,0},{2,3},{3,2},{4,5},{5,4},{6,7},{7,6},{8,9},{9,8},{10,11... | collective-permute-start | bytes 7864328 | tf_op jit(solution)/shard_map/ppermute | solution.py:281
  93.7 1.2 reshape.29.moved
  95.0 3.4 %collective-permute-done.5.w3 = bf16[5120,256]{1,0:T(8,128)(2,1)} collective-permute-done((bf16[5120,256]{1,0:T(8,128)(2,1)}, bf16[5120,256]{1,0:T(8,128)(2,1)}, u32[]{:S(2)}, u32[]{:S(2)}) %collective-permute-start.5) | collective-permute-done | bytes 2621472 | tf_op jit(solution)/shard_map/ppermute | solution.py:281
  98.4 6.9 %col_layer.1 = bf16[4,128,256]{2,1,0:T(8,128)(2,1)S(1)} custom-call(s32[4]{0:T(128)S(1)} %pad_add_fusion.place, bf16[4,128,512]{2,1,0:T(8,128)(2,1)S(1)} %reshape.29.moved, f32[4,1,256]{2,1,0:T(1,128)S(1)} %bitcast.27, bf16[5120,256]{1,0:T(8,128)(2,1)S(1)} %pack_weights.1.w0, bf16[5120,256]{1,0:T(8,128)(2,1)} %collective-permute-done.3.w1, ...), custom_call_target="tpu_custom_call" | custom-call | flops 1 | bytes 1 | tf_op jit(solution)/shard_map/col_layer/pallas_call | solution.py:227
  105.3 28.4 %all_to_all.10 = bf16[512,2,128]{2,1,0:T(2,128)(2,1)S(1)} all-to-all(bf16[512,2,128]{2,1,0:T(2,128)(2,1)S(1)} %reshape.31), channel_id=1, replica_groups=mesh['yh'=4,'z'=8,'x'=4,'yl'=2,'c'=2] {'yl','c','yh','z','x'}, dimensions={0} | all-to-all | bytes 524288 | tf_op jit(solution)/shard_map/all_to_all | solution.py:288
  133.8 0.7 copy.11
  (21 shorter events, 0.7 us)
Async XLA Ops:
  0.0 17.2 %collective-permute-start = (bf16[512,256]{1,0:T(8,128)(2,1)}, bf16[512,256]{1,0:T(8,128)(2,1)S(1)}, u32[]{:S(2)}, u32[]{:S(2)}) collective-permute-start(bf16[512,256]{1,0:T(8,128)(2,1)} %source.1), channel_id=1, source_target_pairs={{0,4},{4,8},{8,12},{12,16},{16,20},{20,24},{24,28},{28,32},{32,36}... | collective-permute-start | bytes 786440 | tf_op jit(solution)/shard_map/ppermute | solution.py:263
  4.0 16.9 %collective-permute-start.1 = (bf16[512,256]{1,0:T(8,128)(2,1)}, bf16[512,256]{1,0:T(8,128)(2,1)}, u32[]{:S(2)}, u32[]{:S(2)}) collective-permute-start(bf16[512,256]{1,0:T(8,128)(2,1)} %source.1), channel_id=1, source_target_pairs={{0,2},{2,0},{1,3},{3,1},{4,6},{6,4},{5,7},{7,5},{8,10},{10,8},{9,1... | collective-permute-start | bytes 786440 | tf_op jit(solution)/shard_map/ppermute | solution.py:264
  12.1 1.4 %copy-start = (bf16[1024,3,256]{2,0,1:T(8,128)(2,1)S(1)}, bf16[1024,3,256]{2,0,1:T(8,128)(2,1)}, u32[]{:S(2)}) copy-start(bf16[1024,3,256]{2,0,1:T(8,128)(2,1)} %param.13) | copy-start | bytes 4718596
  13.5 1.0 copy-start.2
  14.6 1.0 copy-start.3
  15.6 1.4 %copy-start.6 = (bf16[1024,3,256]{2,0,1:T(8,128)(2,1)S(1)}, bf16[1024,3,256]{2,0,1:T(8,128)(2,1)}, u32[]{:S(2)}) copy-start(bf16[1024,3,256]{2,0,1:T(8,128)(2,1)} %param.10) | copy-start | bytes 4718596
  15.6 1.4 %copy-start.7 = (bf16[3]{0:T(256)(128)(2,1)S(1)}, bf16[3]{0:T(256)(128)(2,1)}, u32[]{:S(2)}) copy-start(bf16[3]{0:T(256)(128)(2,1)} %constant.30.clone) | copy-start | bytes 22
  17.2 8.5 %copy-start.4 = (f32[1024]{0:T(1024)S(1)}, f32[1024]{0:T(1024)}, u32[]{:S(2)}) copy-start(f32[1024]{0:T(1024)} %param.9) | copy-start | bytes 12292
  17.2 11.7 %collective-permute-start.2 = (bf16[512,256]{1,0:T(8,128)(2,1)S(1)}, bf16[512,256]{1,0:T(8,128)(2,1)S(1)}, u32[]{:S(2)}, u32[]{:S(2)}) collective-permute-start(bf16[512,256]{1,0:T(8,128)(2,1)S(1)} %collective-permute-done), channel_id=1, source_target_pairs={{0,2},{2,0},{1,3},{3,1},{4,6},{6,4},{5,7},{7,5},{8,10},{10,8},{9,1... | collective-permute-start | bytes 786440 | tf_op jit(solution)/shard_map/ppermute | solution.py:268
  25.7 21.2 %copy-start.1 = (bf16[512,256]{1,0:T(8,128)(2,1)S(1)}, bf16[512,256]{1,0:T(8,128)(2,1)}, u32[]{:S(2)}) copy-start(bf16[512,256]{1,0:T(8,128)(2,1)} %source.1) | copy-start | bytes 786436
  31.1 57.7 %collective-permute-start.4 = (bf16[5120,256]{1,0:T(8,128)(2,1)S(1)}, bf16[5120,256]{1,0:T(8,128)(2,1)}, u32[]{:S(2)}, u32[]{:S(2)}) collective-permute-start(bf16[5120,256]{1,0:T(8,128)(2,1)S(1)} %pack_weights.1.w0), channel_id=1, source_target_pairs={{2,0},{0,2},{3,129},{129,3},{130,128},{128,130},{131,257},{257,131... | collective-permute-start | bytes 7864328 | tf_op jit(solution)/shard_map/ppermute | solution.py:276
  50.3 48.0 %copy-start.5 = (f32[1024]{0:T(1024)S(1)}, f32[1024]{0:T(1024)}, u32[]{:S(2)}) copy-start(f32[1024]{0:T(1024)} %param.12) | copy-start | bytes 12292
  51.3 37.5 %all-to-all-start = ((bf16[512,4,128]{2,1,0:T(4,128)(2,1)}), bf16[512,4,128]{2,1,0:T(4,128)(2,1)}, u32[]{:S(2)}, u32[]{:S(2)}) async-start(bf16[512,4,128]{2,1,0:T(4,128)(2,1)} %reshape.28), calls=%async_computation | async-start | bytes 1048576 | tf_op jit(solution)/shard_map/all_to_all | solution.py:280
  62.6 32.3 %collective-permute-start.3 = (bf16[5120,256]{1,0:T(8,128)(2,1)S(1)}, bf16[5120,256]{1,0:T(8,128)(2,1)}, u32[]{:S(2)}, u32[]{:S(2)}) collective-permute-start(bf16[5120,256]{1,0:T(8,128)(2,1)S(1)} %pack_weights.1.w0), channel_id=1, source_target_pairs={{0,1},{1,0},{2,3},{3,2},{4,5},{5,4},{6,7},{7,6},{8,9},{9,8},{10,11... | collective-permute-start | bytes 7864328 | tf_op jit(solution)/shard_map/ppermute | solution.py:278
  88.8 9.6 %collective-permute-start.5 = (bf16[5120,256]{1,0:T(8,128)(2,1)}, bf16[5120,256]{1,0:T(8,128)(2,1)}, u32[]{:S(2)}, u32[]{:S(2)}) collective-permute-start(bf16[5120,256]{1,0:T(8,128)(2,1)} %collective-permute-done.4.w2), channel_id=1, source_target_pairs={{0,1},{1,0},{2,3},{3,2},{4,5},{5,4},{6,7},{7,6},{8,9},{9,8},{10,11... | collective-permute-start | bytes 7864328 | tf_op jit(solution)/shard_map/ppermute | solution.py:281

commit v7 on v6

--- a/solution.py
+++ b/solution.py
@@ -156,70 +156,71 @@
     )(place, near, far, gain, weight, *state, source)
 
 
-QKV_AT, OUT_AT, WEIGHT_ROWS = 1024, 4096, 5120
-
-
-def pack_kernel(row_out, col_qkv, col_out, packed, sem):
-    pairs = [(col_qkv, packed.at[QKV_AT:OUT_AT])]
-    for source, at in ((row_out, 0), (col_out, OUT_AT)):
+QKV_ROWS, OUT_ROWS = 3072, 1024
+
+
+def pack_kernel(row_out, col_out, col_qkv, outs, everything, sem):
+    copies = [(col_qkv, everything.at[2 * OUT_ROWS :])]
+    for i, source in enumerate((row_out, col_out)):
         for n in range(PARTS):
-            rows = slice(at + n * GROUP, at + (n + 1) * GROUP)
-            pairs.append((source.at[:, n * GROUP : (n + 1) * GROUP], packed.at[rows]))
-    copies = [pltpu.make_async_copy(a, b, sem.at[i]) for i, (a, b) in enumerate(pairs)]
+            rows = slice(i * OUT_ROWS + n * GROUP, i * OUT_ROWS + (n + 1) * GROUP)
+            part = source.at[:, n * GROUP : (n + 1) * GROUP]
+            copies += [(part, outs.at[rows]), (part, everything.at[rows])]
+    copies = [pltpu.make_async_copy(a, b, sem.at[i]) for i, (a, b) in enumerate(copies)]
     for copy in copies:
         copy.start()
     for copy in copies:
         copy.wait()
 
 
-def pack_weights(row_out, col_qkv, col_out):
+def pack_weights(row_out, col_out, col_qkv):
     return pl.pallas_call(
         pack_kernel,
-        out_shape=jax.ShapeDtypeStruct((WEIGHT_ROWS, GROUP), jnp.bfloat16),
+        out_shape=(
+            jax.ShapeDtypeStruct((2 * OUT_ROWS, GROUP), jnp.bfloat16),
+            jax.ShapeDtypeStruct((2 * OUT_ROWS + QKV_ROWS, GROUP), jnp.bfloat16),
+        ),
         in_specs=[ANY] * 3,
-        out_specs=ANY,
-        scratch_shapes=[pltpu.SemaphoreType.DMA((2 * PARTS + 1,))],
+        out_specs=(ANY, ANY),
+        scratch_shapes=[pltpu.SemaphoreType.DMA((4 * PARTS + 1,))],
         compiler_params=pltpu.CompilerParams(vmem_limit_bytes=MIB),
         cost_estimate=pl.CostEstimate(flops=1, bytes_accessed=1, transcendentals=0),
         name="pack_weights",
-    )(row_out, col_qkv, col_out)
-
-
-def col_layer_kernel(place, moved, gain, w0, w1, w2, w3, out, held, sem):
-    arrays = (w0, w1, w2, w3)
+    )(row_out, col_out, col_qkv)
+
+
+def col_layer_kernel(place, moved, gain, qkv0, out0, both1, qkv2, out2, qkv3, out3, out, qkv, outs, sem):
+    pairs = [(a, outs.at[i]) for i, a in enumerate((out0, both1.at[: 2 * OUT_ROWS], out2, out3))]
+    pairs += [(a, qkv.at[i]) for i, a in enumerate((qkv0, both1.at[2 * OUT_ROWS :], qkv2, qkv3))]
+    copies = [pltpu.make_async_copy(a, b, sem.at[i]) for i, (a, b) in enumerate(pairs)]
+    for copy in copies:
+        copy.start()
     groups = [place[0] + place[3], place[0] + 1 - place[3], place[1] + place[3], place[1] + 1 - place[3]]
-    first = [pltpu.make_async_copy(w.at[:QKV_AT], held.at[i, :QKV_AT], sem.at[0, i]) for i, w in enumerate(arrays)]
-    rest = [pltpu.make_async_copy(w.at[QKV_AT:], held.at[i, QKV_AT:], sem.at[1, i]) for i, w in enumerate(arrays)]
-    for copy in first + rest:
-        copy.start()
 
     def add_projected(pieces, atts, at):
         result = []
         for n in range(PARTS):
             rows = slice(at + n * GROUP, at + (n + 1) * GROUP)
-            total = sum(dot(a, held[i, rows, :]) for i, a in enumerate(atts))
+            total = sum(dot(a, outs[i, rows, :]) for i, a in enumerate(atts))
             result.append((pieces[n].astype(jnp.float32) + total).astype(jnp.bfloat16))
         return result
 
     atts = [moved[g, :, :GROUP] for g in groups]
-    for copy in first:
+    for copy in copies[:PARTS]:
         copy.wait()
     pieces = add_projected([moved[n, :, GROUP:] for n in range(PARTS)], atts, 0)
     normed = normed_pieces(pieces, [gain[n] for n in range(PARTS)])
     normed = jnp.concatenate(normed, axis=1)
     row, col = triangle(normed.shape[0])
     atts = []
-    for i, copy in enumerate(rest):
+    for i, copy in enumerate(copies[PARTS:]):
         copy.wait()
-        q, k, v = [
-            dot(normed, held[i, QKV_AT + j * 1024 : QKV_AT + (j + 1) * 1024, :]).astype(jnp.bfloat16)
-            for j in range(3)
-        ]
+        q, k, v = [dot(normed, qkv[i, j * 1024 : (j + 1) * 1024, :]).astype(jnp.bfloat16) for j in range(3)]
         _, norm, acc = attend_blocks(
             q * jnp.bfloat16(SCALE), [k], [v], [lambda s: jnp.where(col <= row, s, -1e30)]
         )
         atts.append((acc / norm).astype(jnp.bfloat16))
-    for n, piece in enumerate(add_projected(pieces, atts, OUT_AT)):
+    for n, piece in enumerate(add_projected(pieces, atts, OUT_ROWS)):
         out[n] = piece
 
 
@@ -227,9 +228,13 @@
     return pl.pallas_call(
         col_layer_kernel,
         out_shape=jax.ShapeDtypeStruct((PARTS, 128, GROUP), jnp.bfloat16),
-        in_specs=[SMEM, VMEM, VMEM] + [ANY] * 4,
+        in_specs=[SMEM, VMEM, VMEM] + [ANY] * 7,
         out_specs=VMEM,
-        scratch_shapes=[pltpu.VMEM((PARTS, WEIGHT_ROWS, GROUP), jnp.bfloat16), pltpu.SemaphoreType.DMA((2, PARTS))],
+        scratch_shapes=[
+            pltpu.VMEM((PARTS, QKV_ROWS, GROUP), jnp.bfloat16),
+            pltpu.VMEM((PARTS, 2 * OUT_ROWS, GROUP), jnp.bfloat16),
+            pltpu.SemaphoreType.DMA((2 * PARTS,)),
+        ],
         compiler_params=pltpu.CompilerParams(vmem_limit_bytes=20 * MIB),
         cost_estimate=pl.CostEstimate(flops=1, bytes_accessed=1, transcendentals=0),
         name="col_layer",
@@ -243,12 +248,12 @@
     return lax.optimization_barrier((value, *others))[0]
 
 
-def cross_route(outer):
+def cross_route():
     route = []
     for yh in range(4):
         for core in range(2):
             a = yh * 4 + 2 + core
-            b = ((yh + 1) % 4 if core in outer else yh) * 4 + core
+            b = ((yh + 1) % 4 if core == 1 else yh) * 4 + core
             route += [(a, b), (b, a)]
     return route
 
@@ -260,11 +265,14 @@
     row_qkv = row_qkv.transpose(1, 0, 2).reshape(3, PARTS, GROUP, GROUP)
     row_qkv = row_qkv * jnp.array([SCALE, 1, 1], jnp.bfloat16)[:, None, None, None]
 
+    col_qkv = col_qkv.transpose(1, 0, 2).reshape(QKV_ROWS, GROUP)
+    qkv_theirs = lax.ppermute(col_qkv, ("yh", "yl", "c"), cross_route())
+
     before = lax.ppermute(inputs, SEQ, [(i, i + 1) for i in range(127)])
     other = lax.ppermute(inputs, "yl", SWAP)
     near = lax.all_gather(inputs, "c", axis=0)
-    mine = pack_weights(row_out, col_qkv.transpose(1, 0, 2).reshape(3 * 1024, GROUP), col_out)
-    mine, row_qkv, before = lax.optimization_barrier((mine, row_qkv, before, near))[:3]
+    outs, mine = pack_weights(row_out, col_out, col_qkv)
+    outs, mine, row_qkv, before = lax.optimization_barrier((outs, mine, row_qkv, before, near))[:4]
     before_other = lax.ppermute(before, "yl", SWAP)
     far = lax.all_gather(after(other, before), "c", axis=0)
     before_near = lax.all_gather(after(before, far), "c", axis=0)
@@ -272,18 +280,18 @@
     state = row_own(place, near, far, row_gain, row_qkv)
     before_far = lax.all_gather(after(before_other, state[0]), "c", axis=0)
 
-    mine = after(mine, before_far)
-    theirs = lax.ppermute(mine, ("yh", "yl", "c"), cross_route((1,)))
+    outs_theirs = lax.ppermute(after(outs, before_far), ("yh", "yl", "c"), cross_route())
     sent = row_halo(place, before_near, before_far, row_gain, row_qkv, state, inputs)
     mine_swapped = lax.ppermute(after(mine, sent), "c", SWAP)
+    qkv_swapped = lax.ppermute(after(qkv_theirs, sent), "c", SWAP)
 
     moved = lax.all_to_all(sent.reshape(COLS, 4, 128), HEAD + SEQ, 0, 0, tiled=True)
-    theirs_swapped = lax.ppermute(after(theirs, moved), "c", SWAP)
+    outs_swapped = lax.ppermute(after(outs_theirs, moved), "c", SWAP)
     mixed = col_layer(
         place,
         moved.reshape(PARTS, 128, 2 * GROUP),
         col_gain.reshape(PARTS, 1, GROUP),
-        [mine, mine_swapped, theirs, theirs_swapped],
+        [col_qkv, outs, mine_swapped, qkv_theirs, outs_theirs, qkv_swapped, outs_swapped],
     )
     mixed = lax.all_to_all(mixed.reshape(COLS, 2, 128), HEAD + SEQ, 0, 0, tiled=True)
     return mixed.reshape(COLS, GROUP)

time: 135 us -> 141 us (1.044)
  waiting for transfers between devices: 23.3 us -> 17.7 us
  starting transfers between devices: 49.2 us -> 54.3 us
  blocking collectives: 40.4 us -> 45.3 us
  Pallas kernels: 13.7 us -> 15.5 us
  other arithmetic: 0.25 us -> 1.81 us
  local copies, waits for them, and re-layouts: 7.48 us -> 5.99 us
    all_to_all x1, starting transfers between devices: 11.3 us -> 22.7 us  [on_device(): lax.all_to_all(sent.reshape(COLS, 4, 128), HEAD + SEQ, 0, 0, tiled=True)]
    all_gather x1, blocking collectives: 2.18 us -> 10.3 us  [on_device(): before_far = lax.all_gather(after(before_other, state[0]), 'c', axis=0)]
    all_to_all x1, waiting for transfers between devices: 19.9 us -> 15.9 us  [on_device(): lax.all_to_all(sent.reshape(COLS, 4, 128), HEAD + SEQ, 0, 0, tiled=True)]
    ppermute x1, starting transfers between devices: 6.28 us -> 2.4 us  [on_device(): mine_swapped = lax.ppermute(after(mine, sent), 'c', SWAP)]
    all_to_all x1, blocking collectives: 28.4 us -> 25.7 us  [on_device(): lax.all_to_all(mixed.reshape(COLS, 2, 128), HEAD + SEQ, 0, 0, tiled=True)]
    unnamed x17, local copies, waits for them, and re-layouts: 5.22 us -> 2.72 us
    ppermute x2 -> x4, waiting for transfers between devices: 3.42 us -> 0.98 us  [the longest x1 0.97 us: on_device(): outs_swapped = lax.ppermute(after(outs_theirs, moved), 'c', SWAP)]
    ppermute x1, starting transfers between devices: 3.64 us -> 1.91 us  [on_device(): before_other = lax.ppermute(before, 'yl', SWAP)]
  transfers between devices with their start and end apart: 7 -> 9, of which waited for: 2 -> 3; matrix products, arithmetic and copies ran while one was open for 2% -> 4% of each run, Pallas kernels for 5% -> 6%
where the time goes in v7:
time: 141 us
  starting transfers between devices  54.3 us (39%)
  blocking collectives  45.3 us (32%)
  waiting for transfers between devices  17.7 us (13%)
  Pallas kernels  15.5 us (11%)
  local copies, waits for them, and re-layouts  5.99 us (4%)
  other arithmetic  1.81 us (1%)
    all_to_all x1, blocking collectives, on_device(): lax.all_to_all(mixed.reshape(COLS, 2, 128), HEAD + SEQ, 0, 0, tiled=True)  25.7 us
    all_to_all x1, starting transfers between devices, on_device(): lax.all_to_all(sent.reshape(COLS, 4, 128), HEAD + SEQ, 0, 0, tiled=True)  22.7 us
    all_to_all x1, waiting for transfers between devices, on_device(): lax.all_to_all(sent.reshape(COLS, 4, 128), HEAD + SEQ, 0, 0, tiled=True)  15.9 us
    all_gather x1, blocking collectives, on_device(): before_far = lax.all_gather(after(before_other, state[0]), 'c', axis=0)  10.3 us
    pallas_call x1, Pallas kernels, col_layer(): pl.pallas_call(col_layer_kernel, out_shape=jax.ShapeDtypeStruct((PARTS, 1...  7.35 us
    ppermute x1, starting transfers between devices, on_device(): qkv_swapped = lax.ppermute(after(qkv_theirs, sent), 'c', SWAP)  6.21 us
    ppermute x1, starting transfers between devices, on_device(): lax.ppermute(after(outs, before_far), ('yh', 'yl', 'c'), cross_route())  5.57 us
    ppermute x1, starting transfers between devices, on_device(): before = lax.ppermute(inputs, SEQ, [(i, i + 1) for i in range(127)])  4.66 us
  transfers between devices with their start and end apart: 9, of which 3 were waited for; matrix products, arithmetic and copies ran while one was open for 4% of the time, Pallas kernels for 6%

profile of v7, /device:TPU:1, one launch (start us, length us, event | category | flops | bytes accessed | tf_op | source)
XLA Modules:
  0.0 140.7 jit_solution(8243933128987951923)
XLA Ops:
  0.0 4.7 %collective-permute-start = (bf16[512,256]{1,0:T(8,128)(2,1)}, bf16[512,256]{1,0:T(8,128)(2,1)}, u32[]{:S(2)}, u32[]{:S(2)}) collective-permute-start(bf16[512,256]{1,0:T(8,128)(2,1)} %source.1), channel_id=1, source_target_pairs={{0,4},{4,8},{8,12},{12,16},{16,20},{20,24},{24,28},{28,32},{32,36}... | collective-permute-start | bytes 786440 | tf_op jit(solution)/shard_map/ppermute | solution.py:271
  4.7 3.2 %collective-permute-start.1 = (bf16[512,256]{1,0:T(8,128)(2,1)}, bf16[512,256]{1,0:T(8,128)(2,1)}, u32[]{:S(2)}, u32[]{:S(2)}) collective-permute-start(bf16[512,256]{1,0:T(8,128)(2,1)} %source.1), channel_id=1, source_target_pairs={{0,2},{2,0},{1,3},{3,1},{4,6},{6,4},{5,7},{7,5},{8,10},{10,8},{9,1... | collective-permute-start | bytes 786440 | tf_op jit(solution)/shard_map/ppermute | solution.py:272
  7.9 4.2 %collective-permute-start.4 = (bf16[3072,256]{1,0:T(8,128)(2,1)}, bf16[3072,256]{1,0:T(8,128)(2,1)}, u32[]{:S(2)}, u32[]{:S(2)}) collective-permute-start(bf16[3072,256]{1,0:T(8,128)(2,1)} %bitcast.20), channel_id=1, source_target_pairs={{2,0},{0,2},{3,129},{129,3},{130,128},{128,130},{131,257},{257,131... | collective-permute-start | bytes 4718600 | tf_op jit(solution)/shard_map/ppermute | solution.py:269
  12.1 1.7 %broadcast_multiply_fusion.weight = bf16[3,4,256,256]{3,2,1,0:T(8,128)(2,1)S(1)} fusion(bf16[3,4,256,256]{3,2,1,0:T(8,128)(2,1)} %bitcast.30, bf16[3]{0:T(256)(128)(2,1)} %constant.30.clone), kind=kLoop, calls=%fused_computation | loop fusion | flops 786432 | bytes 3145734 | tf_op jit(solution)/shard_map/mul | solution.py:266
  14.2 1.9 %pack_weights.1 = (bf16[2048,256]{1,0:T(8,128)(2,1)}, bf16[5120,256]{1,0:T(8,128)(2,1)}) custom-call(bf16[256,1024]{1,0:T(8,128)(2,1)S(1)} %copy-done.3, bf16[256,1024]{1,0:T(8,128)(2,1)S(1)} %copy-done.4, bf16[3072,256]{1,0:T(8,128)(2,1)S(1)} %bitcast.21), custom_call_target="tpu_custom_call" | custom-call | flops 1 | bytes 1 | tf_op jit(solution)/shard_map/pack_weights/pallas_call | solution.py:177
  16.2 4.5 %all-gather = bf16[1024,256]{1,0:T(8,128)(2,1)S(1)} all-gather(bf16[512,256]{1,0:T(8,128)(2,1)S(1)} %copy-done.2), channel_id=2, replica_groups=mesh['yh'=4,'z'=8,'x'=4,'yl'=2,'c'=2] {'c'}, dimensions={0}, use_global_device_ids=true | all-gather | bytes 786432 | tf_op jit(solution)/shard_map/all_gather | solution.py:273
  20.7 1.9 %collective-permute-start.2 = (bf16[512,256]{1,0:T(8,128)(2,1)}, bf16[512,256]{1,0:T(8,128)(2,1)S(1)}, u32[]{:S(2)}, u32[]{:S(2)}) collective-permute-start(bf16[512,256]{1,0:T(8,128)(2,1)} %collective-permute-done), channel_id=1, source_target_pairs={{0,2},{2,0},{1,3},{3,1},{4,6},{6,4},{5,7},{7,5},{8,10},{10,8},{9,1... | collective-permute-start | bytes 786440 | tf_op jit(solution)/shard_map/ppermute | solution.py:276
  22.7 2.4 %all-gather.1 = bf16[1024,256]{1,0:T(8,128)(2,1)S(1)} all-gather(bf16[512,256]{1,0:T(8,128)(2,1)} %collective-permute-done.1), channel_id=3, replica_groups=mesh['yh'=4,'z'=8,'x'=4,'yl'=2,'c'=2] {'c'}, dimensions={0}, use_global_device_ids=true | all-gather | bytes 786432 | tf_op jit(solution)/shard_map/all_gather | solution.py:277
  25.1 2.4 %all-gather.2 = bf16[1024,256]{1,0:T(8,128)(2,1)S(1)} all-gather(bf16[512,256]{1,0:T(8,128)(2,1)} %collective-permute-done), channel_id=4, replica_groups=mesh['yh'=4,'z'=8,'x'=4,'yl'=2,'c'=2] {'c'}, dimensions={0}, use_global_device_ids=true | all-gather | bytes 786432 | tf_op jit(solution)/shard_map/all_gather | solution.py:278
  27.4 3.1 %row_own.1 = (bf16[512,256]{1,0:T(8,128)(2,1)S(1)}, f32[512,256]{1,0:T(8,128)S(1)}, f32[512,256]{1,0:T(8,128)S(1)}, f32[512,256]{1,0:T(8,128)S(1)}) custom-call(s32[4]{0:T(128)S(1)} %pad_add_fusion.place, bf16[2,512,256]{2,1,0:T(8,128)(2,1)S(1)} %bitcast.25, bf16[2,512,256]{2,1,0:T(8,128)(2,1)S(1)} %bitcast.26, f32[4,1,256]{2,1,0:T(1,128)S(1)} %bitcast.27, ...), custom_call_target="tpu_custom_call" | custom-call | flops 1 | bytes 1 | tf_op jit(solution)/shard_map/row_own/pallas_call | solution.py:102
  30.5 0.8 collective-permute-done.2
  31.3 10.3 %all-gather.3 = bf16[1024,256]{1,0:T(8,128)(2,1)S(1)} all-gather(bf16[512,256]{1,0:T(8,128)(2,1)S(1)} %collective-permute-done.2), channel_id=5, replica_groups=mesh['yh'=4,'z'=8,'x'=4,'yl'=2,'c'=2] {'c'}, dimensions={0}, use_global_device_ids=true | all-gather | bytes 786432 | tf_op jit(solution)/shard_map/all_gather | solution.py:281
  41.6 3.2 %row_halo.1 = bf16[512,512]{1,0:T(8,128)(2,1)S(1)} custom-call(s32[4]{0:T(128)S(1)} %pad_add_fusion.place, bf16[2,512,256]{2,1,0:T(8,128)(2,1)S(1)} %bitcast.23, bf16[2,512,256]{2,1,0:T(8,128)(2,1)S(1)} %bitcast.24, f32[4,1,256]{2,1,0:T(1,128)S(1)} %bitcast.28, bf16[3,4,256,256]{3,2,1,0:T(8,128)(2,1)S(1)} %broadcast_multiply_fusion.weight, ...), custom_call_target="tpu_custom_call" | custom-call | flops 1 | bytes 1 | tf_op jit(solution)/shard_map/row_halo/pallas_call | solution.py:145
  45.6 2.4 %collective-permute-start.3 = (bf16[5120,256]{1,0:T(8,128)(2,1)}, bf16[5120,256]{1,0:T(8,128)(2,1)}, u32[]{:S(2)}, u32[]{:S(2)}) collective-permute-start(bf16[5120,256]{1,0:T(8,128)(2,1)} %get-tuple-element.37), channel_id=1, source_target_pairs={{0,1},{1,0},{2,3},{3,2},{4,5},{5,4},{6,7},{7,6},{8,9},{9,8},{10,11... | collective-permute-start | bytes 7864328 | tf_op jit(solution)/shard_map/ppermute | solution.py:285
  48.0 5.6 %collective-permute-start.5 = (bf16[2048,256]{1,0:T(8,128)(2,1)}, bf16[2048,256]{1,0:T(8,128)(2,1)S(1)}, u32[]{:S(2)}, u32[]{:S(2)}) collective-permute-start(bf16[2048,256]{1,0:T(8,128)(2,1)} %get-tuple-element.38.out0), channel_id=1, source_target_pairs={{2,0},{0,2},{3,129},{129,3},{130,128},{128,130},{131,257},{257,131... | collective-permute-start | bytes 3145736 | tf_op jit(solution)/shard_map/ppermute | solution.py:283
  53.6 2.0 %reshape.28 = bf16[512,4,128]{2,1,0:T(4,128)(2,1)} reshape(bf16[512,512]{1,0:T(8,128)(2,1)} %copy-done.1) | data formatting | bytes 1048576 | tf_op jit(solution)/shard_map/reshape | solution.py:288
  55.5 22.7 %all-to-all-start = ((bf16[512,4,128]{2,1,0:T(4,128)(2,1)}), bf16[512,4,128]{2,1,0:T(4,128)(2,1)S(1)}, u32[]{:S(2)}, u32[]{:S(2)}) async-start(bf16[512,4,128]{2,1,0:T(4,128)(2,1)} %reshape.28), calls=%async_computation | async-start | bytes 1048576 | tf_op jit(solution)/shard_map/all_to_all | solution.py:288
  78.2 6.2 %collective-permute-start.6 = (bf16[3072,256]{1,0:T(8,128)(2,1)}, bf16[3072,256]{1,0:T(8,128)(2,1)}, u32[]{:S(2)}, u32[]{:S(2)}) collective-permute-start(bf16[3072,256]{1,0:T(8,128)(2,1)} %collective-permute-done.4.qkv2), channel_id=1, source_target_pairs={{0,1},{1,0},{2,3},{3,2},{4,5},{5,4},{6,7},{7,6},{8,9},{9,8},{10,11... | collective-permute-start | bytes 4718600 | tf_op jit(solution)/shard_map/ppermute | solution.py:286
  84.5 15.9 %all-to-all-done = bf16[512,4,128]{2,1,0:T(4,128)(2,1)S(1)} async-done(((bf16[512,4,128]{2,1,0:T(4,128)(2,1)}), bf16[512,4,128]{2,1,0:T(4,128)(2,1)S(1)}, u32[]{:S(2)}, u32[]{:S(2)}) %all-to-all-start) | async-done | bytes 524320 | tf_op jit(solution)/shard_map/all_to_all | solution.py:288
  101.1 3.5 %collective-permute-start.7 = (bf16[2048,256]{1,0:T(8,128)(2,1)S(1)}, bf16[2048,256]{1,0:T(8,128)(2,1)}, u32[]{:S(2)}, u32[]{:S(2)}) collective-permute-start(bf16[2048,256]{1,0:T(8,128)(2,1)S(1)} %collective-permute-done.5.out2), channel_id=1, source_target_pairs={{0,1},{1,0},{2,3},{3,2},{4,5},{5,4},{6,7},{7,6},{8,9},{9,8},{10,11... | collective-permute-start | bytes 3145736 | tf_op jit(solution)/shard_map/ppermute | solution.py:289
  104.6 1.2 reshape.29.moved
  105.9 1.0 collective-permute-done.7.out3
  106.8 7.3 %col_layer.1 = bf16[4,128,256]{2,1,0:T(8,128)(2,1)S(1)} custom-call(s32[4]{0:T(128)S(1)} %pad_add_fusion.place, bf16[4,128,512]{2,1,0:T(8,128)(2,1)S(1)} %reshape.29.moved, f32[4,1,256]{2,1,0:T(1,128)S(1)} %bitcast.29, bf16[3072,256]{1,0:T(8,128)(2,1)S(1)} %bitcast.22, bf16[2048,256]{1,0:T(8,128)(2,1)} %get-tuple-element.38.out0, ...), custom_call_target="tpu_custom_call" | custom-call | flops 1 | bytes 1 | tf_op jit(solution)/shard_map/col_layer/pallas_call | solution.py:228
  114.3 25.7 %all_to_all.10 = bf16[512,2,128]{2,1,0:T(2,128)(2,1)S(1)} all-to-all(bf16[512,2,128]{2,1,0:T(2,128)(2,1)S(1)} %reshape.31), channel_id=1, replica_groups=mesh['yh'=4,'z'=8,'x'=4,'yl'=2,'c'=2] {'yl','c','yh','z','x'}, dimensions={0} | all-to-all | bytes 524288 | tf_op jit(solution)/shard_map/all_to_all | solution.py:296
  (25 shorter events, 2.9 us)
Async XLA Ops:
  0.0 20.7 %collective-permute-start = (bf16[512,256]{1,0:T(8,128)(2,1)}, bf16[512,256]{1,0:T(8,128)(2,1)}, u32[]{:S(2)}, u32[]{:S(2)}) collective-permute-start(bf16[512,256]{1,0:T(8,128)(2,1)} %source.1), channel_id=1, source_target_pairs={{0,4},{4,8},{8,12},{12,16},{16,20},{20,24},{24,28},{28,32},{32,36}... | collective-permute-start | bytes 786440 | tf_op jit(solution)/shard_map/ppermute | solution.py:271
  4.7 18.0 %collective-permute-start.1 = (bf16[512,256]{1,0:T(8,128)(2,1)}, bf16[512,256]{1,0:T(8,128)(2,1)}, u32[]{:S(2)}, u32[]{:S(2)}) collective-permute-start(bf16[512,256]{1,0:T(8,128)(2,1)} %source.1), channel_id=1, source_target_pairs={{0,2},{2,0},{1,3},{3,1},{4,6},{6,4},{5,7},{7,5},{8,10},{10,8},{9,1... | collective-permute-start | bytes 786440 | tf_op jit(solution)/shard_map/ppermute | solution.py:272
  7.9 70.4 %collective-permute-start.4 = (bf16[3072,256]{1,0:T(8,128)(2,1)}, bf16[3072,256]{1,0:T(8,128)(2,1)}, u32[]{:S(2)}, u32[]{:S(2)}) collective-permute-start(bf16[3072,256]{1,0:T(8,128)(2,1)} %bitcast.20), channel_id=1, source_target_pairs={{2,0},{0,2},{3,129},{129,3},{130,128},{128,130},{131,257},{257,131... | collective-permute-start | bytes 4718600 | tf_op jit(solution)/shard_map/ppermute | solution.py:269
  12.0 1.9 %copy-start = (bf16[1024,3,256]{2,0,1:T(8,128)(2,1)S(1)}, bf16[1024,3,256]{2,0,1:T(8,128)(2,1)}, u32[]{:S(2)}) copy-start(bf16[1024,3,256]{2,0,1:T(8,128)(2,1)} %param.13) | copy-start | bytes 4718596
  12.1 2.0 %copy-start.3 = (bf16[256,1024]{1,0:T(8,128)(2,1)S(1)}, bf16[256,1024]{1,0:T(8,128)(2,1)}, u32[]{:S(2)}) copy-start(bf16[256,1024]{1,0:T(8,128)(2,1)} %row_out.1) | copy-start | bytes 1572868
  12.1 2.1 %copy-start.4 = (bf16[256,1024]{1,0:T(8,128)(2,1)S(1)}, bf16[256,1024]{1,0:T(8,128)(2,1)}, u32[]{:S(2)}) copy-start(bf16[256,1024]{1,0:T(8,128)(2,1)} %col_out.1) | copy-start | bytes 1572868
  14.2 2.0 %copy-start.2 = (bf16[512,256]{1,0:T(8,128)(2,1)S(1)}, bf16[512,256]{1,0:T(8,128)(2,1)}, u32[]{:S(2)}) copy-start(bf16[512,256]{1,0:T(8,128)(2,1)} %source.1) | copy-start | bytes 786436
  16.1 11.3 %copy-start.5 = (f32[1024]{0:T(1024)S(1)}, f32[1024]{0:T(1024)}, u32[]{:S(2)}) copy-start(f32[1024]{0:T(1024)} %param.9) | copy-start | bytes 12292
  20.7 10.6 %collective-permute-start.2 = (bf16[512,256]{1,0:T(8,128)(2,1)}, bf16[512,256]{1,0:T(8,128)(2,1)S(1)}, u32[]{:S(2)}, u32[]{:S(2)}) collective-permute-start(bf16[512,256]{1,0:T(8,128)(2,1)} %collective-permute-done), channel_id=1, source_target_pairs={{0,2},{2,0},{1,3},{3,1},{4,6},{6,4},{5,7},{7,5},{8,10},{10,8},{9,1... | collective-permute-start | bytes 786440 | tf_op jit(solution)/shard_map/ppermute | solution.py:276
  44.8 0.8 copy-start.1
  45.6 61.3 %copy-start.6 = (f32[1024]{0:T(1024)S(1)}, f32[1024]{0:T(1024)}, u32[]{:S(2)}) copy-start(f32[1024]{0:T(1024)} %param.12) | copy-start | bytes 12292
  45.6 61.2 %collective-permute-start.3 = (bf16[5120,256]{1,0:T(8,128)(2,1)}, bf16[5120,256]{1,0:T(8,128)(2,1)}, u32[]{:S(2)}, u32[]{:S(2)}) collective-permute-start(bf16[5120,256]{1,0:T(8,128)(2,1)} %get-tuple-element.37), channel_id=1, source_target_pairs={{0,1},{1,0},{2,3},{3,2},{4,5},{5,4},{6,7},{7,6},{8,9},{9,8},{10,11... | collective-permute-start | bytes 7864328 | tf_op jit(solution)/shard_map/ppermute | solution.py:285
  48.0 52.3 %collective-permute-start.5 = (bf16[2048,256]{1,0:T(8,128)(2,1)}, bf16[2048,256]{1,0:T(8,128)(2,1)S(1)}, u32[]{:S(2)}, u32[]{:S(2)}) collective-permute-start(bf16[2048,256]{1,0:T(8,128)(2,1)} %get-tuple-element.38.out0), channel_id=1, source_target_pairs={{2,0},{0,2},{3,129},{129,3},{130,128},{128,130},{131,257},{257,131... | collective-permute-start | bytes 3145736 | tf_op jit(solution)/shard_map/ppermute | solution.py:283
  55.5 44.8 %all-to-all-start = ((bf16[512,4,128]{2,1,0:T(4,128)(2,1)}), bf16[512,4,128]{2,1,0:T(4,128)(2,1)S(1)}, u32[]{:S(2)}, u32[]{:S(2)}) async-start(bf16[512,4,128]{2,1,0:T(4,128)(2,1)} %reshape.28), calls=%async_computation | async-start | bytes 1048576 | tf_op jit(solution)/shard_map/all_to_all | solution.py:288
  78.2 28.6 %collective-permute-start.6 = (bf16[3072,256]{1,0:T(8,128)(2,1)}, bf16[3072,256]{1,0:T(8,128)(2,1)}, u32[]{:S(2)}, u32[]{:S(2)}) collective-permute-start(bf16[3072,256]{1,0:T(8,128)(2,1)} %collective-permute-done.4.qkv2), channel_id=1, source_target_pairs={{0,1},{1,0},{2,3},{3,2},{4,5},{5,4},{6,7},{7,6},{8,9},{9,8},{10,11... | collective-permute-start | bytes 4718600 | tf_op jit(solution)/shard_map/ppermute | solution.py:286
  100.3 0.8 copy-start.7
  101.1 5.7 %collective-permute-start.7 = (bf16[2048,256]{1,0:T(8,128)(2,1)S(1)}, bf16[2048,256]{1,0:T(8,128)(2,1)}, u32[]{:S(2)}, u32[]{:S(2)}) collective-permute-start(bf16[2048,256]{1,0:T(8,128)(2,1)S(1)} %collective-permute-done.5.out2), channel_id=1, source_target_pairs={{0,1},{1,0},{2,3},{3,2},{4,5},{5,4},{6,7},{7,6},{8,9},{9,8},{10,11... | collective-permute-start | bytes 3145736 | tf_op jit(solution)/shard_map/ppermute | solution.py:289

commit v8 on v6

--- a/solution.py
+++ b/solution.py
@@ -264,13 +264,13 @@
     other = lax.ppermute(inputs, "yl", SWAP)
     near = lax.all_gather(inputs, "c", axis=0)
     mine = pack_weights(row_out, col_qkv.transpose(1, 0, 2).reshape(3 * 1024, GROUP), col_out)
-    mine, row_qkv, before = lax.optimization_barrier((mine, row_qkv, before, near))[:3]
+    mine, row_qkv, other = lax.optimization_barrier((mine, row_qkv, other, near))[:3]
+    far = lax.all_gather(other, "c", axis=0)
+    state = row_own(place, near, far, row_gain, row_qkv)
+    before = after(before, state[0])
     before_other = lax.ppermute(before, "yl", SWAP)
-    far = lax.all_gather(after(other, before), "c", axis=0)
-    before_near = lax.all_gather(after(before, far), "c", axis=0)
-    place = after(place, before_near)
-    state = row_own(place, near, far, row_gain, row_qkv)
-    before_far = lax.all_gather(after(before_other, state[0]), "c", axis=0)
+    before_near = lax.all_gather(before, "c", axis=0)
+    before_far = lax.all_gather(after(before_other, before_near), "c", axis=0)
 
     mine = after(mine, before_far)
     theirs = lax.ppermute(mine, ("yh", "yl", "c"), cross_route((1,)))

time: 135 us -> 140 us (1.037)
  local copies, waits for them, and re-layouts: 7.48 us -> 3.42 us
  starting transfers between devices: 49.2 us -> 53 us
  waiting for transfers between devices: 23.3 us -> 26.4 us
  other arithmetic: 0.25 us -> 1.81 us
    all_to_all x1, starting transfers between devices: 11.3 us -> 21.3 us  [on_device(): lax.all_to_all(sent.reshape(COLS, 4, 128), HEAD + SEQ, 0, 0, tiled=True)]
    ppermute x1, starting transfers between devices: 15.9 us -> 9.95 us  [on_device(): theirs = lax.ppermute(mine, ('yh', 'yl', 'c'), cross_route((1,)))]
    unnamed x17 -> x13, local copies, waits for them, and re-layouts: 5.22 us -> 1.15 us
    ppermute x1, waiting for transfers between devices: 0.01 us -> 3.8 us  [on_device(): before_other = lax.ppermute(before, 'yl', SWAP)]
    mul x1, other arithmetic: 0.17 us -> 1.74 us  [on_device(): row_qkv * jnp.array([SCALE, 1, 1], jnp.bfloat16)[:, None, None, None]]
  transfers between devices with their start and end apart: 7 -> 7, of which waited for: 2 -> 3; matrix products, arithmetic and copies ran while one was open for 2% -> 3% of each run, Pallas kernels for 5% -> 6%
where the time goes in v8:
time: 140 us
  starting transfers between devices  53 us (38%)
  blocking collectives  39.9 us (28%)
  waiting for transfers between devices  26.4 us (19%)
  Pallas kernels  14.8 us (11%)
  local copies, waits for them, and re-layouts  3.42 us (2%)
  other arithmetic  1.81 us (1%)
    all_to_all x1, blocking collectives, on_device(): lax.all_to_all(mixed.reshape(COLS, 2, 128), HEAD + SEQ, 0, 0, tiled=True)  27 us
    all_to_all x1, starting transfers between devices, on_device(): lax.all_to_all(sent.reshape(COLS, 4, 128), HEAD + SEQ, 0, 0, tiled=True)  21.3 us
    all_to_all x1, waiting for transfers between devices, on_device(): lax.all_to_all(sent.reshape(COLS, 4, 128), HEAD + SEQ, 0, 0, tiled=True)  19.2 us
    ppermute x1, starting transfers between devices, on_device(): theirs = lax.ppermute(mine, ('yh', 'yl', 'c'), cross_route((1,)))  9.95 us
    pallas_call x1, Pallas kernels, col_layer(): pl.pallas_call(col_layer_kernel, out_shape=jax.ShapeDtypeStruct((PARTS, 1...  6.88 us
    ppermute x1, starting transfers between devices, on_device(): mine_swapped = lax.ppermute(after(mine, sent), 'c', SWAP)  6.28 us
    ppermute x1, starting transfers between devices, on_device(): theirs_swapped = lax.ppermute(after(theirs, moved), 'c', SWAP)  5.19 us
    all_gather x1, blocking collectives, on_device(): near = lax.all_gather(inputs, 'c', axis=0)  4.74 us
  transfers between devices with their start and end apart: 7, of which 3 were waited for; matrix products, arithmetic and copies ran while one was open for 3% of the time, Pallas kernels for 6%

profile of v8, /device:TPU:1, one launch (start us, length us, event | category | flops | bytes accessed | tf_op | source)
XLA Modules:
  0.0 139.5 jit_solution(15883089970266785872)
XLA Ops:
  0.0 4.0 %collective-permute-start = (bf16[512,256]{1,0:T(8,128)(2,1)}, bf16[512,256]{1,0:T(8,128)(2,1)S(1)}, u32[]{:S(2)}, u32[]{:S(2)}) collective-permute-start(bf16[512,256]{1,0:T(8,128)(2,1)} %source.1), channel_id=1, source_target_pairs={{0,4},{4,8},{8,12},{12,16},{16,20},{20,24},{24,28},{28,32},{32,36}... | collective-permute-start | bytes 786440 | tf_op jit(solution)/shard_map/ppermute | solution.py:263
  4.0 3.2 %collective-permute-start.1 = (bf16[512,256]{1,0:T(8,128)(2,1)}, bf16[512,256]{1,0:T(8,128)(2,1)S(1)}, u32[]{:S(2)}, u32[]{:S(2)}) collective-permute-start(bf16[512,256]{1,0:T(8,128)(2,1)} %source.1), channel_id=1, source_target_pairs={{0,2},{2,0},{1,3},{3,1},{4,6},{6,4},{5,7},{7,5},{8,10},{10,8},{9,1... | collective-permute-start | bytes 786440 | tf_op jit(solution)/shard_map/ppermute | solution.py:264
  7.2 1.7 %broadcast_multiply_fusion.weight = bf16[3,4,256,256]{3,2,1,0:T(8,128)(2,1)S(1)} fusion(bf16[3,4,256,256]{3,2,1,0:T(8,128)(2,1)} %bitcast.28, bf16[3]{0:T(256)(128)(2,1)} %constant.30.clone), kind=kLoop, calls=%fused_computation | loop fusion | flops 786432 | bytes 3145734 | tf_op jit(solution)/shard_map/mul | solution.py:261
  9.2 0.2 copy-done.3
  9.3 1.6 %pack_weights.1.w0 = bf16[5120,256]{1,0:T(8,128)(2,1)} custom-call(bf16[256,1024]{1,0:T(8,128)(2,1)S(1)} %copy-done.2, bf16[3072,256]{1,0:T(8,128)(2,1)S(1)} %bitcast.24, bf16[256,1024]{1,0:T(8,128)(2,1)S(1)} %copy-done.3), custom_call_target="tpu_custom_call" | custom-call | flops 1 | bytes 1 | tf_op jit(solution)/shard_map/pack_weights/pallas_call | solution.py:176
  11.0 4.7 %all-gather = bf16[1024,256]{1,0:T(8,128)(2,1)S(1)} all-gather(bf16[512,256]{1,0:T(8,128)(2,1)S(1)} %copy-done.1), channel_id=2, replica_groups=mesh['yh'=4,'z'=8,'x'=4,'yl'=2,'c'=2] {'c'}, dimensions={0}, use_global_device_ids=true | all-gather | bytes 786432 | tf_op jit(solution)/shard_map/all_gather | solution.py:265
  15.8 2.7 %all-gather.1 = bf16[1024,256]{1,0:T(8,128)(2,1)S(1)} all-gather(bf16[512,256]{1,0:T(8,128)(2,1)S(1)} %collective-permute-done.1), channel_id=3, replica_groups=mesh['yh'=4,'z'=8,'x'=4,'yl'=2,'c'=2] {'c'}, dimensions={0}, use_global_device_ids=true | all-gather | bytes 786432 | tf_op jit(solution)/shard_map/all_gather | solution.py:268
  18.5 3.1 %row_own.1 = (bf16[512,256]{1,0:T(8,128)(2,1)S(1)}, f32[512,256]{1,0:T(8,128)S(1)}, f32[512,256]{1,0:T(8,128)S(1)}, f32[512,256]{1,0:T(8,128)S(1)}) custom-call(s32[4]{0:T(128)S(1)} %pad_add_fusion.place, bf16[2,512,256]{2,1,0:T(8,128)(2,1)S(1)} %bitcast.22, bf16[2,512,256]{2,1,0:T(8,128)(2,1)S(1)} %bitcast.23, f32[4,1,256]{2,1,0:T(1,128)S(1)} %bitcast.25, ...), custom_call_target="tpu_custom_call" | custom-call | flops 1 | bytes 1 | tf_op jit(solution)/shard_map/row_own/pallas_call | solution.py:102
  21.6 3.1 %collective-permute-start.2 = (bf16[512,256]{1,0:T(8,128)(2,1)S(1)}, bf16[512,256]{1,0:T(8,128)(2,1)S(1)}, u32[]{:S(2)}, u32[]{:S(2)}) collective-permute-start(bf16[512,256]{1,0:T(8,128)(2,1)S(1)} %collective-permute-done), channel_id=1, source_target_pairs={{0,2},{2,0},{1,3},{3,1},{4,6},{6,4},{5,7},{7,5},{8,10},{10,8},{9,1... | collective-permute-start | bytes 786440 | tf_op jit(solution)/shard_map/ppermute | solution.py:271
  24.7 2.5 %all-gather.2 = bf16[1024,256]{1,0:T(8,128)(2,1)S(1)} all-gather(bf16[512,256]{1,0:T(8,128)(2,1)S(1)} %collective-permute-done), channel_id=4, replica_groups=mesh['yh'=4,'z'=8,'x'=4,'yl'=2,'c'=2] {'c'}, dimensions={0}, use_global_device_ids=true | all-gather | bytes 786432 | tf_op jit(solution)/shard_map/all_gather | solution.py:272
  27.2 3.8 %collective-permute-done.2 = bf16[512,256]{1,0:T(8,128)(2,1)S(1)} collective-permute-done((bf16[512,256]{1,0:T(8,128)(2,1)S(1)}, bf16[512,256]{1,0:T(8,128)(2,1)S(1)}, u32[]{:S(2)}, u32[]{:S(2)}) %collective-permute-start.2) | collective-permute-done | bytes 262176 | tf_op jit(solution)/shard_map/ppermute | solution.py:271
  31.0 3.0 %all-gather.3 = bf16[1024,256]{1,0:T(8,128)(2,1)S(1)} all-gather(bf16[512,256]{1,0:T(8,128)(2,1)S(1)} %collective-permute-done.2), channel_id=5, replica_groups=mesh['yh'=4,'z'=8,'x'=4,'yl'=2,'c'=2] {'c'}, dimensions={0}, use_global_device_ids=true | all-gather | bytes 786432 | tf_op jit(solution)/shard_map/all_gather | solution.py:273
  34.0 9.9 %collective-permute-start.4 = (bf16[5120,256]{1,0:T(8,128)(2,1)}, bf16[5120,256]{1,0:T(8,128)(2,1)}, u32[]{:S(2)}, u32[]{:S(2)}) collective-permute-start(bf16[5120,256]{1,0:T(8,128)(2,1)} %pack_weights.1.w0), channel_id=1, source_target_pairs={{2,0},{0,2},{3,129},{129,3},{130,128},{128,130},{131,257},{257,131... | collective-permute-start | bytes 7864328 | tf_op jit(solution)/shard_map/ppermute | solution.py:276
  43.9 3.3 %row_halo.1 = bf16[512,512]{1,0:T(8,128)(2,1)S(1)} custom-call(s32[4]{0:T(128)S(1)} %pad_add_fusion.place, bf16[2,512,256]{2,1,0:T(8,128)(2,1)S(1)} %bitcast.20, bf16[2,512,256]{2,1,0:T(8,128)(2,1)S(1)} %bitcast.21, f32[4,1,256]{2,1,0:T(1,128)S(1)} %bitcast.26, bf16[3,4,256,256]{3,2,1,0:T(8,128)(2,1)S(1)} %broadcast_multiply_fusion.weight, ...), custom_call_target="tpu_custom_call" | custom-call | flops 1 | bytes 1 | tf_op jit(solution)/shard_map/row_halo/pallas_call | solution.py:145
  47.2 1.0 reshape.28
  48.2 21.3 %all-to-all-start = ((bf16[512,4,128]{2,1,0:T(4,128)(2,1)}), bf16[512,4,128]{2,1,0:T(4,128)(2,1)}, u32[]{:S(2)}, u32[]{:S(2)}) async-start(bf16[512,4,128]{2,1,0:T(4,128)(2,1)} %reshape.28), calls=%async_computation | async-start | bytes 1048576 | tf_op jit(solution)/shard_map/all_to_all | solution.py:280
  69.5 6.3 %collective-permute-start.3 = (bf16[5120,256]{1,0:T(8,128)(2,1)}, bf16[5120,256]{1,0:T(8,128)(2,1)S(1)}, u32[]{:S(2)}, u32[]{:S(2)}) collective-permute-start(bf16[5120,256]{1,0:T(8,128)(2,1)} %pack_weights.1.w0), channel_id=1, source_target_pairs={{0,1},{1,0},{2,3},{3,2},{4,5},{5,4},{6,7},{7,6},{8,9},{9,8},{10,11... | collective-permute-start | bytes 7864328 | tf_op jit(solution)/shard_map/ppermute | solution.py:278
  75.7 19.2 %all-to-all-done = bf16[512,4,128]{2,1,0:T(4,128)(2,1)} async-done(((bf16[512,4,128]{2,1,0:T(4,128)(2,1)}), bf16[512,4,128]{2,1,0:T(4,128)(2,1)}, u32[]{:S(2)}, u32[]{:S(2)}) %all-to-all-start) | async-done | bytes 524320 | tf_op jit(solution)/shard_map/all_to_all | solution.py:280
  94.9 5.2 %collective-permute-start.5 = (bf16[5120,256]{1,0:T(8,128)(2,1)}, bf16[5120,256]{1,0:T(8,128)(2,1)}, u32[]{:S(2)}, u32[]{:S(2)}) collective-permute-start(bf16[5120,256]{1,0:T(8,128)(2,1)} %collective-permute-done.4.w2), channel_id=1, source_target_pairs={{0,1},{1,0},{2,3},{3,2},{4,5},{5,4},{6,7},{7,6},{8,9},{9,8},{10,11... | collective-permute-start | bytes 7864328 | tf_op jit(solution)/shard_map/ppermute | solution.py:281
  100.1 1.2 reshape.29.moved
  101.4 3.4 %collective-permute-done.5.w3 = bf16[5120,256]{1,0:T(8,128)(2,1)} collective-permute-done((bf16[5120,256]{1,0:T(8,128)(2,1)}, bf16[5120,256]{1,0:T(8,128)(2,1)}, u32[]{:S(2)}, u32[]{:S(2)}) %collective-permute-start.5) | collective-permute-done | bytes 2621472 | tf_op jit(solution)/shard_map/ppermute | solution.py:281
  104.8 6.9 %col_layer.1 = bf16[4,128,256]{2,1,0:T(8,128)(2,1)S(1)} custom-call(s32[4]{0:T(128)S(1)} %pad_add_fusion.place, bf16[4,128,512]{2,1,0:T(8,128)(2,1)S(1)} %reshape.29.moved, f32[4,1,256]{2,1,0:T(1,128)S(1)} %bitcast.27, bf16[5120,256]{1,0:T(8,128)(2,1)} %pack_weights.1.w0, bf16[5120,256]{1,0:T(8,128)(2,1)S(1)} %collective-permute-done.3.w1, ...), custom_call_target="tpu_custom_call" | custom-call | flops 1 | bytes 1 | tf_op jit(solution)/shard_map/col_layer/pallas_call | solution.py:227
  111.7 27.0 %all_to_all.10 = bf16[512,2,128]{2,1,0:T(2,128)(2,1)S(1)} all-to-all(bf16[512,2,128]{2,1,0:T(2,128)(2,1)S(1)} %reshape.31), channel_id=1, replica_groups=mesh['yh'=4,'z'=8,'x'=4,'yl'=2,'c'=2] {'yl','c','yh','z','x'}, dimensions={0} | all-to-all | bytes 524288 | tf_op jit(solution)/shard_map/all_to_all | solution.py:288
  138.8 0.7 copy.11
  (17 shorter events, 0.4 us)
Async XLA Ops:
  0.0 21.5 %collective-permute-start = (bf16[512,256]{1,0:T(8,128)(2,1)}, bf16[512,256]{1,0:T(8,128)(2,1)S(1)}, u32[]{:S(2)}, u32[]{:S(2)}) collective-permute-start(bf16[512,256]{1,0:T(8,128)(2,1)} %source.1), channel_id=1, source_target_pairs={{0,4},{4,8},{8,12},{12,16},{16,20},{20,24},{24,28},{28,32},{32,36}... | collective-permute-start | bytes 786440 | tf_op jit(solution)/shard_map/ppermute | solution.py:263
  4.0 11.8 %collective-permute-start.1 = (bf16[512,256]{1,0:T(8,128)(2,1)}, bf16[512,256]{1,0:T(8,128)(2,1)S(1)}, u32[]{:S(2)}, u32[]{:S(2)}) collective-permute-start(bf16[512,256]{1,0:T(8,128)(2,1)} %source.1), channel_id=1, source_target_pairs={{0,2},{2,0},{1,3},{3,1},{4,6},{6,4},{5,7},{7,5},{8,10},{10,8},{9,1... | collective-permute-start | bytes 786440 | tf_op jit(solution)/shard_map/ppermute | solution.py:264
  7.2 1.9 %copy-start = (bf16[1024,3,256]{2,0,1:T(8,128)(2,1)S(1)}, bf16[1024,3,256]{2,0,1:T(8,128)(2,1)}, u32[]{:S(2)}) copy-start(bf16[1024,3,256]{2,0,1:T(8,128)(2,1)} %param.13) | copy-start | bytes 4718596
  7.2 2.0 %copy-start.2 = (bf16[256,1024]{1,0:T(8,128)(2,1)S(1)}, bf16[256,1024]{1,0:T(8,128)(2,1)}, u32[]{:S(2)}) copy-start(bf16[256,1024]{1,0:T(8,128)(2,1)} %row_out.1) | copy-start | bytes 1572868
  7.2 2.1 %copy-start.3 = (bf16[256,1024]{1,0:T(8,128)(2,1)S(1)}, bf16[256,1024]{1,0:T(8,128)(2,1)}, u32[]{:S(2)}) copy-start(bf16[256,1024]{1,0:T(8,128)(2,1)} %col_out.1) | copy-start | bytes 1572868
  9.3 1.7 %copy-start.1 = (bf16[512,256]{1,0:T(8,128)(2,1)S(1)}, bf16[512,256]{1,0:T(8,128)(2,1)}, u32[]{:S(2)}) copy-start(bf16[512,256]{1,0:T(8,128)(2,1)} %source.1) | copy-start | bytes 786436
  10.9 7.5 %copy-start.4 = (f32[1024]{0:T(1024)S(1)}, f32[1024]{0:T(1024)}, u32[]{:S(2)}) copy-start(f32[1024]{0:T(1024)} %param.9) | copy-start | bytes 12292
  21.6 9.4 %collective-permute-start.2 = (bf16[512,256]{1,0:T(8,128)(2,1)S(1)}, bf16[512,256]{1,0:T(8,128)(2,1)S(1)}, u32[]{:S(2)}, u32[]{:S(2)}) collective-permute-start(bf16[512,256]{1,0:T(8,128)(2,1)S(1)} %collective-permute-done), channel_id=1, source_target_pairs={{0,2},{2,0},{1,3},{3,1},{4,6},{6,4},{5,7},{7,5},{8,10},{10,8},{9,1... | collective-permute-start | bytes 786440 | tf_op jit(solution)/shard_map/ppermute | solution.py:271
  34.0 60.9 %collective-permute-start.4 = (bf16[5120,256]{1,0:T(8,128)(2,1)}, bf16[5120,256]{1,0:T(8,128)(2,1)}, u32[]{:S(2)}, u32[]{:S(2)}) collective-permute-start(bf16[5120,256]{1,0:T(8,128)(2,1)} %pack_weights.1.w0), channel_id=1, source_target_pairs={{2,0},{0,2},{3,129},{129,3},{130,128},{128,130},{131,257},{257,131... | collective-permute-start | bytes 7864328 | tf_op jit(solution)/shard_map/ppermute | solution.py:276
  47.2 57.6 %copy-start.5 = (f32[1024]{0:T(1024)S(1)}, f32[1024]{0:T(1024)}, u32[]{:S(2)}) copy-start(f32[1024]{0:T(1024)} %param.12) | copy-start | bytes 12292
  48.2 46.7 %all-to-all-start = ((bf16[512,4,128]{2,1,0:T(4,128)(2,1)}), bf16[512,4,128]{2,1,0:T(4,128)(2,1)}, u32[]{:S(2)}, u32[]{:S(2)}) async-start(bf16[512,4,128]{2,1,0:T(4,128)(2,1)} %reshape.28), calls=%async_computation | async-start | bytes 1048576 | tf_op jit(solution)/shard_map/all_to_all | solution.py:280
  69.5 31.9 %collective-permute-start.3 = (bf16[5120,256]{1,0:T(8,128)(2,1)}, bf16[5120,256]{1,0:T(8,128)(2,1)S(1)}, u32[]{:S(2)}, u32[]{:S(2)}) collective-permute-start(bf16[5120,256]{1,0:T(8,128)(2,1)} %pack_weights.1.w0), channel_id=1, source_target_pairs={{0,1},{1,0},{2,3},{3,2},{4,5},{5,4},{6,7},{7,6},{8,9},{9,8},{10,11... | collective-permute-start | bytes 7864328 | tf_op jit(solution)/shard_map/ppermute | solution.py:278
  94.9 9.9 %collective-permute-start.5 = (bf16[5120,256]{1,0:T(8,128)(2,1)}, bf16[5120,256]{1,0:T(8,128)(2,1)}, u32[]{:S(2)}, u32[]{:S(2)}) collective-permute-start(bf16[5120,256]{1,0:T(8,128)(2,1)} %collective-permute-done.4.w2), channel_id=1, source_target_pairs={{0,1},{1,0},{2,3},{3,2},{4,5},{5,4},{6,7},{7,6},{8,9},{9,8},{10,11... | collective-permute-start | bytes 7864328 | tf_op jit(solution)/shard_map/ppermute | solution.py:281

commit v9 on v6

--- a/solution.py
+++ b/solution.py
@@ -157,6 +157,7 @@
 
 
 QKV_AT, OUT_AT, WEIGHT_ROWS = 1024, 4096, 5120
+LONG = 2*10**10
 
 
 def pack_kernel(row_out, col_qkv, col_out, packed, sem):
@@ -185,55 +186,80 @@
     )(row_out, col_qkv, col_out)
 
 
-def col_layer_kernel(place, moved, gain, w0, w1, w2, w3, out, held, sem):
+def weight_groups(place):
+    return [place[0] + place[3], place[0] + 1 - place[3], place[1] + place[3], place[1] + 1 - place[3]]
+
+
+def row_output_kernel(place, moved, w0, w1, w2, out, held, sem):
+    copies = [
+        pltpu.make_async_copy(w.at[:QKV_AT], held.at[i], sem.at[i]) for i, w in enumerate((w0, w1, w2))
+    ]
+    for copy in copies:
+        copy.start()
+    atts = [moved[g, :, :GROUP] for g in weight_groups(place)[:3]]
+    for copy in copies:
+        copy.wait()
+    for n in range(PARTS):
+        total = sum(dot(a, held[i, n * GROUP : (n + 1) * GROUP, :]) for i, a in enumerate(atts))
+        out[n] = moved[n, :, GROUP:].astype(jnp.float32) + total
+
+
+def row_output(place, moved, weights):
+    return pl.pallas_call(
+        row_output_kernel,
+        out_shape=jax.ShapeDtypeStruct((PARTS, 128, GROUP), jnp.float32),
+        in_specs=[SMEM, VMEM] + [ANY] * 3,
+        out_specs=VMEM,
+        scratch_shapes=[pltpu.VMEM((3, QKV_AT, GROUP), jnp.bfloat16), pltpu.SemaphoreType.DMA((3,))],
+        compiler_params=pltpu.CompilerParams(vmem_limit_bytes=8 * MIB),
+        cost_estimate=pl.CostEstimate(flops=LONG, bytes_accessed=1, transcendentals=0),
+        name="row_output",
+    )(place, moved, *weights)
+
+
+def col_layer_kernel(place, moved, partial, gain, w0, w1, w2, w3, out, held, last, sem):
     arrays = (w0, w1, w2, w3)
-    groups = [place[0] + place[3], place[0] + 1 - place[3], place[1] + place[3], place[1] + 1 - place[3]]
-    first = [pltpu.make_async_copy(w.at[:QKV_AT], held.at[i, :QKV_AT], sem.at[0, i]) for i, w in enumerate(arrays)]
-    rest = [pltpu.make_async_copy(w.at[QKV_AT:], held.at[i, QKV_AT:], sem.at[1, i]) for i, w in enumerate(arrays)]
-    for copy in first + rest:
+    first = pltpu.make_async_copy(w3.at[:QKV_AT], last, sem.at[PARTS])
+    rest = [pltpu.make_async_copy(w.at[QKV_AT:], held.at[i], sem.at[i]) for i, w in enumerate(arrays)]
+    for copy in [first] + rest:
         copy.start()
-
-    def add_projected(pieces, atts, at):
-        result = []
-        for n in range(PARTS):
-            rows = slice(at + n * GROUP, at + (n + 1) * GROUP)
-            total = sum(dot(a, held[i, rows, :]) for i, a in enumerate(atts))
-            result.append((pieces[n].astype(jnp.float32) + total).astype(jnp.bfloat16))
-        return result
-
-    atts = [moved[g, :, :GROUP] for g in groups]
-    for copy in first:
-        copy.wait()
-    pieces = add_projected([moved[n, :, GROUP:] for n in range(PARTS)], atts, 0)
+    att = moved[weight_groups(place)[3], :, :GROUP]
+    first.wait()
+    pieces = [
+        (partial[n] + dot(att, last[n * GROUP : (n + 1) * GROUP, :])).astype(jnp.bfloat16) for n in range(PARTS)
+    ]
     normed = normed_pieces(pieces, [gain[n] for n in range(PARTS)])
     normed = jnp.concatenate(normed, axis=1)
     row, col = triangle(normed.shape[0])
     atts = []
     for i, copy in enumerate(rest):
         copy.wait()
-        q, k, v = [
-            dot(normed, held[i, QKV_AT + j * 1024 : QKV_AT + (j + 1) * 1024, :]).astype(jnp.bfloat16)
-            for j in range(3)
-        ]
+        q, k, v = [dot(normed, held[i, j * 1024 : (j + 1) * 1024, :]).astype(jnp.bfloat16) for j in range(3)]
         _, norm, acc = attend_blocks(
             q * jnp.bfloat16(SCALE), [k], [v], [lambda s: jnp.where(col <= row, s, -1e30)]
         )
         atts.append((acc / norm).astype(jnp.bfloat16))
-    for n, piece in enumerate(add_projected(pieces, atts, OUT_AT)):
-        out[n] = piece
-
-
-def col_layer(place, moved, gain, weights):
+    for n in range(PARTS):
+        rows = slice(OUT_AT - QKV_AT + n * GROUP, OUT_AT - QKV_AT + (n + 1) * GROUP)
+        total = sum(dot(a, held[i, rows, :]) for i, a in enumerate(atts))
+        out[n] = (pieces[n].astype(jnp.float32) + total).astype(jnp.bfloat16)
+
+
+def col_layer(place, moved, partial, gain, weights):
     return pl.pallas_call(
         col_layer_kernel,
         out_shape=jax.ShapeDtypeStruct((PARTS, 128, GROUP), jnp.bfloat16),
-        in_specs=[SMEM, VMEM, VMEM] + [ANY] * 4,
+        in_specs=[SMEM, VMEM, VMEM, VMEM] + [ANY] * 4,
         out_specs=VMEM,
-        scratch_shapes=[pltpu.VMEM((PARTS, WEIGHT_ROWS, GROUP), jnp.bfloat16), pltpu.SemaphoreType.DMA((2, PARTS))],
+        scratch_shapes=[
+            pltpu.VMEM((PARTS, WEIGHT_ROWS - QKV_AT, GROUP), jnp.bfloat16),
+            pltpu.VMEM((QKV_AT, GROUP), jnp.bfloat16),
+            pltpu.SemaphoreType.DMA((PARTS + 1,)),
+        ],
         compiler_params=pltpu.CompilerParams(vmem_limit_bytes=20 * MIB),
         cost_estimate=pl.CostEstimate(flops=1, bytes_accessed=1, transcendentals=0),
         name="col_layer",
-    )(place, moved, gain, *weights)
+    )(place, moved, partial, gain, *weights)
 
 
 SWAP = [(0, 1), (1, 0)]
@@ -278,10 +304,13 @@
     mine_swapped = lax.ppermute(after(mine, sent), "c", SWAP)
 
     moved = lax.all_to_all(sent.reshape(COLS, 4, 128), HEAD + SEQ, 0, 0, tiled=True)
-    theirs_swapped = lax.ppermute(after(theirs, moved), "c", SWAP)
+    moved = moved.reshape(PARTS, 128, 2 * GROUP)
+    theirs_swapped = lax.ppermute(after(theirs, sent), "c", SWAP)
+    partial = row_output(place, moved, [mine, mine_swapped, theirs])
     mixed = col_layer(
         place,
-        moved.reshape(PARTS, 128, 2 * GROUP),
+        moved,
+        partial,
         col_gain.reshape(PARTS, 1, GROUP),
         [mine, mine_swapped, theirs, theirs_swapped],
     )

time: 135 us -> 131 us (0.970)
  starting transfers between devices: 49.2 us -> 42.1 us
  blocking collectives: 40.4 us -> 42.9 us
  Pallas kernels: 13.7 us -> 15.3 us
    ppermute x1, waiting for transfers between devices: 0.01 us -> 20 us  [on_device(): theirs = lax.ppermute(mine, ('yh', 'yl', 'c'), cross_route((1,)))]
    all_to_all x1, waiting for transfers between devices: 19.9 us -> 2.01 us  [on_device(): lax.all_to_all(sent.reshape(COLS, 4, 128), HEAD + SEQ, 0, 0, tiled=True)]
    ppermute x1, starting transfers between devices: 6.28 us -> 1.92 us  [on_device(): mine_swapped = lax.ppermute(after(mine, sent), 'c', SWAP)]
    ppermute x1, waiting for transfers between devices: 3.42 us -> 0.01 us  [on_device(): theirs_swapped = lax.ppermute(after(theirs, sent), 'c', SWAP)]
    ppermute x1, starting transfers between devices: 4.91 us -> 2.09 us  [on_device(): theirs_swapped = lax.ppermute(after(theirs, sent), 'c', SWAP)]
    all_to_all x1, blocking collectives: 28.4 us -> 30.9 us  [on_device(): lax.all_to_all(mixed.reshape(COLS, 2, 128), HEAD + SEQ, 0, 0, tiled=True)]
    pallas_call x0 -> x1, Pallas kernels: none -> 2.18 us  [row_output(): pl.pallas_call(row_output_kernel, out_shape=jax.ShapeDtypeStruct((PARTS,...]
  transfers between devices with their start and end apart: 7 -> 7, of which waited for: 2 -> 2; matrix products, arithmetic and copies ran while one was open for 2% -> 2% of each run, Pallas kernels for 5% -> 7%
where the time goes in v9:
time: 131 us; the launch traced here: 130 us
  blocking collectives  42.9 us (33%)
  starting transfers between devices  42.1 us (32%)
  waiting for transfers between devices  22.1 us (17%)
  Pallas kernels  15.3 us (12%)
  local copies, waits for them, and re-layouts  7.48 us (6%)
    all_to_all x1, blocking collectives, on_device(): lax.all_to_all(mixed.reshape(COLS, 2, 128), HEAD + SEQ, 0, 0, tiled=True)  30.9 us
    ppermute x1, waiting for transfers between devices, on_device(): theirs = lax.ppermute(mine, ('yh', 'yl', 'c'), cross_route((1,)))  20 us
    ppermute x1, starting transfers between devices, on_device(): theirs = lax.ppermute(mine, ('yh', 'yl', 'c'), cross_route((1,)))  15.9 us
    all_to_all x1, starting transfers between devices, on_device(): lax.all_to_all(sent.reshape(COLS, 4, 128), HEAD + SEQ, 0, 0, tiled=True)  11.4 us
    pallas_call x1, Pallas kernels, col_layer(): pl.pallas_call(col_layer_kernel, out_shape=jax.ShapeDtypeStruct((PARTS, 1...  6.26 us
    unnamed x17, local copies, waits for them, and re-layouts  5.22 us
    all_gather x1, blocking collectives, on_device(): near = lax.all_gather(inputs, 'c', axis=0)  4.96 us
    ppermute x1, starting transfers between devices, on_device(): before = lax.ppermute(inputs, SEQ, [(i, i + 1) for i in range(127)])  3.95 us
  transfers between devices with their start and end apart: 7, of which 2 were waited for; matrix products, arithmetic and copies ran while one was open for 2% of the time, Pallas kernels for 7%

profile of v9, /device:TPU:1, one launch (start us, length us, event | category | flops | bytes accessed | tf_op | source)
XLA Modules:
  0.0 130.2 jit_solution(12481349902124418737)
XLA Ops:
  0.0 4.0 %collective-permute-start = (bf16[512,256]{1,0:T(8,128)(2,1)}, bf16[512,256]{1,0:T(8,128)(2,1)S(1)}, u32[]{:S(2)}, u32[]{:S(2)}) collective-permute-start(bf16[512,256]{1,0:T(8,128)(2,1)} %source.1), channel_id=1, source_target_pairs={{0,4},{4,8},{8,12},{12,16},{16,20},{20,24},{24,28},{28,32},{32,36}... | collective-permute-start | bytes 786440 | tf_op jit(solution)/shard_map/ppermute | solution.py:289
  4.0 3.2 %collective-permute-start.1 = (bf16[512,256]{1,0:T(8,128)(2,1)}, bf16[512,256]{1,0:T(8,128)(2,1)}, u32[]{:S(2)}, u32[]{:S(2)}) collective-permute-start(bf16[512,256]{1,0:T(8,128)(2,1)} %source.1), channel_id=1, source_target_pairs={{0,2},{2,0},{1,3},{3,1},{4,6},{6,4},{5,7},{7,5},{8,10},{10,8},{9,1... | collective-permute-start | bytes 786440 | tf_op jit(solution)/shard_map/ppermute | solution.py:290
  7.2 5.0 %all-gather = bf16[1024,256]{1,0:T(8,128)(2,1)S(1)} all-gather(bf16[512,256]{1,0:T(8,128)(2,1)} %source.1), channel_id=2, replica_groups=mesh['yh'=4,'z'=8,'x'=4,'yl'=2,'c'=2] {'c'}, dimensions={0}, use_global_device_ids=true | all-gather | bytes 786432 | tf_op jit(solution)/shard_map/all_gather | solution.py:291
  12.1 1.4 %copy-done = bf16[1024,3,256]{2,0,1:T(8,128)(2,1)S(1)} copy-done((bf16[1024,3,256]{2,0,1:T(8,128)(2,1)S(1)}, bf16[1024,3,256]{2,0,1:T(8,128)(2,1)}, u32[]{:S(2)}) %copy-start) | copy-done | bytes 1572888
  13.5 1.0 copy-done.2
  14.6 1.0 copy-done.3
  16.1 1.0 copy-done.6
  17.2 3.6 %collective-permute-start.2 = (bf16[512,256]{1,0:T(8,128)(2,1)S(1)}, bf16[512,256]{1,0:T(8,128)(2,1)S(1)}, u32[]{:S(2)}, u32[]{:S(2)}) collective-permute-start(bf16[512,256]{1,0:T(8,128)(2,1)S(1)} %collective-permute-done), channel_id=1, source_target_pairs={{0,2},{2,0},{1,3},{3,1},{4,6},{6,4},{5,7},{7,5},{8,10},{10,8},{9,1... | collective-permute-start | bytes 786440 | tf_op jit(solution)/shard_map/ppermute | solution.py:294
  20.9 2.7 %all-gather.1 = bf16[1024,256]{1,0:T(8,128)(2,1)S(1)} all-gather(bf16[512,256]{1,0:T(8,128)(2,1)} %collective-permute-done.1), channel_id=3, replica_groups=mesh['yh'=4,'z'=8,'x'=4,'yl'=2,'c'=2] {'c'}, dimensions={0}, use_global_device_ids=true | all-gather | bytes 786432 | tf_op jit(solution)/shard_map/all_gather | solution.py:295
  23.6 2.2 %all-gather.2 = bf16[1024,256]{1,0:T(8,128)(2,1)S(1)} all-gather(bf16[512,256]{1,0:T(8,128)(2,1)S(1)} %collective-permute-done), channel_id=4, replica_groups=mesh['yh'=4,'z'=8,'x'=4,'yl'=2,'c'=2] {'c'}, dimensions={0}, use_global_device_ids=true | all-gather | bytes 786432 | tf_op jit(solution)/shard_map/all_gather | solution.py:296
  25.8 3.2 %row_own.1 = (bf16[512,256]{1,0:T(8,128)(2,1)S(1)}, f32[512,256]{1,0:T(8,128)S(1)}, f32[512,256]{1,0:T(8,128)S(1)}, f32[512,256]{1,0:T(8,128)S(1)}) custom-call(s32[4]{0:T(128)S(1)} %pad_add_fusion.place, bf16[2,512,256]{2,1,0:T(8,128)(2,1)S(1)} %bitcast.22, bf16[2,512,256]{2,1,0:T(8,128)(2,1)S(1)} %bitcast.23, f32[4,1,256]{2,1,0:T(1,128)S(1)} %bitcast.25, ...), custom_call_target="tpu_custom_call" | custom-call | flops 1 | bytes 1 | tf_op jit(solution)/shard_map/row_own/pallas_call | solution.py:102
  28.9 2.2 %all-gather.3 = bf16[1024,256]{1,0:T(8,128)(2,1)S(1)} all-gather(bf16[512,256]{1,0:T(8,128)(2,1)S(1)} %collective-permute-done.2), channel_id=5, replica_groups=mesh['yh'=4,'z'=8,'x'=4,'yl'=2,'c'=2] {'c'}, dimensions={0}, use_global_device_ids=true | all-gather | bytes 786432 | tf_op jit(solution)/shard_map/all_gather | solution.py:299
  31.1 15.9 %collective-permute-start.4 = (bf16[5120,256]{1,0:T(8,128)(2,1)S(1)}, bf16[5120,256]{1,0:T(8,128)(2,1)}, u32[]{:S(2)}, u32[]{:S(2)}) collective-permute-start(bf16[5120,256]{1,0:T(8,128)(2,1)S(1)} %pack_weights.1.w0), channel_id=1, source_target_pairs={{2,0},{0,2},{3,129},{129,3},{130,128},{128,130},{131,257},{257,131... | collective-permute-start | bytes 7864328 | tf_op jit(solution)/shard_map/ppermute | solution.py:302
  47.0 3.3 %row_halo.1 = bf16[512,512]{1,0:T(8,128)(2,1)S(1)} custom-call(s32[4]{0:T(128)S(1)} %pad_add_fusion.place, bf16[2,512,256]{2,1,0:T(8,128)(2,1)S(1)} %bitcast.20, bf16[2,512,256]{2,1,0:T(8,128)(2,1)S(1)} %bitcast.21, f32[4,1,256]{2,1,0:T(1,128)S(1)} %bitcast.26, bf16[3,4,256,256]{3,2,1,0:T(8,128)(2,1)S(1)} %broadcast_multiply_fusion.weight, ...), custom_call_target="tpu_custom_call" | custom-call | flops 1 | bytes 1 | tf_op jit(solution)/shard_map/row_halo/pallas_call | solution.py:145
  50.3 1.9 %collective-permute-start.3 = (bf16[5120,256]{1,0:T(8,128)(2,1)S(1)}, bf16[5120,256]{1,0:T(8,128)(2,1)}, u32[]{:S(2)}, u32[]{:S(2)}) collective-permute-start(bf16[5120,256]{1,0:T(8,128)(2,1)S(1)} %pack_weights.1.w0), channel_id=1, source_target_pairs={{0,1},{1,0},{2,3},{3,2},{4,5},{5,4},{6,7},{7,6},{8,9},{9,8},{10,11... | collective-permute-start | bytes 7864328 | tf_op jit(solution)/shard_map/ppermute | solution.py:304
  52.3 1.0 reshape.28
  53.2 11.4 %all-to-all-start = ((bf16[512,4,128]{2,1,0:T(4,128)(2,1)}), bf16[512,4,128]{2,1,0:T(4,128)(2,1)}, u32[]{:S(2)}, u32[]{:S(2)}) async-start(bf16[512,4,128]{2,1,0:T(4,128)(2,1)} %reshape.28), calls=%async_computation | async-start | bytes 1048576 | tf_op jit(solution)/shard_map/all_to_all | solution.py:306
  64.6 20.0 %collective-permute-done.4.w2 = bf16[5120,256]{1,0:T(8,128)(2,1)} collective-permute-done((bf16[5120,256]{1,0:T(8,128)(2,1)S(1)}, bf16[5120,256]{1,0:T(8,128)(2,1)}, u32[]{:S(2)}, u32[]{:S(2)}) %collective-permute-start.4) | collective-permute-done | bytes 2621472 | tf_op jit(solution)/shard_map/ppermute | solution.py:302
  84.7 2.1 %collective-permute-start.5 = (bf16[5120,256]{1,0:T(8,128)(2,1)}, bf16[5120,256]{1,0:T(8,128)(2,1)}, u32[]{:S(2)}, u32[]{:S(2)}) collective-permute-start(bf16[5120,256]{1,0:T(8,128)(2,1)} %collective-permute-done.4.w2), channel_id=1, source_target_pairs={{0,1},{1,0},{2,3},{3,2},{4,5},{5,4},{6,7},{7,6},{8,9},{9,8},{10,11... | collective-permute-start | bytes 7864328 | tf_op jit(solution)/shard_map/ppermute | solution.py:308
  86.8 2.0 %all-to-all-done = bf16[512,4,128]{2,1,0:T(4,128)(2,1)} async-done(((bf16[512,4,128]{2,1,0:T(4,128)(2,1)}), bf16[512,4,128]{2,1,0:T(4,128)(2,1)}, u32[]{:S(2)}, u32[]{:S(2)}) %all-to-all-start) | async-done | bytes 524320 | tf_op jit(solution)/shard_map/all_to_all | solution.py:306
  88.8 1.2 reshape.29.moved
  90.0 2.2 %row_output.1.partial = f32[4,128,256]{2,1,0:T(8,128)S(1)} custom-call(s32[4]{0:T(128)S(1)} %pad_add_fusion.place, bf16[4,128,512]{2,1,0:T(8,128)(2,1)S(1)} %reshape.29.moved, bf16[5120,256]{1,0:T(8,128)(2,1)S(1)} %pack_weights.1.w0, bf16[5120,256]{1,0:T(8,128)(2,1)} %collective-permute-done.3.w1, bf16[5120,256]{1,0:T(8,128)(2,1)} %collective-permute-done.4.w2), custom_call_target="tpu_custom_call" | custom-call | flops 20000000000 | bytes 1 | tf_op jit(solution)/shard_map/row_output/pallas_call | solution.py:208
  92.3 6.3 %col_layer.1 = bf16[4,128,256]{2,1,0:T(8,128)(2,1)S(1)} custom-call(s32[4]{0:T(128)S(1)} %pad_add_fusion.place, bf16[4,128,512]{2,1,0:T(8,128)(2,1)S(1)} %reshape.29.moved, f32[4,128,256]{2,1,0:T(8,128)S(1)} %row_output.1.partial, f32[4,1,256]{2,1,0:T(1,128)S(1)} %bitcast.27, bf16[5120,256]{1,0:T(8,128)(2,1)S(1)} %pack_weights.1.w0, ...), custom_call_target="tpu_custom_call" | custom-call | flops 1 | bytes 1 | tf_op jit(solution)/shard_map/col_layer/pallas_call | solution.py:249
  98.6 30.9 %all_to_all.10 = bf16[512,2,128]{2,1,0:T(2,128)(2,1)S(1)} all-to-all(bf16[512,2,128]{2,1,0:T(2,128)(2,1)S(1)} %reshape.31), channel_id=1, replica_groups=mesh['yh'=4,'z'=8,'x'=4,'yl'=2,'c'=2] {'yl','c','yh','z','x'}, dimensions={0} | all-to-all | bytes 524288 | tf_op jit(solution)/shard_map/all_to_all | solution.py:317
  (22 shorter events, 1.4 us)
Async XLA Ops:
  0.0 17.2 %collective-permute-start = (bf16[512,256]{1,0:T(8,128)(2,1)}, bf16[512,256]{1,0:T(8,128)(2,1)S(1)}, u32[]{:S(2)}, u32[]{:S(2)}) collective-permute-start(bf16[512,256]{1,0:T(8,128)(2,1)} %source.1), channel_id=1, source_target_pairs={{0,4},{4,8},{8,12},{12,16},{16,20},{20,24},{24,28},{28,32},{32,36}... | collective-permute-start | bytes 786440 | tf_op jit(solution)/shard_map/ppermute | solution.py:289
  4.0 16.9 %collective-permute-start.1 = (bf16[512,256]{1,0:T(8,128)(2,1)}, bf16[512,256]{1,0:T(8,128)(2,1)}, u32[]{:S(2)}, u32[]{:S(2)}) collective-permute-start(bf16[512,256]{1,0:T(8,128)(2,1)} %source.1), channel_id=1, source_target_pairs={{0,2},{2,0},{1,3},{3,1},{4,6},{6,4},{5,7},{7,5},{8,10},{10,8},{9,1... | collective-permute-start | bytes 786440 | tf_op jit(solution)/shard_map/ppermute | solution.py:290
  12.1 1.4 %copy-start = (bf16[1024,3,256]{2,0,1:T(8,128)(2,1)S(1)}, bf16[1024,3,256]{2,0,1:T(8,128)(2,1)}, u32[]{:S(2)}) copy-start(bf16[1024,3,256]{2,0,1:T(8,128)(2,1)} %param.13) | copy-start | bytes 4718596
  13.5 1.0 copy-start.2
  14.6 1.0 copy-start.3
  15.6 1.4 %copy-start.6 = (bf16[1024,3,256]{2,0,1:T(8,128)(2,1)S(1)}, bf16[1024,3,256]{2,0,1:T(8,128)(2,1)}, u32[]{:S(2)}) copy-start(bf16[1024,3,256]{2,0,1:T(8,128)(2,1)} %param.10) | copy-start | bytes 4718596
  15.6 1.4 %copy-start.7 = (bf16[3]{0:T(256)(128)(2,1)S(1)}, bf16[3]{0:T(256)(128)(2,1)}, u32[]{:S(2)}) copy-start(bf16[3]{0:T(256)(128)(2,1)} %constant.30.clone) | copy-start | bytes 22
  17.2 8.5 %copy-start.4 = (f32[1024]{0:T(1024)S(1)}, f32[1024]{0:T(1024)}, u32[]{:S(2)}) copy-start(f32[1024]{0:T(1024)} %param.9) | copy-start | bytes 12292
  17.2 11.7 %collective-permute-start.2 = (bf16[512,256]{1,0:T(8,128)(2,1)S(1)}, bf16[512,256]{1,0:T(8,128)(2,1)S(1)}, u32[]{:S(2)}, u32[]{:S(2)}) collective-permute-start(bf16[512,256]{1,0:T(8,128)(2,1)S(1)} %collective-permute-done), channel_id=1, source_target_pairs={{0,2},{2,0},{1,3},{3,1},{4,6},{6,4},{5,7},{7,5},{8,10},{10,8},{9,1... | collective-permute-start | bytes 786440 | tf_op jit(solution)/shard_map/ppermute | solution.py:294
  25.7 21.2 %copy-start.1 = (bf16[512,256]{1,0:T(8,128)(2,1)S(1)}, bf16[512,256]{1,0:T(8,128)(2,1)}, u32[]{:S(2)}) copy-start(bf16[512,256]{1,0:T(8,128)(2,1)} %source.1) | copy-start | bytes 786436
  31.1 53.6 %collective-permute-start.4 = (bf16[5120,256]{1,0:T(8,128)(2,1)S(1)}, bf16[5120,256]{1,0:T(8,128)(2,1)}, u32[]{:S(2)}, u32[]{:S(2)}) collective-permute-start(bf16[5120,256]{1,0:T(8,128)(2,1)S(1)} %pack_weights.1.w0), channel_id=1, source_target_pairs={{2,0},{0,2},{3,129},{129,3},{130,128},{128,130},{131,257},{257,131... | collective-permute-start | bytes 7864328 | tf_op jit(solution)/shard_map/ppermute | solution.py:302
  50.3 39.7 %collective-permute-start.3 = (bf16[5120,256]{1,0:T(8,128)(2,1)S(1)}, bf16[5120,256]{1,0:T(8,128)(2,1)}, u32[]{:S(2)}, u32[]{:S(2)}) collective-permute-start(bf16[5120,256]{1,0:T(8,128)(2,1)S(1)} %pack_weights.1.w0), channel_id=1, source_target_pairs={{0,1},{1,0},{2,3},{3,2},{4,5},{5,4},{6,7},{7,6},{8,9},{9,8},{10,11... | collective-permute-start | bytes 7864328 | tf_op jit(solution)/shard_map/ppermute | solution.py:304
  53.2 35.6 %all-to-all-start = ((bf16[512,4,128]{2,1,0:T(4,128)(2,1)}), bf16[512,4,128]{2,1,0:T(4,128)(2,1)}, u32[]{:S(2)}, u32[]{:S(2)}) async-start(bf16[512,4,128]{2,1,0:T(4,128)(2,1)} %reshape.28), calls=%async_computation | async-start | bytes 1048576 | tf_op jit(solution)/shard_map/all_to_all | solution.py:306
  84.7 7.6 %collective-permute-start.5 = (bf16[5120,256]{1,0:T(8,128)(2,1)}, bf16[5120,256]{1,0:T(8,128)(2,1)}, u32[]{:S(2)}, u32[]{:S(2)}) collective-permute-start(bf16[5120,256]{1,0:T(8,128)(2,1)} %collective-permute-done.4.w2), channel_id=1, source_target_pairs={{0,1},{1,0},{2,3},{3,2},{4,5},{5,4},{6,7},{7,6},{8,9},{9,8},{10,11... | collective-permute-start | bytes 7864328 | tf_op jit(solution)/shard_map/ppermute | solution.py:308
  90.0 2.2 %copy-start.5 = (f32[1024]{0:T(1024)S(1)}, f32[1024]{0:T(1024)}, u32[]{:S(2)}) copy-start(f32[1024]{0:T(1024)} %param.12) | copy-start | bytes 12292

commit v10 on v9

--- a/solution.py
+++ b/solution.py
@@ -190,58 +190,63 @@
     return [place[0] + place[3], place[0] + 1 - place[3], place[1] + place[3], place[1] + 1 - place[3]]
 
 
-def row_output_kernel(place, moved, w0, w1, w2, out, held, sem):
-    copies = [
-        pltpu.make_async_copy(w.at[:QKV_AT], held.at[i], sem.at[i]) for i, w in enumerate((w0, w1, w2))
-    ]
-    for copy in copies:
-        copy.start()
-    atts = [moved[g, :, :GROUP] for g in weight_groups(place)[:3]]
-    for copy in copies:
-        copy.wait()
+def row_output_kernel(place, moved, weights, out, held, sem):
+    copy = pltpu.make_async_copy(weights.at[:QKV_AT], held, sem)
+    copy.start()
+    att = moved[weight_groups(place)[0], :, :GROUP]
+    copy.wait()
     for n in range(PARTS):
-        total = sum(dot(a, held[i, n * GROUP : (n + 1) * GROUP, :]) for i, a in enumerate(atts))
-        out[n] = moved[n, :, GROUP:].astype(jnp.float32) + total
+        out[n] = moved[n, :, GROUP:].astype(jnp.float32) + dot(att, held[n * GROUP : (n + 1) * GROUP, :])
 
 
 def row_output(place, moved, weights):
     return pl.pallas_call(
         row_output_kernel,
         out_shape=jax.ShapeDtypeStruct((PARTS, 128, GROUP), jnp.float32),
-        in_specs=[SMEM, VMEM] + [ANY] * 3,
+        in_specs=[SMEM, VMEM, ANY],
         out_specs=VMEM,
-        scratch_shapes=[pltpu.VMEM((3, QKV_AT, GROUP), jnp.bfloat16), pltpu.SemaphoreType.DMA((3,))],
+        scratch_shapes=[pltpu.VMEM((QKV_AT, GROUP), jnp.bfloat16), pltpu.SemaphoreType.DMA],
         compiler_params=pltpu.CompilerParams(vmem_limit_bytes=8 * MIB),
         cost_estimate=pl.CostEstimate(flops=LONG, bytes_accessed=1, transcendentals=0),
         name="row_output",
-    )(place, moved, *weights)
+    )(place, moved, weights)
 
 
 def col_layer_kernel(place, moved, partial, gain, w0, w1, w2, w3, out, held, last, sem):
     arrays = (w0, w1, w2, w3)
-    first = pltpu.make_async_copy(w3.at[:QKV_AT], last, sem.at[PARTS])
+    first = [pltpu.make_async_copy(w.at[:QKV_AT], last.at[i], sem.at[PARTS + i]) for i, w in enumerate(arrays[1:])]
     rest = [pltpu.make_async_copy(w.at[QKV_AT:], held.at[i], sem.at[i]) for i, w in enumerate(arrays)]
-    for copy in [first] + rest:
+    for copy in first + rest:
         copy.start()
-    att = moved[weight_groups(place)[3], :, :GROUP]
-    first.wait()
-    pieces = [
-        (partial[n] + dot(att, last[n * GROUP : (n + 1) * GROUP, :])).astype(jnp.bfloat16) for n in range(PARTS)
-    ]
+    atts = [moved[g, :, :GROUP] for g in weight_groups(place)[1:]]
+    for copy in first:
+        copy.wait()
+    pieces = []
+    for n in range(PARTS):
+        total = sum(dot(a, last[i, n * GROUP : (n + 1) * GROUP, :]) for i, a in enumerate(atts))
+        pieces.append((partial[n] + total).astype(jnp.bfloat16))
     normed = normed_pieces(pieces, [gain[n] for n in range(PARTS)])
     normed = jnp.concatenate(normed, axis=1)
-    row, col = triangle(normed.shape[0])
+    rows = normed.shape[0]
+    row, col = triangle(rows)
+    allowed = jnp.concatenate([col <= row] * HEADS_HERE, axis=0)
     atts = []
     for i, copy in enumerate(rest):
         copy.wait()
         q, k, v = [dot(normed, held[i, j * 1024 : (j + 1) * 1024, :]).astype(jnp.bfloat16) for j in range(3)]
-        _, norm, acc = attend_blocks(
-            q * jnp.bfloat16(SCALE), [k], [v], [lambda s: jnp.where(col <= row, s, -1e30)]
-        )
-        atts.append((acc / norm).astype(jnp.bfloat16))
+        q = q * jnp.bfloat16(SCALE)
+        scores = dot_t(jnp.concatenate([one_head(q, head) for head in range(HEADS_HERE)], axis=0), k)
+        scores = jnp.where(allowed, scores, -1e30)
+        expo = jnp.exp(scores - jnp.max(scores, axis=-1, keepdims=True))
+        norm = jnp.sum(expo, axis=-1, keepdims=True)
+        acc = dot(expo.astype(jnp.bfloat16), v) / norm
+        att = acc[:rows]
+        for head in range(1, HEADS_HERE):
+            att = jnp.where(head_mask(rows, head), acc[head * rows : (head + 1) * rows], att)
+        atts.append(att.astype(jnp.bfloat16))
     for n in range(PARTS):
-        rows = slice(OUT_AT - QKV_AT + n * GROUP, OUT_AT - QKV_AT + (n + 1) * GROUP)
-        total = sum(dot(a, held[i, rows, :]) for i, a in enumerate(atts))
+        at = OUT_AT - QKV_AT + n * GROUP
+        total = sum(dot(a, held[i, at : at + GROUP, :]) for i, a in enumerate(atts))
         out[n] = (pieces[n].astype(jnp.float32) + total).astype(jnp.bfloat16)
 
 
@@ -253,8 +258,8 @@
         out_specs=VMEM,
         scratch_shapes=[
             pltpu.VMEM((PARTS, WEIGHT_ROWS - QKV_AT, GROUP), jnp.bfloat16),
-            pltpu.VMEM((QKV_AT, GROUP), jnp.bfloat16),
-            pltpu.SemaphoreType.DMA((PARTS + 1,)),
+            pltpu.VMEM((PARTS - 1, QKV_AT, GROUP), jnp.bfloat16),
+            pltpu.SemaphoreType.DMA((2 * PARTS - 1,)),
         ],
         compiler_params=pltpu.CompilerParams(vmem_limit_bytes=20 * MIB),
         cost_estimate=pl.CostEstimate(flops=1, bytes_accessed=1, transcendentals=0),
@@ -298,7 +303,7 @@
     state = row_own(place, near, far, row_gain, row_qkv)
     before_far = lax.all_gather(after(before_other, state[0]), "c", axis=0)
 
-    mine = after(mine, before_far)
+    mine = after(mine, before_other, state[0])
     theirs = lax.ppermute(mine, ("yh", "yl", "c"), cross_route((1,)))
     sent = row_halo(place, before_near, before_far, row_gain, row_qkv, state, inputs)
     mine_swapped = lax.ppermute(after(mine, sent), "c", SWAP)
@@ -306,7 +311,7 @@
     moved = lax.all_to_all(sent.reshape(COLS, 4, 128), HEAD + SEQ, 0, 0, tiled=True)
     moved = moved.reshape(PARTS, 128, 2 * GROUP)
     theirs_swapped = lax.ppermute(after(theirs, sent), "c", SWAP)
-    partial = row_output(place, moved, [mine, mine_swapped, theirs])
+    partial = row_output(place, moved, mine)
     mixed = col_layer(
         place,
         moved,

time: 131 us -> 127 us (0.969)
  waiting for transfers between devices: 22.1 us -> 16.5 us
  starting transfers between devices: 42.1 us -> 46.4 us
  Pallas kernels: 15.3 us -> 13.6 us
    ppermute x1, waiting for transfers between devices: 20 us -> 13.6 us  [on_device(): theirs = lax.ppermute(mine, ('yh', 'yl', 'c'), cross_route((1,)))]
    ppermute x1, starting transfers between devices: 1.92 us -> 6.28 us  [on_device(): mine_swapped = lax.ppermute(after(mine, sent), 'c', SWAP)]
    pallas_call x1, Pallas kernels: 2.18 us -> 0.83 us  [row_output(): pl.pallas_call(row_output_kernel, out_shape=jax.ShapeDtypeStruct((PARTS,...]
  transfers between devices with their start and end apart: 7 -> 7, of which waited for: 2 -> 3; matrix products, arithmetic and copies ran while one was open for 2% -> 2% of each run, Pallas kernels for 7% -> 6%
where the time goes in v10:
time: 127 us; the launch traced here: 126 us
  starting transfers between devices  46.4 us (37%)
  blocking collectives  42 us (33%)
  waiting for transfers between devices  16.5 us (13%)
  Pallas kernels  13.6 us (11%)
  local copies, waits for them, and re-layouts  7.48 us (6%)
    all_to_all x1, blocking collectives, on_device(): lax.all_to_all(mixed.reshape(COLS, 2, 128), HEAD + SEQ, 0, 0, tiled=True)  30 us
    ppermute x1, starting transfers between devices, on_device(): theirs = lax.ppermute(mine, ('yh', 'yl', 'c'), cross_route((1,)))  15.9 us
    ppermute x1, waiting for transfers between devices, on_device(): theirs = lax.ppermute(mine, ('yh', 'yl', 'c'), cross_route((1,)))  13.6 us
    all_to_all x1, starting transfers between devices, on_device(): lax.all_to_all(sent.reshape(COLS, 4, 128), HEAD + SEQ, 0, 0, tiled=True)  11.3 us
    ppermute x1, starting transfers between devices, on_device(): mine_swapped = lax.ppermute(after(mine, sent), 'c', SWAP)  6.28 us
    pallas_call x1, Pallas kernels, col_layer(): pl.pallas_call(col_layer_kernel, out_shape=jax.ShapeDtypeStruct((PARTS, 1...  5.93 us
    unnamed x17, local copies, waits for them, and re-layouts  5.22 us
    all_gather x1, blocking collectives, on_device(): near = lax.all_gather(inputs, 'c', axis=0)  4.96 us
  transfers between devices with their start and end apart: 7, of which 3 were waited for; matrix products, arithmetic and copies ran while one was open for 2% of the time, Pallas kernels for 6%

profile of v10, /device:TPU:1, one launch (start us, length us, event | category | flops | bytes accessed | tf_op | source)
XLA Modules:
  0.0 126.4 jit_solution(16833577270019834025)
XLA Ops:
  0.0 4.0 %collective-permute-start = (bf16[512,256]{1,0:T(8,128)(2,1)}, bf16[512,256]{1,0:T(8,128)(2,1)S(1)}, u32[]{:S(2)}, u32[]{:S(2)}) collective-permute-start(bf16[512,256]{1,0:T(8,128)(2,1)} %source.1), channel_id=1, source_target_pairs={{0,4},{4,8},{8,12},{12,16},{16,20},{20,24},{24,28},{28,32},{32,36}... | collective-permute-start | bytes 786440 | tf_op jit(solution)/shard_map/ppermute | solution.py:294
  4.0 3.2 %collective-permute-start.1 = (bf16[512,256]{1,0:T(8,128)(2,1)}, bf16[512,256]{1,0:T(8,128)(2,1)}, u32[]{:S(2)}, u32[]{:S(2)}) collective-permute-start(bf16[512,256]{1,0:T(8,128)(2,1)} %source.1), channel_id=1, source_target_pairs={{0,2},{2,0},{1,3},{3,1},{4,6},{6,4},{5,7},{7,5},{8,10},{10,8},{9,1... | collective-permute-start | bytes 786440 | tf_op jit(solution)/shard_map/ppermute | solution.py:295
  7.2 5.0 %all-gather = bf16[1024,256]{1,0:T(8,128)(2,1)S(1)} all-gather(bf16[512,256]{1,0:T(8,128)(2,1)} %source.1), channel_id=2, replica_groups=mesh['yh'=4,'z'=8,'x'=4,'yl'=2,'c'=2] {'c'}, dimensions={0}, use_global_device_ids=true | all-gather | bytes 786432 | tf_op jit(solution)/shard_map/all_gather | solution.py:296
  12.1 1.4 %copy-done = bf16[1024,3,256]{2,0,1:T(8,128)(2,1)S(1)} copy-done((bf16[1024,3,256]{2,0,1:T(8,128)(2,1)S(1)}, bf16[1024,3,256]{2,0,1:T(8,128)(2,1)}, u32[]{:S(2)}) %copy-start) | copy-done | bytes 1572888
  13.5 1.0 copy-done.2
  14.6 1.0 copy-done.3
  16.1 1.0 copy-done.6
  17.2 3.6 %collective-permute-start.2 = (bf16[512,256]{1,0:T(8,128)(2,1)S(1)}, bf16[512,256]{1,0:T(8,128)(2,1)S(1)}, u32[]{:S(2)}, u32[]{:S(2)}) collective-permute-start(bf16[512,256]{1,0:T(8,128)(2,1)S(1)} %collective-permute-done), channel_id=1, source_target_pairs={{0,2},{2,0},{1,3},{3,1},{4,6},{6,4},{5,7},{7,5},{8,10},{10,8},{9,1... | collective-permute-start | bytes 786440 | tf_op jit(solution)/shard_map/ppermute | solution.py:299
  20.9 2.7 %all-gather.1 = bf16[1024,256]{1,0:T(8,128)(2,1)S(1)} all-gather(bf16[512,256]{1,0:T(8,128)(2,1)} %collective-permute-done.1), channel_id=3, replica_groups=mesh['yh'=4,'z'=8,'x'=4,'yl'=2,'c'=2] {'c'}, dimensions={0}, use_global_device_ids=true | all-gather | bytes 786432 | tf_op jit(solution)/shard_map/all_gather | solution.py:300
  23.6 2.2 %all-gather.2 = bf16[1024,256]{1,0:T(8,128)(2,1)S(1)} all-gather(bf16[512,256]{1,0:T(8,128)(2,1)S(1)} %collective-permute-done), channel_id=4, replica_groups=mesh['yh'=4,'z'=8,'x'=4,'yl'=2,'c'=2] {'c'}, dimensions={0}, use_global_device_ids=true | all-gather | bytes 786432 | tf_op jit(solution)/shard_map/all_gather | solution.py:301
  25.8 3.2 %row_own.1 = (bf16[512,256]{1,0:T(8,128)(2,1)S(1)}, f32[512,256]{1,0:T(8,128)S(1)}, f32[512,256]{1,0:T(8,128)S(1)}, f32[512,256]{1,0:T(8,128)S(1)}) custom-call(s32[4]{0:T(128)S(1)} %pad_add_fusion.place, bf16[2,512,256]{2,1,0:T(8,128)(2,1)S(1)} %bitcast.22, bf16[2,512,256]{2,1,0:T(8,128)(2,1)S(1)} %bitcast.23, f32[4,1,256]{2,1,0:T(1,128)S(1)} %bitcast.25, ...), custom_call_target="tpu_custom_call" | custom-call | flops 1 | bytes 1 | tf_op jit(solution)/shard_map/row_own/pallas_call | solution.py:102
  28.9 15.9 %collective-permute-start.4 = (bf16[5120,256]{1,0:T(8,128)(2,1)S(1)}, bf16[5120,256]{1,0:T(8,128)(2,1)}, u32[]{:S(2)}, u32[]{:S(2)}) collective-permute-start(bf16[5120,256]{1,0:T(8,128)(2,1)S(1)} %pack_weights.1.weights.w0), channel_id=1, source_target_pairs={{2,0},{0,2},{3,129},{129,3},{130,128},{128,130},{131,257},{257,131... | collective-permute-start | bytes 7864328 | tf_op jit(solution)/shard_map/ppermute | solution.py:307
  44.8 2.2 %all-gather.3 = bf16[1024,256]{1,0:T(8,128)(2,1)S(1)} all-gather(bf16[512,256]{1,0:T(8,128)(2,1)S(1)} %collective-permute-done.2), channel_id=5, replica_groups=mesh['yh'=4,'z'=8,'x'=4,'yl'=2,'c'=2] {'c'}, dimensions={0}, use_global_device_ids=true | all-gather | bytes 786432 | tf_op jit(solution)/shard_map/all_gather | solution.py:304
  47.0 3.3 %row_halo.1 = bf16[512,512]{1,0:T(8,128)(2,1)S(1)} custom-call(s32[4]{0:T(128)S(1)} %pad_add_fusion.place, bf16[2,512,256]{2,1,0:T(8,128)(2,1)S(1)} %bitcast.20, bf16[2,512,256]{2,1,0:T(8,128)(2,1)S(1)} %bitcast.21, f32[4,1,256]{2,1,0:T(1,128)S(1)} %bitcast.26, bf16[3,4,256,256]{3,2,1,0:T(8,128)(2,1)S(1)} %broadcast_multiply_fusion.weight, ...), custom_call_target="tpu_custom_call" | custom-call | flops 1 | bytes 1 | tf_op jit(solution)/shard_map/row_halo/pallas_call | solution.py:145
  50.3 1.0 reshape.28
  51.3 11.3 %all-to-all-start = ((bf16[512,4,128]{2,1,0:T(4,128)(2,1)}), bf16[512,4,128]{2,1,0:T(4,128)(2,1)}, u32[]{:S(2)}, u32[]{:S(2)}) async-start(bf16[512,4,128]{2,1,0:T(4,128)(2,1)} %reshape.28), calls=%async_computation | async-start | bytes 1048576 | tf_op jit(solution)/shard_map/all_to_all | solution.py:311
  62.6 6.3 %collective-permute-start.3 = (bf16[5120,256]{1,0:T(8,128)(2,1)S(1)}, bf16[5120,256]{1,0:T(8,128)(2,1)}, u32[]{:S(2)}, u32[]{:S(2)}) collective-permute-start(bf16[5120,256]{1,0:T(8,128)(2,1)S(1)} %pack_weights.1.weights.w0), channel_id=1, source_target_pairs={{0,1},{1,0},{2,3},{3,2},{4,5},{5,4},{6,7},{7,6},{8,9},{9,8},{10,11... | collective-permute-start | bytes 7864328 | tf_op jit(solution)/shard_map/ppermute | solution.py:309
  68.9 13.6 %collective-permute-done.4.w2 = bf16[5120,256]{1,0:T(8,128)(2,1)} collective-permute-done((bf16[5120,256]{1,0:T(8,128)(2,1)S(1)}, bf16[5120,256]{1,0:T(8,128)(2,1)}, u32[]{:S(2)}, u32[]{:S(2)}) %collective-permute-start.4) | collective-permute-done | bytes 2621472 | tf_op jit(solution)/shard_map/ppermute | solution.py:307
  82.5 2.1 %collective-permute-start.5 = (bf16[5120,256]{1,0:T(8,128)(2,1)}, bf16[5120,256]{1,0:T(8,128)(2,1)}, u32[]{:S(2)}, u32[]{:S(2)}) collective-permute-start(bf16[5120,256]{1,0:T(8,128)(2,1)} %collective-permute-done.4.w2), channel_id=1, source_target_pairs={{0,1},{1,0},{2,3},{3,2},{4,5},{5,4},{6,7},{7,6},{8,9},{9,8},{10,11... | collective-permute-start | bytes 7864328 | tf_op jit(solution)/shard_map/ppermute | solution.py:313
  84.6 2.0 %all-to-all-done = bf16[512,4,128]{2,1,0:T(4,128)(2,1)} async-done(((bf16[512,4,128]{2,1,0:T(4,128)(2,1)}), bf16[512,4,128]{2,1,0:T(4,128)(2,1)}, u32[]{:S(2)}, u32[]{:S(2)}) %all-to-all-start) | async-done | bytes 524320 | tf_op jit(solution)/shard_map/all_to_all | solution.py:311
  86.6 1.2 reshape.29.moved
  88.7 0.9 collective-permute-done.5.w3
  89.6 5.9 %col_layer.1 = bf16[4,128,256]{2,1,0:T(8,128)(2,1)S(1)} custom-call(s32[4]{0:T(128)S(1)} %pad_add_fusion.place, bf16[4,128,512]{2,1,0:T(8,128)(2,1)S(1)} %reshape.29.moved, f32[4,128,256]{2,1,0:T(8,128)S(1)} %row_output.1.partial, f32[4,1,256]{2,1,0:T(1,128)S(1)} %bitcast.27, bf16[5120,256]{1,0:T(8,128)(2,1)S(1)} %pack_weights.1.weights.w0, ...), custom_call_target="tpu_custom_call" | custom-call | flops 1 | bytes 1 | tf_op jit(solution)/shard_map/col_layer/pallas_call | solution.py:254
  95.6 30.0 %all_to_all.10 = bf16[512,2,128]{2,1,0:T(2,128)(2,1)S(1)} all-to-all(bf16[512,2,128]{2,1,0:T(2,128)(2,1)S(1)} %reshape.31), channel_id=1, replica_groups=mesh['yh'=4,'z'=8,'x'=4,'yl'=2,'c'=2] {'yl','c','yh','z','x'}, dimensions={0} | all-to-all | bytes 524288 | tf_op jit(solution)/shard_map/all_to_all | solution.py:322
  (22 shorter events, 2.3 us)
Async XLA Ops:
  0.0 17.2 %collective-permute-start = (bf16[512,256]{1,0:T(8,128)(2,1)}, bf16[512,256]{1,0:T(8,128)(2,1)S(1)}, u32[]{:S(2)}, u32[]{:S(2)}) collective-permute-start(bf16[512,256]{1,0:T(8,128)(2,1)} %source.1), channel_id=1, source_target_pairs={{0,4},{4,8},{8,12},{12,16},{16,20},{20,24},{24,28},{28,32},{32,36}... | collective-permute-start | bytes 786440 | tf_op jit(solution)/shard_map/ppermute | solution.py:294
  4.0 16.9 %collective-permute-start.1 = (bf16[512,256]{1,0:T(8,128)(2,1)}, bf16[512,256]{1,0:T(8,128)(2,1)}, u32[]{:S(2)}, u32[]{:S(2)}) collective-permute-start(bf16[512,256]{1,0:T(8,128)(2,1)} %source.1), channel_id=1, source_target_pairs={{0,2},{2,0},{1,3},{3,1},{4,6},{6,4},{5,7},{7,5},{8,10},{10,8},{9,1... | collective-permute-start | bytes 786440 | tf_op jit(solution)/shard_map/ppermute | solution.py:295
  12.1 1.4 %copy-start = (bf16[1024,3,256]{2,0,1:T(8,128)(2,1)S(1)}, bf16[1024,3,256]{2,0,1:T(8,128)(2,1)}, u32[]{:S(2)}) copy-start(bf16[1024,3,256]{2,0,1:T(8,128)(2,1)} %param.13) | copy-start | bytes 4718596
  13.5 1.0 copy-start.2
  14.6 1.0 copy-start.3
  15.6 1.4 %copy-start.6 = (bf16[1024,3,256]{2,0,1:T(8,128)(2,1)S(1)}, bf16[1024,3,256]{2,0,1:T(8,128)(2,1)}, u32[]{:S(2)}) copy-start(bf16[1024,3,256]{2,0,1:T(8,128)(2,1)} %param.10) | copy-start | bytes 4718596
  15.6 1.4 %copy-start.7 = (bf16[3]{0:T(256)(128)(2,1)S(1)}, bf16[3]{0:T(256)(128)(2,1)}, u32[]{:S(2)}) copy-start(bf16[3]{0:T(256)(128)(2,1)} %constant.30.clone) | copy-start | bytes 22
  17.2 8.5 %copy-start.4 = (f32[1024]{0:T(1024)S(1)}, f32[1024]{0:T(1024)}, u32[]{:S(2)}) copy-start(f32[1024]{0:T(1024)} %param.9) | copy-start | bytes 12292
  17.2 11.7 %collective-permute-start.2 = (bf16[512,256]{1,0:T(8,128)(2,1)S(1)}, bf16[512,256]{1,0:T(8,128)(2,1)S(1)}, u32[]{:S(2)}, u32[]{:S(2)}) collective-permute-start(bf16[512,256]{1,0:T(8,128)(2,1)S(1)} %collective-permute-done), channel_id=1, source_target_pairs={{0,2},{2,0},{1,3},{3,1},{4,6},{6,4},{5,7},{7,5},{8,10},{10,8},{9,1... | collective-permute-start | bytes 786440 | tf_op jit(solution)/shard_map/ppermute | solution.py:299
  25.7 21.3 %copy-start.1 = (bf16[512,256]{1,0:T(8,128)(2,1)S(1)}, bf16[512,256]{1,0:T(8,128)(2,1)}, u32[]{:S(2)}) copy-start(bf16[512,256]{1,0:T(8,128)(2,1)} %source.1) | copy-start | bytes 786436
  28.9 53.6 %collective-permute-start.4 = (bf16[5120,256]{1,0:T(8,128)(2,1)S(1)}, bf16[5120,256]{1,0:T(8,128)(2,1)}, u32[]{:S(2)}, u32[]{:S(2)}) collective-permute-start(bf16[5120,256]{1,0:T(8,128)(2,1)S(1)} %pack_weights.1.weights.w0), channel_id=1, source_target_pairs={{2,0},{0,2},{3,129},{129,3},{130,128},{128,130},{131,257},{257,131... | collective-permute-start | bytes 7864328 | tf_op jit(solution)/shard_map/ppermute | solution.py:307
  51.3 35.3 %all-to-all-start = ((bf16[512,4,128]{2,1,0:T(4,128)(2,1)}), bf16[512,4,128]{2,1,0:T(4,128)(2,1)}, u32[]{:S(2)}, u32[]{:S(2)}) async-start(bf16[512,4,128]{2,1,0:T(4,128)(2,1)} %reshape.28), calls=%async_computation | async-start | bytes 1048576 | tf_op jit(solution)/shard_map/all_to_all | solution.py:311
  62.6 26.1 %collective-permute-start.3 = (bf16[5120,256]{1,0:T(8,128)(2,1)S(1)}, bf16[5120,256]{1,0:T(8,128)(2,1)}, u32[]{:S(2)}, u32[]{:S(2)}) collective-permute-start(bf16[5120,256]{1,0:T(8,128)(2,1)S(1)} %pack_weights.1.weights.w0), channel_id=1, source_target_pairs={{0,1},{1,0},{2,3},{3,2},{4,5},{5,4},{6,7},{7,6},{8,9},{9,8},{10,11... | collective-permute-start | bytes 7864328 | tf_op jit(solution)/shard_map/ppermute | solution.py:309
  82.5 7.1 %collective-permute-start.5 = (bf16[5120,256]{1,0:T(8,128)(2,1)}, bf16[5120,256]{1,0:T(8,128)(2,1)}, u32[]{:S(2)}, u32[]{:S(2)}) collective-permute-start(bf16[5120,256]{1,0:T(8,128)(2,1)} %collective-permute-done.4.w2), channel_id=1, source_target_pairs={{0,1},{1,0},{2,3},{3,2},{4,5},{5,4},{6,7},{7,6},{8,9},{9,8},{10,11... | collective-permute-start | bytes 7864328 | tf_op jit(solution)/shard_map/ppermute | solution.py:313
  87.9 1.8 %copy-start.5 = (f32[1024]{0:T(1024)S(1)}, f32[1024]{0:T(1024)}, u32[]{:S(2)}) copy-start(f32[1024]{0:T(1024)} %param.12) | copy-start | bytes 12292

commit v11 on v10

--- a/solution.py
+++ b/solution.py
@@ -292,9 +292,9 @@
     row_qkv = row_qkv * jnp.array([SCALE, 1, 1], jnp.bfloat16)[:, None, None, None]
 
     before = lax.ppermute(inputs, SEQ, [(i, i + 1) for i in range(127)])
-    other = lax.ppermute(inputs, "yl", SWAP)
     near = lax.all_gather(inputs, "c", axis=0)
     mine = pack_weights(row_out, col_qkv.transpose(1, 0, 2).reshape(3 * 1024, GROUP), col_out)
+    other = lax.ppermute(after(inputs, near, mine), "yl", SWAP)
     mine, row_qkv, before = lax.optimization_barrier((mine, row_qkv, before, near))[:3]
     before_other = lax.ppermute(before, "yl", SWAP)
     far = lax.all_gather(after(other, before), "c", axis=0)

time: 127 us -> 127 us (level)
  starting transfers between devices: 46.4 us -> 39.6 us
  waiting for transfers between devices: 16.5 us -> 20.2 us
  blocking collectives: 42 us -> 43.7 us
  other arithmetic: 0.25 us -> 1.66 us
    ppermute x1, starting transfers between devices: 15.9 us -> 10.1 us  [on_device(): theirs = lax.ppermute(mine, ('yh', 'yl', 'c'), cross_route((1,)))]
    ppermute x1, waiting for transfers between devices: 0.01 us -> 2.52 us  [on_device(): other = lax.ppermute(after(inputs, near, mine), 'yl', SWAP)]
    all_to_all x1, waiting for transfers between devices: 2.02 us -> 4.02 us  [on_device(): lax.all_to_all(sent.reshape(COLS, 4, 128), HEAD + SEQ, 0, 0, tiled=True)]
    mul x1, other arithmetic: 0.17 us -> 1.58 us  [on_device(): row_qkv * jnp.array([SCALE, 1, 1], jnp.bfloat16)[:, None, None, None]]
    all_gather x1, blocking collectives: 2.67 us -> 4.01 us  [on_device(): far = lax.all_gather(after(other, before), 'c', axis=0)]
    ppermute x1, starting transfers between devices: 3.21 us -> 1.91 us  [on_device(): other = lax.ppermute(after(inputs, near, mine), 'yl', SWAP)]
    all_gather x1, blocking collectives: 4.96 us -> 6.23 us  [on_device(): near = lax.all_gather(inputs, 'c', axis=0)]
    unnamed x17 -> x15, local copies, waits for them, and re-layouts: 5.22 us -> 4.84 us
  transfers between devices with their start and end apart: 7 -> 7, of which waited for: 3 -> 3; matrix products, arithmetic and copies ran while one was open for 2% -> 3% of each run, Pallas kernels for 6% -> 6%
where the time goes in v11:
time: 127 us; the launch traced here: 126 us
  blocking collectives  43.7 us (34%)
  starting transfers between devices  39.6 us (31%)
  waiting for transfers between devices  20.2 us (16%)
  Pallas kernels  13.6 us (11%)
  local copies, waits for them, and re-layouts  7.11 us (6%)
  other arithmetic  1.66 us (1%)
    all_to_all x1, blocking collectives, on_device(): lax.all_to_all(mixed.reshape(COLS, 2, 128), HEAD + SEQ, 0, 0, tiled=True)  28.9 us
    ppermute x1, waiting for transfers between devices, on_device(): theirs = lax.ppermute(mine, ('yh', 'yl', 'c'), cross_route((1,)))  13.7 us
    all_to_all x1, starting transfers between devices, on_device(): lax.all_to_all(sent.reshape(COLS, 4, 128), HEAD + SEQ, 0, 0, tiled=True)  11.2 us
    ppermute x1, starting transfers between devices, on_device(): theirs = lax.ppermute(mine, ('yh', 'yl', 'c'), cross_route((1,)))  10.1 us
    ppermute x1, starting transfers between devices, on_device(): mine_swapped = lax.ppermute(after(mine, sent), 'c', SWAP)  6.28 us
    all_gather x1, blocking collectives, on_device(): near = lax.all_gather(inputs, 'c', axis=0)  6.23 us
    pallas_call x1, Pallas kernels, col_layer(): pl.pallas_call(col_layer_kernel, out_shape=jax.ShapeDtypeStruct((PARTS, 1...  5.93 us
    unnamed x15, local copies, waits for them, and re-layouts  4.84 us
  transfers between devices with their start and end apart: 7, of which 3 were waited for; matrix products, arithmetic and copies ran while one was open for 3% of the time, Pallas kernels for 6%

profile of v11, /device:TPU:1, one launch (start us, length us, event | category | flops | bytes accessed | tf_op | source)
XLA Modules:
  0.0 126.1 jit_solution(6455353679093755395)
XLA Ops:
  0.0 4.6 %collective-permute-start = (bf16[512,256]{1,0:T(8,128)(2,1)}, bf16[512,256]{1,0:T(8,128)(2,1)}, u32[]{:S(2)}, u32[]{:S(2)}) collective-permute-start(bf16[512,256]{1,0:T(8,128)(2,1)} %source.1), channel_id=1, source_target_pairs={{0,4},{4,8},{8,12},{12,16},{16,20},{20,24},{24,28},{28,32},{32,36}... | collective-permute-start | bytes 786440 | tf_op jit(solution)/shard_map/ppermute | solution.py:294
  4.6 6.2 %all-gather = bf16[1024,256]{1,0:T(8,128)(2,1)S(1)} all-gather(bf16[512,256]{1,0:T(8,128)(2,1)} %source.1), channel_id=2, replica_groups=mesh['yh'=4,'z'=8,'x'=4,'yl'=2,'c'=2] {'c'}, dimensions={0}, use_global_device_ids=true | all-gather | bytes 786432 | tf_op jit(solution)/shard_map/all_gather | solution.py:295
  10.9 1.4 %copy-done = bf16[1024,3,256]{2,0,1:T(8,128)(2,1)S(1)} copy-done((bf16[1024,3,256]{2,0,1:T(8,128)(2,1)S(1)}, bf16[1024,3,256]{2,0,1:T(8,128)(2,1)}, u32[]{:S(2)}) %copy-start) | copy-done | bytes 1572888
  12.3 1.0 copy-done.2
  13.3 1.0 copy-done.3
  15.3 1.9 %collective-permute-start.1 = (bf16[512,256]{1,0:T(8,128)(2,1)S(1)}, bf16[512,256]{1,0:T(8,128)(2,1)}, u32[]{:S(2)}, u32[]{:S(2)}) collective-permute-start(bf16[512,256]{1,0:T(8,128)(2,1)S(1)} %copy-done.1), channel_id=1, source_target_pairs={{0,2},{2,0},{1,3},{3,1},{4,6},{6,4},{5,7},{7,5},{8,10},{10,8},{9,1... | collective-permute-start | bytes 786440 | tf_op jit(solution)/shard_map/ppermute | solution.py:297
  17.3 1.6 %broadcast_multiply_fusion.weight = bf16[3,4,256,256]{3,2,1,0:T(8,128)(2,1)S(1)} fusion(bf16[3,4,256,256]{3,2,1,0:T(8,128)(2,1)} %bitcast.28, bf16[3]{0:T(256)(128)(2,1)S(1)} %copy-done.6), kind=kLoop, calls=%fused_computation | loop fusion | flops 786432 | bytes 3145734 | tf_op jit(solution)/shard_map/mul | solution.py:292
  18.9 3.4 %collective-permute-start.2 = (bf16[512,256]{1,0:T(8,128)(2,1)}, bf16[512,256]{1,0:T(8,128)(2,1)S(1)}, u32[]{:S(2)}, u32[]{:S(2)}) collective-permute-start(bf16[512,256]{1,0:T(8,128)(2,1)} %collective-permute-done), channel_id=1, source_target_pairs={{0,2},{2,0},{1,3},{3,1},{4,6},{6,4},{5,7},{7,5},{8,10},{10,8},{9,1... | collective-permute-start | bytes 786440 | tf_op jit(solution)/shard_map/ppermute | solution.py:299
  22.3 2.5 %collective-permute-done.1 = bf16[512,256]{1,0:T(8,128)(2,1)} collective-permute-done((bf16[512,256]{1,0:T(8,128)(2,1)S(1)}, bf16[512,256]{1,0:T(8,128)(2,1)}, u32[]{:S(2)}, u32[]{:S(2)}) %collective-permute-start.1) | collective-permute-done | bytes 262176 | tf_op jit(solution)/shard_map/ppermute | solution.py:297
  24.8 4.0 %all-gather.1 = bf16[1024,256]{1,0:T(8,128)(2,1)S(1)} all-gather(bf16[512,256]{1,0:T(8,128)(2,1)} %collective-permute-done.1), channel_id=3, replica_groups=mesh['yh'=4,'z'=8,'x'=4,'yl'=2,'c'=2] {'c'}, dimensions={0}, use_global_device_ids=true | all-gather | bytes 786432 | tf_op jit(solution)/shard_map/all_gather | solution.py:300
  28.8 2.4 %all-gather.2 = bf16[1024,256]{1,0:T(8,128)(2,1)S(1)} all-gather(bf16[512,256]{1,0:T(8,128)(2,1)} %collective-permute-done), channel_id=4, replica_groups=mesh['yh'=4,'z'=8,'x'=4,'yl'=2,'c'=2] {'c'}, dimensions={0}, use_global_device_ids=true | all-gather | bytes 786432 | tf_op jit(solution)/shard_map/all_gather | solution.py:301
  31.2 3.2 %row_own.1 = (bf16[512,256]{1,0:T(8,128)(2,1)S(1)}, f32[512,256]{1,0:T(8,128)S(1)}, f32[512,256]{1,0:T(8,128)S(1)}, f32[512,256]{1,0:T(8,128)S(1)}) custom-call(s32[4]{0:T(128)S(1)} %pad_add_fusion.place, bf16[2,512,256]{2,1,0:T(8,128)(2,1)S(1)} %bitcast.22, bf16[2,512,256]{2,1,0:T(8,128)(2,1)S(1)} %bitcast.23, f32[4,1,256]{2,1,0:T(1,128)S(1)} %bitcast.25, ...), custom_call_target="tpu_custom_call" | custom-call | flops 1 | bytes 1 | tf_op jit(solution)/shard_map/row_own/pallas_call | solution.py:102
  34.4 10.1 %collective-permute-start.4 = (bf16[5120,256]{1,0:T(8,128)(2,1)S(1)}, bf16[5120,256]{1,0:T(8,128)(2,1)}, u32[]{:S(2)}, u32[]{:S(2)}) collective-permute-start(bf16[5120,256]{1,0:T(8,128)(2,1)S(1)} %pack_weights.1.weights.w0), channel_id=1, source_target_pairs={{2,0},{0,2},{3,129},{129,3},{130,128},{128,130},{131,257},{257,131... | collective-permute-start | bytes 7864328 | tf_op jit(solution)/shard_map/ppermute | solution.py:307
  44.5 2.2 %all-gather.3 = bf16[1024,256]{1,0:T(8,128)(2,1)S(1)} all-gather(bf16[512,256]{1,0:T(8,128)(2,1)S(1)} %collective-permute-done.2), channel_id=5, replica_groups=mesh['yh'=4,'z'=8,'x'=4,'yl'=2,'c'=2] {'c'}, dimensions={0}, use_global_device_ids=true | all-gather | bytes 786432 | tf_op jit(solution)/shard_map/all_gather | solution.py:304
  46.7 3.3 %row_halo.1 = bf16[512,512]{1,0:T(8,128)(2,1)S(1)} custom-call(s32[4]{0:T(128)S(1)} %pad_add_fusion.place, bf16[2,512,256]{2,1,0:T(8,128)(2,1)S(1)} %bitcast.20, bf16[2,512,256]{2,1,0:T(8,128)(2,1)S(1)} %bitcast.21, f32[4,1,256]{2,1,0:T(1,128)S(1)} %bitcast.26, bf16[3,4,256,256]{3,2,1,0:T(8,128)(2,1)S(1)} %broadcast_multiply_fusion.weight, ...), custom_call_target="tpu_custom_call" | custom-call | flops 1 | bytes 1 | tf_op jit(solution)/shard_map/row_halo/pallas_call | solution.py:145
  50.1 1.0 reshape.28
  51.0 11.2 %all-to-all-start = ((bf16[512,4,128]{2,1,0:T(4,128)(2,1)}), bf16[512,4,128]{2,1,0:T(4,128)(2,1)}, u32[]{:S(2)}, u32[]{:S(2)}) async-start(bf16[512,4,128]{2,1,0:T(4,128)(2,1)} %reshape.28), calls=%async_computation | async-start | bytes 1048576 | tf_op jit(solution)/shard_map/all_to_all | solution.py:311
  62.2 6.3 %collective-permute-start.3 = (bf16[5120,256]{1,0:T(8,128)(2,1)S(1)}, bf16[5120,256]{1,0:T(8,128)(2,1)}, u32[]{:S(2)}, u32[]{:S(2)}) collective-permute-start(bf16[5120,256]{1,0:T(8,128)(2,1)S(1)} %pack_weights.1.weights.w0), channel_id=1, source_target_pairs={{0,1},{1,0},{2,3},{3,2},{4,5},{5,4},{6,7},{7,6},{8,9},{9,8},{10,11... | collective-permute-start | bytes 7864328 | tf_op jit(solution)/shard_map/ppermute | solution.py:309
  68.5 13.7 %collective-permute-done.4.w2 = bf16[5120,256]{1,0:T(8,128)(2,1)} collective-permute-done((bf16[5120,256]{1,0:T(8,128)(2,1)S(1)}, bf16[5120,256]{1,0:T(8,128)(2,1)}, u32[]{:S(2)}, u32[]{:S(2)}) %collective-permute-start.4) | collective-permute-done | bytes 2621472 | tf_op jit(solution)/shard_map/ppermute | solution.py:307
  82.2 2.1 %collective-permute-start.5 = (bf16[5120,256]{1,0:T(8,128)(2,1)}, bf16[5120,256]{1,0:T(8,128)(2,1)}, u32[]{:S(2)}, u32[]{:S(2)}) collective-permute-start(bf16[5120,256]{1,0:T(8,128)(2,1)} %collective-permute-done.4.w2), channel_id=1, source_target_pairs={{0,1},{1,0},{2,3},{3,2},{4,5},{5,4},{6,7},{7,6},{8,9},{9,8},{10,11... | collective-permute-start | bytes 7864328 | tf_op jit(solution)/shard_map/ppermute | solution.py:313
  84.3 4.0 %all-to-all-done = bf16[512,4,128]{2,1,0:T(4,128)(2,1)} async-done(((bf16[512,4,128]{2,1,0:T(4,128)(2,1)}), bf16[512,4,128]{2,1,0:T(4,128)(2,1)}, u32[]{:S(2)}, u32[]{:S(2)}) %all-to-all-start) | async-done | bytes 524320 | tf_op jit(solution)/shard_map/all_to_all | solution.py:311
  88.3 1.2 reshape.29.moved
  90.4 5.9 %col_layer.1 = bf16[4,128,256]{2,1,0:T(8,128)(2,1)S(1)} custom-call(s32[4]{0:T(128)S(1)} %pad_add_fusion.place, bf16[4,128,512]{2,1,0:T(8,128)(2,1)S(1)} %reshape.29.moved, f32[4,128,256]{2,1,0:T(8,128)S(1)} %row_output.1.partial, f32[4,1,256]{2,1,0:T(1,128)S(1)} %bitcast.27, bf16[5120,256]{1,0:T(8,128)(2,1)S(1)} %pack_weights.1.weights.w0, ...), custom_call_target="tpu_custom_call" | custom-call | flops 1 | bytes 1 | tf_op jit(solution)/shard_map/col_layer/pallas_call | solution.py:254
  96.5 28.9 %all_to_all.10 = bf16[512,2,128]{2,1,0:T(2,128)(2,1)S(1)} all-to-all(bf16[512,2,128]{2,1,0:T(2,128)(2,1)S(1)} %reshape.31), channel_id=1, replica_groups=mesh['yh'=4,'z'=8,'x'=4,'yl'=2,'c'=2] {'yl','c','yh','z','x'}, dimensions={0} | all-to-all | bytes 524288 | tf_op jit(solution)/shard_map/all_to_all | solution.py:322
  (20 shorter events, 2.7 us)
Async XLA Ops:
  0.0 18.9 %collective-permute-start = (bf16[512,256]{1,0:T(8,128)(2,1)}, bf16[512,256]{1,0:T(8,128)(2,1)}, u32[]{:S(2)}, u32[]{:S(2)}) collective-permute-start(bf16[512,256]{1,0:T(8,128)(2,1)} %source.1), channel_id=1, source_target_pairs={{0,4},{4,8},{8,12},{12,16},{16,20},{20,24},{24,28},{28,32},{32,36}... | collective-permute-start | bytes 786440 | tf_op jit(solution)/shard_map/ppermute | solution.py:294
  10.9 1.4 %copy-start = (bf16[1024,3,256]{2,0,1:T(8,128)(2,1)S(1)}, bf16[1024,3,256]{2,0,1:T(8,128)(2,1)}, u32[]{:S(2)}) copy-start(bf16[1024,3,256]{2,0,1:T(8,128)(2,1)} %param.13) | copy-start | bytes 4718596
  12.3 1.0 copy-start.2
  13.3 1.0 copy-start.3
  14.4 0.9 copy-start.1
  14.4 3.0 %copy-start.6 = (bf16[3]{0:T(256)(128)(2,1)S(1)}, bf16[3]{0:T(256)(128)(2,1)}, u32[]{:S(2)}) copy-start(bf16[3]{0:T(256)(128)(2,1)} %constant.30.clone) | copy-start | bytes 22
  15.3 9.5 %collective-permute-start.1 = (bf16[512,256]{1,0:T(8,128)(2,1)S(1)}, bf16[512,256]{1,0:T(8,128)(2,1)}, u32[]{:S(2)}, u32[]{:S(2)}) collective-permute-start(bf16[512,256]{1,0:T(8,128)(2,1)S(1)} %copy-done.1), channel_id=1, source_target_pairs={{0,2},{2,0},{1,3},{3,1},{4,6},{6,4},{5,7},{7,5},{8,10},{10,8},{9,1... | collective-permute-start | bytes 786440 | tf_op jit(solution)/shard_map/ppermute | solution.py:297
  18.9 12.3 %copy-start.4 = (f32[1024]{0:T(1024)S(1)}, f32[1024]{0:T(1024)}, u32[]{:S(2)}) copy-start(f32[1024]{0:T(1024)} %param.9) | copy-start | bytes 12292
  18.9 15.5 %collective-permute-start.2 = (bf16[512,256]{1,0:T(8,128)(2,1)}, bf16[512,256]{1,0:T(8,128)(2,1)S(1)}, u32[]{:S(2)}, u32[]{:S(2)}) collective-permute-start(bf16[512,256]{1,0:T(8,128)(2,1)} %collective-permute-done), channel_id=1, source_target_pairs={{0,2},{2,0},{1,3},{3,1},{4,6},{6,4},{5,7},{7,5},{8,10},{10,8},{9,1... | collective-permute-start | bytes 786440 | tf_op jit(solution)/shard_map/ppermute | solution.py:299
  34.4 47.8 %collective-permute-start.4 = (bf16[5120,256]{1,0:T(8,128)(2,1)S(1)}, bf16[5120,256]{1,0:T(8,128)(2,1)}, u32[]{:S(2)}, u32[]{:S(2)}) collective-permute-start(bf16[5120,256]{1,0:T(8,128)(2,1)S(1)} %pack_weights.1.weights.w0), channel_id=1, source_target_pairs={{2,0},{0,2},{3,129},{129,3},{130,128},{128,130},{131,257},{257,131... | collective-permute-start | bytes 7864328 | tf_op jit(solution)/shard_map/ppermute | solution.py:307
  51.0 37.3 %all-to-all-start = ((bf16[512,4,128]{2,1,0:T(4,128)(2,1)}), bf16[512,4,128]{2,1,0:T(4,128)(2,1)}, u32[]{:S(2)}, u32[]{:S(2)}) async-start(bf16[512,4,128]{2,1,0:T(4,128)(2,1)} %reshape.28), calls=%async_computation | async-start | bytes 1048576 | tf_op jit(solution)/shard_map/all_to_all | solution.py:311
  62.2 28.2 %collective-permute-start.3 = (bf16[5120,256]{1,0:T(8,128)(2,1)S(1)}, bf16[5120,256]{1,0:T(8,128)(2,1)}, u32[]{:S(2)}, u32[]{:S(2)}) collective-permute-start(bf16[5120,256]{1,0:T(8,128)(2,1)S(1)} %pack_weights.1.weights.w0), channel_id=1, source_target_pairs={{0,1},{1,0},{2,3},{3,2},{4,5},{5,4},{6,7},{7,6},{8,9},{9,8},{10,11... | collective-permute-start | bytes 7864328 | tf_op jit(solution)/shard_map/ppermute | solution.py:309
  82.2 8.2 %collective-permute-start.5 = (bf16[5120,256]{1,0:T(8,128)(2,1)}, bf16[5120,256]{1,0:T(8,128)(2,1)}, u32[]{:S(2)}, u32[]{:S(2)}) collective-permute-start(bf16[5120,256]{1,0:T(8,128)(2,1)} %collective-permute-done.4.w2), channel_id=1, source_target_pairs={{0,1},{1,0},{2,3},{3,2},{4,5},{5,4},{6,7},{7,6},{8,9},{9,8},{10,11... | collective-permute-start | bytes 7864328 | tf_op jit(solution)/shard_map/ppermute | solution.py:313
  89.6 0.9 copy-start.5

commit v12 on v11

--- a/solution.py
+++ b/solution.py
@@ -160,12 +160,13 @@
 LONG = 2*10**10
 
 
-def pack_kernel(row_out, col_qkv, col_out, packed, sem):
-    pairs = [(col_qkv, packed.at[QKV_AT:OUT_AT])]
-    for source, at in ((row_out, 0), (col_out, OUT_AT)):
-        for n in range(PARTS):
-            rows = slice(at + n * GROUP, at + (n + 1) * GROUP)
-            pairs.append((source.at[:, n * GROUP : (n + 1) * GROUP], packed.at[rows]))
+def pack_kernel(row_out, col_qkv, col_out, packed, main, last, sem):
+    pairs = [(col_qkv, packed.at[QKV_AT:OUT_AT]), (col_qkv, main.at[QKV_AT:OUT_AT])]
+    for n in range(PARTS):
+        rows = slice(n * GROUP, (n + 1) * GROUP)
+        pairs += [(row_out.at[:, rows], to.at[rows]) for to in (packed, main)]
+        pairs += [(col_out.at[:, rows], last.at[rows])]
+        pairs += [(col_out.at[:, rows], packed.at[OUT_AT + n * GROUP : OUT_AT + (n + 1) * GROUP])]
     copies = [pltpu.make_async_copy(a, b, sem.at[i]) for i, (a, b) in enumerate(pairs)]
     for copy in copies:
         copy.start()
@@ -176,10 +177,10 @@
 def pack_weights(row_out, col_qkv, col_out):
     return pl.pallas_call(
         pack_kernel,
-        out_shape=jax.ShapeDtypeStruct((WEIGHT_ROWS, GROUP), jnp.bfloat16),
+        out_shape=[jax.ShapeDtypeStruct((n, GROUP), jnp.bfloat16) for n in (WEIGHT_ROWS, OUT_AT, WEIGHT_ROWS - OUT_AT)],
         in_specs=[ANY] * 3,
-        out_specs=ANY,
-        scratch_shapes=[pltpu.SemaphoreType.DMA((2 * PARTS + 1,))],
+        out_specs=[ANY] * 3,
+        scratch_shapes=[pltpu.SemaphoreType.DMA((4 * PARTS + 2,))],
         compiler_params=pltpu.CompilerParams(vmem_limit_bytes=MIB),
         cost_estimate=pl.CostEstimate(flops=1, bytes_accessed=1, transcendentals=0),
         name="pack_weights",
@@ -212,11 +213,18 @@
     )(place, moved, weights)
 
 
-def col_layer_kernel(place, moved, partial, gain, w0, w1, w2, w3, out, held, last, sem):
+def col_layer_kernel(place, moved, partial, gain, w0, w1, w2, w3, out2, out3, out, held, last, sem):
     arrays = (w0, w1, w2, w3)
     first = [pltpu.make_async_copy(w.at[:QKV_AT], last.at[i], sem.at[PARTS + i]) for i, w in enumerate(arrays[1:])]
-    rest = [pltpu.make_async_copy(w.at[QKV_AT:], held.at[i], sem.at[i]) for i, w in enumerate(arrays)]
-    for copy in first + rest:
+    rest = [
+        pltpu.make_async_copy(w.at[QKV_AT:], held.at[i] if i < 2 else held.at[i, : OUT_AT - QKV_AT], sem.at[i])
+        for i, w in enumerate(arrays)
+    ]
+    ends = [
+        pltpu.make_async_copy(w, held.at[2 + i, OUT_AT - QKV_AT :], sem.at[2 * PARTS - 1 + i])
+        for i, w in enumerate((out2, out3))
+    ]
+    for copy in first + rest + ends:
         copy.start()
     atts = [moved[g, :, :GROUP] for g in weight_groups(place)[1:]]
     for copy in first:
@@ -244,6 +252,8 @@
         for head in range(1, HEADS_HERE):
             att = jnp.where(head_mask(rows, head), acc[head * rows : (head + 1) * rows], att)
         atts.append(att.astype(jnp.bfloat16))
+    for copy in ends:
+        copy.wait()
     for n in range(PARTS):
         at = OUT_AT - QKV_AT + n * GROUP
         total = sum(dot(a, held[i, at : at + GROUP, :]) for i, a in enumerate(atts))
@@ -254,12 +264,12 @@
     return pl.pallas_call(
         col_layer_kernel,
         out_shape=jax.ShapeDtypeStruct((PARTS, 128, GROUP), jnp.bfloat16),
-        in_specs=[SMEM, VMEM, VMEM, VMEM] + [ANY] * 4,
+        in_specs=[SMEM, VMEM, VMEM, VMEM] + [ANY] * 6,
         out_specs=VMEM,
         scratch_shapes=[
             pltpu.VMEM((PARTS, WEIGHT_ROWS - QKV_AT, GROUP), jnp.bfloat16),
             pltpu.VMEM((PARTS - 1, QKV_AT, GROUP), jnp.bfloat16),
-            pltpu.SemaphoreType.DMA((2 * PARTS - 1,)),
+            pltpu.SemaphoreType.DMA((2 * PARTS + 1,)),
         ],
         compiler_params=pltpu.CompilerParams(vmem_limit_bytes=20 * MIB),
         cost_estimate=pl.CostEstimate(flops=1, bytes_accessed=1, transcendentals=0),
@@ -293,9 +303,9 @@
 
     before = lax.ppermute(inputs, SEQ, [(i, i + 1) for i in range(127)])
     near = lax.all_gather(inputs, "c", axis=0)
-    mine = pack_weights(row_out, col_qkv.transpose(1, 0, 2).reshape(3 * 1024, GROUP), col_out)
+    mine, main, last = pack_weights(row_out, col_qkv.transpose(1, 0, 2).reshape(3 * 1024, GROUP), col_out)
     other = lax.ppermute(after(inputs, near, mine), "yl", SWAP)
-    mine, row_qkv, before = lax.optimization_barrier((mine, row_qkv, before, near))[:3]
+    mine, main, last, row_qkv, before = lax.optimization_barrier((mine, main, last, row_qkv, before, near))[:5]
     before_other = lax.ppermute(before, "yl", SWAP)
     far = lax.all_gather(after(other, before), "c", axis=0)
     before_near = lax.all_gather(after(before, far), "c", axis=0)
@@ -303,21 +313,23 @@
     state = row_own(place, near, far, row_gain, row_qkv)
     before_far = lax.all_gather(after(before_other, state[0]), "c", axis=0)
 
-    mine = after(mine, before_other, state[0])
-    theirs = lax.ppermute(mine, ("yh", "yl", "c"), cross_route((1,)))
+    main = after(main, before_other, state[0])
+    theirs = lax.ppermute(main, ("yh", "yl", "c"), cross_route((1,)))
     sent = row_halo(place, before_near, before_far, row_gain, row_qkv, state, inputs)
     mine_swapped = lax.ppermute(after(mine, sent), "c", SWAP)
 
     moved = lax.all_to_all(sent.reshape(COLS, 4, 128), HEAD + SEQ, 0, 0, tiled=True)
     moved = moved.reshape(PARTS, 128, 2 * GROUP)
     theirs_swapped = lax.ppermute(after(theirs, sent), "c", SWAP)
+    last_theirs = lax.ppermute(after(last, sent), ("yh", "yl", "c"), cross_route((1,)))
+    last_swapped = lax.ppermute(after(last_theirs, moved), "c", SWAP)
     partial = row_output(place, moved, mine)
     mixed = col_layer(
         place,
         moved,
         partial,
         col_gain.reshape(PARTS, 1, GROUP),
-        [mine, mine_swapped, theirs, theirs_swapped],
+        [mine, mine_swapped, theirs, theirs_swapped, last_theirs, last_swapped],
     )
     mixed = lax.all_to_all(mixed.reshape(COLS, 2, 128), HEAD + SEQ, 0, 0, tiled=True)
     return mixed.reshape(COLS, GROUP)

time: 127 us -> 126 us (level)
  waiting for transfers between devices: 20.2 us -> 13.8 us
  starting transfers between devices: 39.6 us -> 44 us
  Pallas kernels: 13.6 us -> 15 us
    ppermute x1 -> x3, waiting for transfers between devices: 13.7 us -> 5.75 us  [the longest x1 5.04 us: on_device(): theirs = lax.ppermute(main, ('yh', 'yl', 'c'), cross_route((1,)))]
    ppermute x1 -> x3, starting transfers between devices: 10.1 us -> 13.1 us  [the longest x1 8.66 us: on_device(): theirs = lax.ppermute(main, ('yh', 'yl', 'c'), cross_route((1,)))]
    all_to_all x1, waiting for transfers between devices: 4.02 us -> 5.5 us  [on_device(): lax.all_to_all(sent.reshape(COLS, 4, 128), HEAD + SEQ, 0, 0, tiled=True)]
    all_to_all x1, starting transfers between devices: 11.2 us -> 12.7 us  [on_device(): lax.all_to_all(sent.reshape(COLS, 4, 128), HEAD + SEQ, 0, 0, tiled=True)]
    unnamed x15 -> x17, local copies, waits for them, and re-layouts: 4.84 us -> 5.03 us
  transfers between devices with their start and end apart: 7 -> 9, of which waited for: 3 -> 4; matrix products, arithmetic and copies ran while one was open for 3% -> 3% of each run, Pallas kernels for 6% -> 7%
where the time goes in v12:
time: 126 us; the launch traced here: 125 us
  starting transfers between devices  44 us (35%)
  blocking collectives  43.3 us (34%)
  Pallas kernels  15 us (12%)
  waiting for transfers between devices  13.8 us (11%)
  local copies, waits for them, and re-layouts  7.3 us (6%)
  other arithmetic  1.66 us (1%)
    all_to_all x1, blocking collectives, on_device(): lax.all_to_all(mixed.reshape(COLS, 2, 128), HEAD + SEQ, 0, 0, tiled=True)  28.5 us
    all_to_all x1, starting transfers between devices, on_device(): lax.all_to_all(sent.reshape(COLS, 4, 128), HEAD + SEQ, 0, 0, tiled=True)  12.7 us
    ppermute x1, starting transfers between devices, on_device(): theirs = lax.ppermute(main, ('yh', 'yl', 'c'), cross_route((1,)))  8.66 us
    ppermute x1, starting transfers between devices, on_device(): mine_swapped = lax.ppermute(after(mine, sent), 'c', SWAP)  6.28 us
    all_gather x1, blocking collectives, on_device(): near = lax.all_gather(inputs, 'c', axis=0)  6.23 us
    pallas_call x1, Pallas kernels, col_layer(): pl.pallas_call(col_layer_kernel, out_shape=jax.ShapeDtypeStruct((PARTS, 1...  6.11 us
    all_to_all x1, waiting for transfers between devices, on_device(): lax.all_to_all(sent.reshape(COLS, 4, 128), HEAD + SEQ, 0, 0, tiled=True)  5.5 us
    ppermute x1, waiting for transfers between devices, on_device(): theirs = lax.ppermute(main, ('yh', 'yl', 'c'), cross_route((1,)))  5.04 us
  transfers between devices with their start and end apart: 9, of which 4 were waited for; matrix products, arithmetic and copies ran while one was open for 3% of the time, Pallas kernels for 7%

profile of v12, /device:TPU:1, one launch (start us, length us, event | category | flops | bytes accessed | tf_op | source)
XLA Modules:
  0.0 125.3 jit_solution(10573584121233921356)
XLA Ops:
  0.0 4.8 %collective-permute-start = (bf16[512,256]{1,0:T(8,128)(2,1)}, bf16[512,256]{1,0:T(8,128)(2,1)}, u32[]{:S(2)}, u32[]{:S(2)}) collective-permute-start(bf16[512,256]{1,0:T(8,128)(2,1)} %source.1), channel_id=1, source_target_pairs={{0,4},{4,8},{8,12},{12,16},{16,20},{20,24},{24,28},{28,32},{32,36}... | collective-permute-start | bytes 786440 | tf_op jit(solution)/shard_map/ppermute | solution.py:304
  4.8 6.2 %all-gather = bf16[1024,256]{1,0:T(8,128)(2,1)S(1)} all-gather(bf16[512,256]{1,0:T(8,128)(2,1)} %source.1), channel_id=2, replica_groups=mesh['yh'=4,'z'=8,'x'=4,'yl'=2,'c'=2] {'c'}, dimensions={0}, use_global_device_ids=true | all-gather | bytes 786432 | tf_op jit(solution)/shard_map/all_gather | solution.py:305
  11.0 1.4 %copy-done = bf16[1024,3,256]{2,0,1:T(8,128)(2,1)S(1)} copy-done((bf16[1024,3,256]{2,0,1:T(8,128)(2,1)S(1)}, bf16[1024,3,256]{2,0,1:T(8,128)(2,1)}, u32[]{:S(2)}) %copy-start) | copy-done | bytes 1572888
  14.5 1.6 %pack_weights.1 = (bf16[5120,256]{1,0:T(8,128)(2,1)S(1)}, bf16[4096,256]{1,0:T(8,128)(2,1)}, bf16[1024,256]{1,0:T(8,128)(2,1)S(1)}) custom-call(bf16[256,1024]{1,0:T(8,128)(2,1)S(1)} %copy-done.2, bf16[3072,256]{1,0:T(8,128)(2,1)S(1)} %bitcast.24, bf16[256,1024]{1,0:T(8,128)(2,1)S(1)} %copy-done.3), custom_call_target="tpu_custom_call" | custom-call | flops 1 | bytes 1 | tf_op jit(solution)/shard_map/pack_weights/pallas_call | solution.py:178
  16.9 1.9 %collective-permute-start.1 = (bf16[512,256]{1,0:T(8,128)(2,1)S(1)}, bf16[512,256]{1,0:T(8,128)(2,1)}, u32[]{:S(2)}, u32[]{:S(2)}) collective-permute-start(bf16[512,256]{1,0:T(8,128)(2,1)S(1)} %copy-done.1), channel_id=1, source_target_pairs={{0,2},{2,0},{1,3},{3,1},{4,6},{6,4},{5,7},{7,5},{8,10},{10,8},{9,1... | collective-permute-start | bytes 786440 | tf_op jit(solution)/shard_map/ppermute | solution.py:307
  18.9 1.6 %broadcast_multiply_fusion.weight = bf16[3,4,256,256]{3,2,1,0:T(8,128)(2,1)S(1)} fusion(bf16[3,4,256,256]{3,2,1,0:T(8,128)(2,1)} %bitcast.28, bf16[3]{0:T(256)(128)(2,1)S(1)} %copy-done.7), kind=kLoop, calls=%fused_computation | loop fusion | flops 786432 | bytes 3145734 | tf_op jit(solution)/shard_map/mul | solution.py:302
  20.5 3.4 %collective-permute-start.2 = (bf16[512,256]{1,0:T(8,128)(2,1)}, bf16[512,256]{1,0:T(8,128)(2,1)S(1)}, u32[]{:S(2)}, u32[]{:S(2)}) collective-permute-start(bf16[512,256]{1,0:T(8,128)(2,1)} %collective-permute-done), channel_id=1, source_target_pairs={{0,2},{2,0},{1,3},{3,1},{4,6},{6,4},{5,7},{7,5},{8,10},{10,8},{9,1... | collective-permute-start | bytes 786440 | tf_op jit(solution)/shard_map/ppermute | solution.py:309
  23.9 2.5 %collective-permute-done.1 = bf16[512,256]{1,0:T(8,128)(2,1)} collective-permute-done((bf16[512,256]{1,0:T(8,128)(2,1)S(1)}, bf16[512,256]{1,0:T(8,128)(2,1)}, u32[]{:S(2)}, u32[]{:S(2)}) %collective-permute-start.1) | collective-permute-done | bytes 262176 | tf_op jit(solution)/shard_map/ppermute | solution.py:307
  26.4 4.0 %all-gather.1 = bf16[1024,256]{1,0:T(8,128)(2,1)S(1)} all-gather(bf16[512,256]{1,0:T(8,128)(2,1)} %collective-permute-done.1), channel_id=3, replica_groups=mesh['yh'=4,'z'=8,'x'=4,'yl'=2,'c'=2] {'c'}, dimensions={0}, use_global_device_ids=true | all-gather | bytes 786432 | tf_op jit(solution)/shard_map/all_gather | solution.py:310
  30.4 2.4 %all-gather.2 = bf16[1024,256]{1,0:T(8,128)(2,1)S(1)} all-gather(bf16[512,256]{1,0:T(8,128)(2,1)} %collective-permute-done), channel_id=4, replica_groups=mesh['yh'=4,'z'=8,'x'=4,'yl'=2,'c'=2] {'c'}, dimensions={0}, use_global_device_ids=true | all-gather | bytes 786432 | tf_op jit(solution)/shard_map/all_gather | solution.py:311
  32.8 3.2 %row_own.1 = (bf16[512,256]{1,0:T(8,128)(2,1)S(1)}, f32[512,256]{1,0:T(8,128)S(1)}, f32[512,256]{1,0:T(8,128)S(1)}, f32[512,256]{1,0:T(8,128)S(1)}) custom-call(s32[4]{0:T(128)S(1)} %pad_add_fusion.place, bf16[2,512,256]{2,1,0:T(8,128)(2,1)S(1)} %bitcast.22, bf16[2,512,256]{2,1,0:T(8,128)(2,1)S(1)} %bitcast.23, f32[4,1,256]{2,1,0:T(1,128)S(1)} %bitcast.25, ...), custom_call_target="tpu_custom_call" | custom-call | flops 1 | bytes 1 | tf_op jit(solution)/shard_map/row_own/pallas_call | solution.py:102
  36.0 8.7 %collective-permute-start.4 = (bf16[4096,256]{1,0:T(8,128)(2,1)}, bf16[4096,256]{1,0:T(8,128)(2,1)}, u32[]{:S(2)}, u32[]{:S(2)}) collective-permute-start(bf16[4096,256]{1,0:T(8,128)(2,1)} %get-tuple-element.44), channel_id=1, source_target_pairs={{2,0},{0,2},{3,129},{129,3},{130,128},{128,130},{131,257},{257,131... | collective-permute-start | bytes 6291464 | tf_op jit(solution)/shard_map/ppermute | solution.py:317
  44.7 2.2 %all-gather.3 = bf16[1024,256]{1,0:T(8,128)(2,1)S(1)} all-gather(bf16[512,256]{1,0:T(8,128)(2,1)S(1)} %collective-permute-done.2), channel_id=5, replica_groups=mesh['yh'=4,'z'=8,'x'=4,'yl'=2,'c'=2] {'c'}, dimensions={0}, use_global_device_ids=true | all-gather | bytes 786432 | tf_op jit(solution)/shard_map/all_gather | solution.py:314
  46.9 3.3 %row_halo.1 = bf16[512,512]{1,0:T(8,128)(2,1)S(1)} custom-call(s32[4]{0:T(128)S(1)} %pad_add_fusion.place, bf16[2,512,256]{2,1,0:T(8,128)(2,1)S(1)} %bitcast.20, bf16[2,512,256]{2,1,0:T(8,128)(2,1)S(1)} %bitcast.21, f32[4,1,256]{2,1,0:T(1,128)S(1)} %bitcast.26, bf16[3,4,256,256]{3,2,1,0:T(8,128)(2,1)S(1)} %broadcast_multiply_fusion.weight, ...), custom_call_target="tpu_custom_call" | custom-call | flops 1 | bytes 1 | tf_op jit(solution)/shard_map/row_halo/pallas_call | solution.py:145
  51.2 12.7 %all-to-all-start = ((bf16[512,4,128]{2,1,0:T(4,128)(2,1)}), bf16[512,4,128]{2,1,0:T(4,128)(2,1)}, u32[]{:S(2)}, u32[]{:S(2)}) async-start(bf16[512,4,128]{2,1,0:T(4,128)(2,1)} %reshape.28), calls=%async_computation | async-start | bytes 1048576 | tf_op jit(solution)/shard_map/all_to_all | solution.py:321
  63.8 6.3 %collective-permute-start.3 = (bf16[5120,256]{1,0:T(8,128)(2,1)S(1)}, bf16[5120,256]{1,0:T(8,128)(2,1)}, u32[]{:S(2)}, u32[]{:S(2)}) collective-permute-start(bf16[5120,256]{1,0:T(8,128)(2,1)S(1)} %get-tuple-element.42.weights.w0), channel_id=1, source_target_pairs={{0,1},{1,0},{2,3},{3,2},{4,5},{5,4},{6,7},{7,6},{8,9},{9,8},{10,11... | collective-permute-start | bytes 7864328 | tf_op jit(solution)/shard_map/ppermute | solution.py:319
  70.1 1.9 %collective-permute-start.6 = (bf16[1024,256]{1,0:T(8,128)(2,1)}, bf16[1024,256]{1,0:T(8,128)(2,1)}, u32[]{:S(2)}, u32[]{:S(2)}) collective-permute-start(bf16[1024,256]{1,0:T(8,128)(2,1)} %copy-done.6), channel_id=1, source_target_pairs={{2,0},{0,2},{3,129},{129,3},{130,128},{128,130},{131,257},{257,131... | collective-permute-start | bytes 1572872 | tf_op jit(solution)/shard_map/ppermute | solution.py:324
  72.0 5.0 %collective-permute-done.4.w2 = bf16[4096,256]{1,0:T(8,128)(2,1)} collective-permute-done((bf16[4096,256]{1,0:T(8,128)(2,1)}, bf16[4096,256]{1,0:T(8,128)(2,1)}, u32[]{:S(2)}, u32[]{:S(2)}) %collective-permute-start.4) | collective-permute-done | bytes 2097184 | tf_op jit(solution)/shard_map/ppermute | solution.py:317
  77.1 1.9 %collective-permute-start.5 = (bf16[4096,256]{1,0:T(8,128)(2,1)}, bf16[4096,256]{1,0:T(8,128)(2,1)}, u32[]{:S(2)}, u32[]{:S(2)}) collective-permute-start(bf16[4096,256]{1,0:T(8,128)(2,1)} %collective-permute-done.4.w2), channel_id=1, source_target_pairs={{0,1},{1,0},{2,3},{3,2},{4,5},{5,4},{6,7},{7,6},{8,9},{9,8},{10,11... | collective-permute-start | bytes 6291464 | tf_op jit(solution)/shard_map/ppermute | solution.py:323
  79.0 5.5 %all-to-all-done = bf16[512,4,128]{2,1,0:T(4,128)(2,1)} async-done(((bf16[512,4,128]{2,1,0:T(4,128)(2,1)}), bf16[512,4,128]{2,1,0:T(4,128)(2,1)}, u32[]{:S(2)}, u32[]{:S(2)}) %all-to-all-start) | async-done | bytes 524320 | tf_op jit(solution)/shard_map/all_to_all | solution.py:321
  84.5 1.2 reshape.29.moved
  85.8 2.5 %collective-permute-start.7 = (bf16[1024,256]{1,0:T(8,128)(2,1)}, bf16[1024,256]{1,0:T(8,128)(2,1)S(1)}, u32[]{:S(2)}, u32[]{:S(2)}) collective-permute-start(bf16[1024,256]{1,0:T(8,128)(2,1)} %collective-permute-done.6.out2), channel_id=1, source_target_pairs={{0,1},{1,0},{2,3},{3,2},{4,5},{5,4},{6,7},{7,6},{8,9},{9,8},{10,11... | collective-permute-start | bytes 1572872 | tf_op jit(solution)/shard_map/ppermute | solution.py:325
  89.8 6.1 %col_layer.1 = bf16[4,128,256]{2,1,0:T(8,128)(2,1)S(1)} custom-call(s32[4]{0:T(128)S(1)} %pad_add_fusion.place, bf16[4,128,512]{2,1,0:T(8,128)(2,1)S(1)} %reshape.29.moved, f32[4,128,256]{2,1,0:T(8,128)S(1)} %row_output.1.partial, f32[4,1,256]{2,1,0:T(1,128)S(1)} %bitcast.27, bf16[5120,256]{1,0:T(8,128)(2,1)S(1)} %get-tuple-element.42.weights.w0, ...), custom_call_target="tpu_custom_call" | custom-call | flops 1 | bytes 1 | tf_op jit(solution)/shard_map/col_layer/pallas_call | solution.py:264
  96.0 28.5 %all_to_all.10 = bf16[512,2,128]{2,1,0:T(2,128)(2,1)S(1)} all-to-all(bf16[512,2,128]{2,1,0:T(2,128)(2,1)S(1)} %reshape.31), channel_id=1, replica_groups=mesh['yh'=4,'z'=8,'x'=4,'yl'=2,'c'=2] {'yl','c','yh','z','x'}, dimensions={0} | all-to-all | bytes 524288 | tf_op jit(solution)/shard_map/all_to_all | solution.py:334
  (26 shorter events, 6.3 us)
Async XLA Ops:
  0.0 18.9 %copy-start.7 = (bf16[3]{0:T(256)(128)(2,1)S(1)}, bf16[3]{0:T(256)(128)(2,1)}, u32[]{:S(2)}) copy-start(bf16[3]{0:T(256)(128)(2,1)} %constant.30.clone) | copy-start | bytes 22
  0.0 16.9 %copy-start.1 = (bf16[512,256]{1,0:T(8,128)(2,1)S(1)}, bf16[512,256]{1,0:T(8,128)(2,1)}, u32[]{:S(2)}) copy-start(bf16[512,256]{1,0:T(8,128)(2,1)} %source.1) | copy-start | bytes 786436
  0.0 20.5 %collective-permute-start = (bf16[512,256]{1,0:T(8,128)(2,1)}, bf16[512,256]{1,0:T(8,128)(2,1)}, u32[]{:S(2)}, u32[]{:S(2)}) collective-permute-start(bf16[512,256]{1,0:T(8,128)(2,1)} %source.1), channel_id=1, source_target_pairs={{0,4},{4,8},{8,12},{12,16},{16,20},{20,24},{24,28},{28,32},{32,36}... | collective-permute-start | bytes 786440 | tf_op jit(solution)/shard_map/ppermute | solution.py:304
  11.0 1.4 %copy-start = (bf16[1024,3,256]{2,0,1:T(8,128)(2,1)S(1)}, bf16[1024,3,256]{2,0,1:T(8,128)(2,1)}, u32[]{:S(2)}) copy-start(bf16[1024,3,256]{2,0,1:T(8,128)(2,1)} %param.13) | copy-start | bytes 4718596
  12.4 1.0 copy-start.2
  13.5 1.0 copy-start.3
  16.1 0.8 copy-start.6
  16.9 9.5 %collective-permute-start.1 = (bf16[512,256]{1,0:T(8,128)(2,1)S(1)}, bf16[512,256]{1,0:T(8,128)(2,1)}, u32[]{:S(2)}, u32[]{:S(2)}) collective-permute-start(bf16[512,256]{1,0:T(8,128)(2,1)S(1)} %copy-done.1), channel_id=1, source_target_pairs={{0,2},{2,0},{1,3},{3,1},{4,6},{6,4},{5,7},{7,5},{8,10},{10,8},{9,1... | collective-permute-start | bytes 786440 | tf_op jit(solution)/shard_map/ppermute | solution.py:307
  20.5 12.3 %copy-start.4 = (f32[1024]{0:T(1024)S(1)}, f32[1024]{0:T(1024)}, u32[]{:S(2)}) copy-start(f32[1024]{0:T(1024)} %param.9) | copy-start | bytes 12292
  20.5 15.5 %collective-permute-start.2 = (bf16[512,256]{1,0:T(8,128)(2,1)}, bf16[512,256]{1,0:T(8,128)(2,1)S(1)}, u32[]{:S(2)}, u32[]{:S(2)}) collective-permute-start(bf16[512,256]{1,0:T(8,128)(2,1)} %collective-permute-done), channel_id=1, source_target_pairs={{0,2},{2,0},{1,3},{3,1},{4,6},{6,4},{5,7},{7,5},{8,10},{10,8},{9,1... | collective-permute-start | bytes 786440 | tf_op jit(solution)/shard_map/ppermute | solution.py:309
  36.0 41.1 %collective-permute-start.4 = (bf16[4096,256]{1,0:T(8,128)(2,1)}, bf16[4096,256]{1,0:T(8,128)(2,1)}, u32[]{:S(2)}, u32[]{:S(2)}) collective-permute-start(bf16[4096,256]{1,0:T(8,128)(2,1)} %get-tuple-element.44), channel_id=1, source_target_pairs={{2,0},{0,2},{3,129},{129,3},{130,128},{128,130},{131,257},{257,131... | collective-permute-start | bytes 6291464 | tf_op jit(solution)/shard_map/ppermute | solution.py:317
  51.2 33.4 %all-to-all-start = ((bf16[512,4,128]{2,1,0:T(4,128)(2,1)}), bf16[512,4,128]{2,1,0:T(4,128)(2,1)}, u32[]{:S(2)}, u32[]{:S(2)}) async-start(bf16[512,4,128]{2,1,0:T(4,128)(2,1)} %reshape.28), calls=%async_computation | async-start | bytes 1048576 | tf_op jit(solution)/shard_map/all_to_all | solution.py:321
  63.8 26.0 %collective-permute-start.3 = (bf16[5120,256]{1,0:T(8,128)(2,1)S(1)}, bf16[5120,256]{1,0:T(8,128)(2,1)}, u32[]{:S(2)}, u32[]{:S(2)}) collective-permute-start(bf16[5120,256]{1,0:T(8,128)(2,1)S(1)} %get-tuple-element.42.weights.w0), channel_id=1, source_target_pairs={{0,1},{1,0},{2,3},{3,2},{4,5},{5,4},{6,7},{7,6},{8,9},{9,8},{10,11... | collective-permute-start | bytes 7864328 | tf_op jit(solution)/shard_map/ppermute | solution.py:319
  70.1 15.6 %collective-permute-start.6 = (bf16[1024,256]{1,0:T(8,128)(2,1)}, bf16[1024,256]{1,0:T(8,128)(2,1)}, u32[]{:S(2)}, u32[]{:S(2)}) collective-permute-start(bf16[1024,256]{1,0:T(8,128)(2,1)} %copy-done.6), channel_id=1, source_target_pairs={{2,0},{0,2},{3,129},{129,3},{130,128},{128,130},{131,257},{257,131... | collective-permute-start | bytes 1572872 | tf_op jit(solution)/shard_map/ppermute | solution.py:324
  77.1 12.7 %collective-permute-start.5 = (bf16[4096,256]{1,0:T(8,128)(2,1)}, bf16[4096,256]{1,0:T(8,128)(2,1)}, u32[]{:S(2)}, u32[]{:S(2)}) collective-permute-start(bf16[4096,256]{1,0:T(8,128)(2,1)} %collective-permute-done.4.w2), channel_id=1, source_target_pairs={{0,1},{1,0},{2,3},{3,2},{4,5},{5,4},{6,7},{7,6},{8,9},{9,8},{10,11... | collective-permute-start | bytes 6291464 | tf_op jit(solution)/shard_map/ppermute | solution.py:323
  85.8 4.1 %copy-start.5 = (f32[1024]{0:T(1024)S(1)}, f32[1024]{0:T(1024)}, u32[]{:S(2)}) copy-start(f32[1024]{0:T(1024)} %param.12) | copy-start | bytes 12292
  85.8 4.0 %collective-permute-start.7 = (bf16[1024,256]{1,0:T(8,128)(2,1)}, bf16[1024,256]{1,0:T(8,128)(2,1)S(1)}, u32[]{:S(2)}, u32[]{:S(2)}) collective-permute-start(bf16[1024,256]{1,0:T(8,128)(2,1)} %collective-permute-done.6.out2), channel_id=1, source_target_pairs={{0,1},{1,0},{2,3},{3,2},{4,5},{5,4},{6,7},{7,6},{8,9},{9,8},{10,11... | collective-permute-start | bytes 1572872 | tf_op jit(solution)/shard_map/ppermute | solution.py:325

commit v13 on v12

--- a/solution.py
+++ b/solution.py
@@ -302,9 +302,9 @@
     row_qkv = row_qkv * jnp.array([SCALE, 1, 1], jnp.bfloat16)[:, None, None, None]
 
     before = lax.ppermute(inputs, SEQ, [(i, i + 1) for i in range(127)])
+    other = lax.ppermute(inputs, "yl", SWAP)
     near = lax.all_gather(inputs, "c", axis=0)
     mine, main, last = pack_weights(row_out, col_qkv.transpose(1, 0, 2).reshape(3 * 1024, GROUP), col_out)
-    other = lax.ppermute(after(inputs, near, mine), "yl", SWAP)
     mine, main, last, row_qkv, before = lax.optimization_barrier((mine, main, last, row_qkv, before, near))[:5]
     before_other = lax.ppermute(before, "yl", SWAP)
     far = lax.all_gather(after(other, before), "c", axis=0)

time: 126 us -> 125 us (level)
  starting transfers between devices: 44 us -> 49.1 us
  blocking collectives: 43.3 us -> 40 us
  other arithmetic: 1.66 us -> 0.25 us
  waiting for transfers between devices: 13.8 us -> 12.5 us
    ppermute x1, starting transfers between devices: 8.66 us -> 14.8 us  [on_device(): theirs = lax.ppermute(main, ('yh', 'yl', 'c'), cross_route((1,)))]
    ppermute x1, waiting for transfers between devices: 2.52 us -> 0.01 us  [on_device(): other = lax.ppermute(inputs, 'yl', SWAP)]
    all_to_all x1, waiting for transfers between devices: 5.5 us -> 3.37 us  [on_device(): lax.all_to_all(sent.reshape(COLS, 4, 128), HEAD + SEQ, 0, 0, tiled=True)]
    ppermute x1, waiting for transfers between devices: 0.01 us -> 1.62 us  [on_device(): lax.ppermute(after(last, sent), ('yh', 'yl', 'c'), cross_route((1,)))]
    mul x1, other arithmetic: 1.58 us -> 0.17 us  [on_device(): row_qkv * jnp.array([SCALE, 1, 1], jnp.bfloat16)[:, None, None, None]]
    ppermute x1, waiting for transfers between devices: 5.04 us -> 6.39 us  [on_device(): theirs = lax.ppermute(main, ('yh', 'yl', 'c'), cross_route((1,)))]
    all_to_all x1, starting transfers between devices: 12.7 us -> 11.3 us  [on_device(): lax.all_to_all(sent.reshape(COLS, 4, 128), HEAD + SEQ, 0, 0, tiled=True)]
    all_gather x1, blocking collectives: 4.01 us -> 2.67 us  [on_device(): far = lax.all_gather(after(other, before), 'c', axis=0)]
  transfers between devices with their start and end apart: 9 -> 9, of which waited for: 4 -> 4; matrix products, arithmetic and copies ran while one was open for 3% -> 2% of each run, Pallas kernels for 7% -> 7%
where the time goes in v13:
time: 125 us; the launch traced here: 124 us
  starting transfers between devices  49.1 us (39%)
  blocking collectives  40 us (32%)
  Pallas kernels  15 us (12%)
  waiting for transfers between devices  12.5 us (10%)
  local copies, waits for them, and re-layouts  7.34 us (6%)
    all_to_all x1, blocking collectives, on_device(): lax.all_to_all(mixed.reshape(COLS, 2, 128), HEAD + SEQ, 0, 0, tiled=True)  28 us
    ppermute x1, starting transfers between devices, on_device(): theirs = lax.ppermute(main, ('yh', 'yl', 'c'), cross_route((1,)))  14.8 us
    all_to_all x1, starting transfers between devices, on_device(): lax.all_to_all(sent.reshape(COLS, 4, 128), HEAD + SEQ, 0, 0, tiled=True)  11.3 us
    ppermute x1, waiting for transfers between devices, on_device(): theirs = lax.ppermute(main, ('yh', 'yl', 'c'), cross_route((1,)))  6.39 us
    ppermute x1, starting transfers between devices, on_device(): mine_swapped = lax.ppermute(after(mine, sent), 'c', SWAP)  6.28 us
    pallas_call x1, Pallas kernels, col_layer(): pl.pallas_call(col_layer_kernel, out_shape=jax.ShapeDtypeStruct((PARTS, 1...  6.11 us
    unnamed x19, local copies, waits for them, and re-layouts  5.05 us
    all_gather x1, blocking collectives, on_device(): near = lax.all_gather(inputs, 'c', axis=0)  4.96 us
  transfers between devices with their start and end apart: 9, of which 4 were waited for; matrix products, arithmetic and copies ran while one was open for 2% of the time, Pallas kernels for 7%

profile of v13, /device:TPU:1, one launch (start us, length us, event | category | flops | bytes accessed | tf_op | source)
XLA Modules:
  0.0 124.3 jit_solution(4044589731272326397)
XLA Ops:
  0.0 4.0 %collective-permute-start = (bf16[512,256]{1,0:T(8,128)(2,1)}, bf16[512,256]{1,0:T(8,128)(2,1)S(1)}, u32[]{:S(2)}, u32[]{:S(2)}) collective-permute-start(bf16[512,256]{1,0:T(8,128)(2,1)} %source.1), channel_id=1, source_target_pairs={{0,4},{4,8},{8,12},{12,16},{16,20},{20,24},{24,28},{28,32},{32,36}... | collective-permute-start | bytes 786440 | tf_op jit(solution)/shard_map/ppermute | solution.py:304
  4.0 3.2 %collective-permute-start.1 = (bf16[512,256]{1,0:T(8,128)(2,1)}, bf16[512,256]{1,0:T(8,128)(2,1)}, u32[]{:S(2)}, u32[]{:S(2)}) collective-permute-start(bf16[512,256]{1,0:T(8,128)(2,1)} %source.1), channel_id=1, source_target_pairs={{0,2},{2,0},{1,3},{3,1},{4,6},{6,4},{5,7},{7,5},{8,10},{10,8},{9,1... | collective-permute-start | bytes 786440 | tf_op jit(solution)/shard_map/ppermute | solution.py:305
  7.2 5.0 %all-gather = bf16[1024,256]{1,0:T(8,128)(2,1)S(1)} all-gather(bf16[512,256]{1,0:T(8,128)(2,1)} %source.1), channel_id=2, replica_groups=mesh['yh'=4,'z'=8,'x'=4,'yl'=2,'c'=2] {'c'}, dimensions={0}, use_global_device_ids=true | all-gather | bytes 786432 | tf_op jit(solution)/shard_map/all_gather | solution.py:306
  12.2 1.4 %copy-done = bf16[1024,3,256]{2,0,1:T(8,128)(2,1)S(1)} copy-done((bf16[1024,3,256]{2,0,1:T(8,128)(2,1)S(1)}, bf16[1024,3,256]{2,0,1:T(8,128)(2,1)}, u32[]{:S(2)}) %copy-start) | copy-done | bytes 1572888
  15.6 1.6 %pack_weights.1 = (bf16[5120,256]{1,0:T(8,128)(2,1)S(1)}, bf16[4096,256]{1,0:T(8,128)(2,1)}, bf16[1024,256]{1,0:T(8,128)(2,1)S(1)}) custom-call(bf16[256,1024]{1,0:T(8,128)(2,1)S(1)} %copy-done.2, bf16[3072,256]{1,0:T(8,128)(2,1)S(1)} %bitcast.24, bf16[256,1024]{1,0:T(8,128)(2,1)S(1)} %copy-done.3), custom_call_target="tpu_custom_call" | custom-call | flops 1 | bytes 1 | tf_op jit(solution)/shard_map/pack_weights/pallas_call | solution.py:178
  18.3 3.6 %collective-permute-start.2 = (bf16[512,256]{1,0:T(8,128)(2,1)S(1)}, bf16[512,256]{1,0:T(8,128)(2,1)S(1)}, u32[]{:S(2)}, u32[]{:S(2)}) collective-permute-start(bf16[512,256]{1,0:T(8,128)(2,1)S(1)} %collective-permute-done), channel_id=1, source_target_pairs={{0,2},{2,0},{1,3},{3,1},{4,6},{6,4},{5,7},{7,5},{8,10},{10,8},{9,1... | collective-permute-start | bytes 786440 | tf_op jit(solution)/shard_map/ppermute | solution.py:309
  22.0 2.7 %all-gather.1 = bf16[1024,256]{1,0:T(8,128)(2,1)S(1)} all-gather(bf16[512,256]{1,0:T(8,128)(2,1)} %collective-permute-done.1), channel_id=3, replica_groups=mesh['yh'=4,'z'=8,'x'=4,'yl'=2,'c'=2] {'c'}, dimensions={0}, use_global_device_ids=true | all-gather | bytes 786432 | tf_op jit(solution)/shard_map/all_gather | solution.py:310
  24.7 2.2 %all-gather.2 = bf16[1024,256]{1,0:T(8,128)(2,1)S(1)} all-gather(bf16[512,256]{1,0:T(8,128)(2,1)S(1)} %collective-permute-done), channel_id=4, replica_groups=mesh['yh'=4,'z'=8,'x'=4,'yl'=2,'c'=2] {'c'}, dimensions={0}, use_global_device_ids=true | all-gather | bytes 786432 | tf_op jit(solution)/shard_map/all_gather | solution.py:311
  26.9 3.1 %row_own.1 = (bf16[512,256]{1,0:T(8,128)(2,1)S(1)}, f32[512,256]{1,0:T(8,128)S(1)}, f32[512,256]{1,0:T(8,128)S(1)}, f32[512,256]{1,0:T(8,128)S(1)}) custom-call(s32[4]{0:T(128)S(1)} %pad_add_fusion.place, bf16[2,512,256]{2,1,0:T(8,128)(2,1)S(1)} %bitcast.22, bf16[2,512,256]{2,1,0:T(8,128)(2,1)S(1)} %bitcast.23, f32[4,1,256]{2,1,0:T(1,128)S(1)} %bitcast.25, ...), custom_call_target="tpu_custom_call" | custom-call | flops 1 | bytes 1 | tf_op jit(solution)/shard_map/row_own/pallas_call | solution.py:102
  30.0 14.8 %collective-permute-start.4 = (bf16[4096,256]{1,0:T(8,128)(2,1)}, bf16[4096,256]{1,0:T(8,128)(2,1)}, u32[]{:S(2)}, u32[]{:S(2)}) collective-permute-start(bf16[4096,256]{1,0:T(8,128)(2,1)} %get-tuple-element.42), channel_id=1, source_target_pairs={{2,0},{0,2},{3,129},{129,3},{130,128},{128,130},{131,257},{257,131... | collective-permute-start | bytes 6291464 | tf_op jit(solution)/shard_map/ppermute | solution.py:317
  44.8 2.2 %all-gather.3 = bf16[1024,256]{1,0:T(8,128)(2,1)S(1)} all-gather(bf16[512,256]{1,0:T(8,128)(2,1)S(1)} %collective-permute-done.2), channel_id=5, replica_groups=mesh['yh'=4,'z'=8,'x'=4,'yl'=2,'c'=2] {'c'}, dimensions={0}, use_global_device_ids=true | all-gather | bytes 786432 | tf_op jit(solution)/shard_map/all_gather | solution.py:314
  47.0 3.3 %row_halo.1 = bf16[512,512]{1,0:T(8,128)(2,1)S(1)} custom-call(s32[4]{0:T(128)S(1)} %pad_add_fusion.place, bf16[2,512,256]{2,1,0:T(8,128)(2,1)S(1)} %bitcast.20, bf16[2,512,256]{2,1,0:T(8,128)(2,1)S(1)} %bitcast.21, f32[4,1,256]{2,1,0:T(1,128)S(1)} %bitcast.26, bf16[3,4,256,256]{3,2,1,0:T(8,128)(2,1)S(1)} %broadcast_multiply_fusion.weight, ...), custom_call_target="tpu_custom_call" | custom-call | flops 1 | bytes 1 | tf_op jit(solution)/shard_map/row_halo/pallas_call | solution.py:145
  51.3 11.3 %all-to-all-start = ((bf16[512,4,128]{2,1,0:T(4,128)(2,1)}), bf16[512,4,128]{2,1,0:T(4,128)(2,1)}, u32[]{:S(2)}, u32[]{:S(2)}) async-start(bf16[512,4,128]{2,1,0:T(4,128)(2,1)} %reshape.28), calls=%async_computation | async-start | bytes 1048576 | tf_op jit(solution)/shard_map/all_to_all | solution.py:321
  62.6 6.3 %collective-permute-start.3 = (bf16[5120,256]{1,0:T(8,128)(2,1)S(1)}, bf16[5120,256]{1,0:T(8,128)(2,1)}, u32[]{:S(2)}, u32[]{:S(2)}) collective-permute-start(bf16[5120,256]{1,0:T(8,128)(2,1)S(1)} %get-tuple-element.40.weights.w0), channel_id=1, source_target_pairs={{0,1},{1,0},{2,3},{3,2},{4,5},{5,4},{6,7},{7,6},{8,9},{9,8},{10,11... | collective-permute-start | bytes 7864328 | tf_op jit(solution)/shard_map/ppermute | solution.py:319
  68.9 1.9 %collective-permute-start.6 = (bf16[1024,256]{1,0:T(8,128)(2,1)}, bf16[1024,256]{1,0:T(8,128)(2,1)}, u32[]{:S(2)}, u32[]{:S(2)}) collective-permute-start(bf16[1024,256]{1,0:T(8,128)(2,1)} %copy-done.6), channel_id=1, source_target_pairs={{2,0},{0,2},{3,129},{129,3},{130,128},{128,130},{131,257},{257,131... | collective-permute-start | bytes 1572872 | tf_op jit(solution)/shard_map/ppermute | solution.py:324
  70.8 6.4 %collective-permute-done.4.w2 = bf16[4096,256]{1,0:T(8,128)(2,1)} collective-permute-done((bf16[4096,256]{1,0:T(8,128)(2,1)}, bf16[4096,256]{1,0:T(8,128)(2,1)}, u32[]{:S(2)}, u32[]{:S(2)}) %collective-permute-start.4) | collective-permute-done | bytes 2097184 | tf_op jit(solution)/shard_map/ppermute | solution.py:317
  77.2 1.9 %collective-permute-start.5 = (bf16[4096,256]{1,0:T(8,128)(2,1)}, bf16[4096,256]{1,0:T(8,128)(2,1)}, u32[]{:S(2)}, u32[]{:S(2)}) collective-permute-start(bf16[4096,256]{1,0:T(8,128)(2,1)} %collective-permute-done.4.w2), channel_id=1, source_target_pairs={{0,1},{1,0},{2,3},{3,2},{4,5},{5,4},{6,7},{7,6},{8,9},{9,8},{10,11... | collective-permute-start | bytes 6291464 | tf_op jit(solution)/shard_map/ppermute | solution.py:323
  79.1 3.4 %all-to-all-done = bf16[512,4,128]{2,1,0:T(4,128)(2,1)} async-done(((bf16[512,4,128]{2,1,0:T(4,128)(2,1)}), bf16[512,4,128]{2,1,0:T(4,128)(2,1)}, u32[]{:S(2)}, u32[]{:S(2)}) %all-to-all-start) | async-done | bytes 524320 | tf_op jit(solution)/shard_map/all_to_all | solution.py:321
  82.5 1.2 reshape.29.moved
  83.7 1.6 %collective-permute-done.6.out2 = bf16[1024,256]{1,0:T(8,128)(2,1)} collective-permute-done((bf16[1024,256]{1,0:T(8,128)(2,1)}, bf16[1024,256]{1,0:T(8,128)(2,1)}, u32[]{:S(2)}, u32[]{:S(2)}) %collective-permute-start.6) | collective-permute-done | bytes 524320 | tf_op jit(solution)/shard_map/ppermute | solution.py:324
  85.4 2.1 %collective-permute-start.7 = (bf16[1024,256]{1,0:T(8,128)(2,1)}, bf16[1024,256]{1,0:T(8,128)(2,1)S(1)}, u32[]{:S(2)}, u32[]{:S(2)}) collective-permute-start(bf16[1024,256]{1,0:T(8,128)(2,1)} %collective-permute-done.6.out2), channel_id=1, source_target_pairs={{0,1},{1,0},{2,3},{3,2},{4,5},{5,4},{6,7},{7,6},{8,9},{9,8},{10,11... | collective-permute-start | bytes 1572872 | tf_op jit(solution)/shard_map/ppermute | solution.py:325
  88.3 1.1 collective-permute-done.7.out3
  89.4 6.1 %col_layer.1 = bf16[4,128,256]{2,1,0:T(8,128)(2,1)S(1)} custom-call(s32[4]{0:T(128)S(1)} %pad_add_fusion.place, bf16[4,128,512]{2,1,0:T(8,128)(2,1)S(1)} %reshape.29.moved, f32[4,128,256]{2,1,0:T(8,128)S(1)} %row_output.1.partial, f32[4,1,256]{2,1,0:T(1,128)S(1)} %bitcast.27, bf16[5120,256]{1,0:T(8,128)(2,1)S(1)} %get-tuple-element.40.weights.w0, ...), custom_call_target="tpu_custom_call" | custom-call | flops 1 | bytes 1 | tf_op jit(solution)/shard_map/col_layer/pallas_call | solution.py:264
  95.6 28.0 %all_to_all.10 = bf16[512,2,128]{2,1,0:T(2,128)(2,1)S(1)} all-to-all(bf16[512,2,128]{2,1,0:T(2,128)(2,1)S(1)} %reshape.31), channel_id=1, replica_groups=mesh['yh'=4,'z'=8,'x'=4,'yl'=2,'c'=2] {'yl','c','yh','z','x'}, dimensions={0} | all-to-all | bytes 524288 | tf_op jit(solution)/shard_map/all_to_all | solution.py:334
  (28 shorter events, 5.8 us)
Async XLA Ops:
  0.0 18.3 %collective-permute-start = (bf16[512,256]{1,0:T(8,128)(2,1)}, bf16[512,256]{1,0:T(8,128)(2,1)S(1)}, u32[]{:S(2)}, u32[]{:S(2)}) collective-permute-start(bf16[512,256]{1,0:T(8,128)(2,1)} %source.1), channel_id=1, source_target_pairs={{0,4},{4,8},{8,12},{12,16},{16,20},{20,24},{24,28},{28,32},{32,36}... | collective-permute-start | bytes 786440 | tf_op jit(solution)/shard_map/ppermute | solution.py:304
  4.0 18.0 %collective-permute-start.1 = (bf16[512,256]{1,0:T(8,128)(2,1)}, bf16[512,256]{1,0:T(8,128)(2,1)}, u32[]{:S(2)}, u32[]{:S(2)}) collective-permute-start(bf16[512,256]{1,0:T(8,128)(2,1)} %source.1), channel_id=1, source_target_pairs={{0,2},{2,0},{1,3},{3,1},{4,6},{6,4},{5,7},{7,5},{8,10},{10,8},{9,1... | collective-permute-start | bytes 786440 | tf_op jit(solution)/shard_map/ppermute | solution.py:305
  7.2 11.0 %copy-start.8 = (bf16[3]{0:T(256)(128)(2,1)S(1)}, bf16[3]{0:T(256)(128)(2,1)}, u32[]{:S(2)}) copy-start(bf16[3]{0:T(256)(128)(2,1)} %constant.30.clone) | copy-start | bytes 22
  12.2 1.4 %copy-start = (bf16[1024,3,256]{2,0,1:T(8,128)(2,1)S(1)}, bf16[1024,3,256]{2,0,1:T(8,128)(2,1)}, u32[]{:S(2)}) copy-start(bf16[1024,3,256]{2,0,1:T(8,128)(2,1)} %param.13) | copy-start | bytes 4718596
  13.6 1.0 copy-start.2
  14.6 1.0 copy-start.3
  15.6 2.5 %copy-start.7 = (bf16[1024,3,256]{2,0,1:T(8,128)(2,1)S(1)}, bf16[1024,3,256]{2,0,1:T(8,128)(2,1)}, u32[]{:S(2)}) copy-start(bf16[1024,3,256]{2,0,1:T(8,128)(2,1)} %param.10) | copy-start | bytes 4718596
  17.3 0.8 copy-start.6
  18.3 8.5 %copy-start.4 = (f32[1024]{0:T(1024)S(1)}, f32[1024]{0:T(1024)}, u32[]{:S(2)}) copy-start(f32[1024]{0:T(1024)} %param.9) | copy-start | bytes 12292
  18.3 11.6 %collective-permute-start.2 = (bf16[512,256]{1,0:T(8,128)(2,1)S(1)}, bf16[512,256]{1,0:T(8,128)(2,1)S(1)}, u32[]{:S(2)}, u32[]{:S(2)}) collective-permute-start(bf16[512,256]{1,0:T(8,128)(2,1)S(1)} %collective-permute-done), channel_id=1, source_target_pairs={{0,2},{2,0},{1,3},{3,1},{4,6},{6,4},{5,7},{7,5},{8,10},{10,8},{9,1... | collective-permute-start | bytes 786440 | tf_op jit(solution)/shard_map/ppermute | solution.py:309
  26.9 20.1 %copy-start.1 = (bf16[512,256]{1,0:T(8,128)(2,1)S(1)}, bf16[512,256]{1,0:T(8,128)(2,1)}, u32[]{:S(2)}) copy-start(bf16[512,256]{1,0:T(8,128)(2,1)} %source.1) | copy-start | bytes 786436
  30.0 47.2 %collective-permute-start.4 = (bf16[4096,256]{1,0:T(8,128)(2,1)}, bf16[4096,256]{1,0:T(8,128)(2,1)}, u32[]{:S(2)}, u32[]{:S(2)}) collective-permute-start(bf16[4096,256]{1,0:T(8,128)(2,1)} %get-tuple-element.42), channel_id=1, source_target_pairs={{2,0},{0,2},{3,129},{129,3},{130,128},{128,130},{131,257},{257,131... | collective-permute-start | bytes 6291464 | tf_op jit(solution)/shard_map/ppermute | solution.py:317
  51.3 31.2 %all-to-all-start = ((bf16[512,4,128]{2,1,0:T(4,128)(2,1)}), bf16[512,4,128]{2,1,0:T(4,128)(2,1)}, u32[]{:S(2)}, u32[]{:S(2)}) async-start(bf16[512,4,128]{2,1,0:T(4,128)(2,1)} %reshape.28), calls=%async_computation | async-start | bytes 1048576 | tf_op jit(solution)/shard_map/all_to_all | solution.py:321
  62.6 26.8 %collective-permute-start.3 = (bf16[5120,256]{1,0:T(8,128)(2,1)S(1)}, bf16[5120,256]{1,0:T(8,128)(2,1)}, u32[]{:S(2)}, u32[]{:S(2)}) collective-permute-start(bf16[5120,256]{1,0:T(8,128)(2,1)S(1)} %get-tuple-element.40.weights.w0), channel_id=1, source_target_pairs={{0,1},{1,0},{2,3},{3,2},{4,5},{5,4},{6,7},{7,6},{8,9},{9,8},{10,11... | collective-permute-start | bytes 7864328 | tf_op jit(solution)/shard_map/ppermute | solution.py:319
  68.9 16.5 %collective-permute-start.6 = (bf16[1024,256]{1,0:T(8,128)(2,1)}, bf16[1024,256]{1,0:T(8,128)(2,1)}, u32[]{:S(2)}, u32[]{:S(2)}) collective-permute-start(bf16[1024,256]{1,0:T(8,128)(2,1)} %copy-done.6), channel_id=1, source_target_pairs={{2,0},{0,2},{3,129},{129,3},{130,128},{128,130},{131,257},{257,131... | collective-permute-start | bytes 1572872 | tf_op jit(solution)/shard_map/ppermute | solution.py:324
  77.2 12.2 %collective-permute-start.5 = (bf16[4096,256]{1,0:T(8,128)(2,1)}, bf16[4096,256]{1,0:T(8,128)(2,1)}, u32[]{:S(2)}, u32[]{:S(2)}) collective-permute-start(bf16[4096,256]{1,0:T(8,128)(2,1)} %collective-permute-done.4.w2), channel_id=1, source_target_pairs={{0,1},{1,0},{2,3},{3,2},{4,5},{5,4},{6,7},{7,6},{8,9},{9,8},{10,11... | collective-permute-start | bytes 6291464 | tf_op jit(solution)/shard_map/ppermute | solution.py:323
  83.7 5.6 %copy-start.5 = (f32[1024]{0:T(1024)S(1)}, f32[1024]{0:T(1024)}, u32[]{:S(2)}) copy-start(f32[1024]{0:T(1024)} %param.12) | copy-start | bytes 12292
  85.4 4.0 %collective-permute-start.7 = (bf16[1024,256]{1,0:T(8,128)(2,1)}, bf16[1024,256]{1,0:T(8,128)(2,1)S(1)}, u32[]{:S(2)}, u32[]{:S(2)}) collective-permute-start(bf16[1024,256]{1,0:T(8,128)(2,1)} %collective-permute-done.6.out2), channel_id=1, source_target_pairs={{0,1},{1,0},{2,3},{3,2},{4,5},{5,4},{6,7},{7,6},{8,9},{9,8},{10,11... | collective-permute-start | bytes 1572872 | tf_op jit(solution)/shard_map/ppermute | solution.py:325
